TPU v7x, 32 devices: a whole 2x2x4 slice. The times are simulated.
32 devices in a mesh: grp: 2 (over x), path: 16 (over z, y, core).
Axes of the slice: x: 2, y: 2, z: 4, core: 2. Of those that a mesh axis runs over, the one named last changes fastest.
Arguments:
- normals: float32 [32, 524288], P(None, ('grp', 'path')), may hold values from -10.1 to 10.1
- spot_today: float32 [32], replicated, may hold values from 0.5 to 2
- volatility: float32 [32], replicated, may hold values from 0.1 to 0.5
- weights: float32 [32], replicated, may hold values from 0.5 to 1.5
- cash_flows: float32 [524288], P(('grp', 'path')), may hold values from -300 to 300
- exercise: int32 [524288], P(('grp', 'path')), may hold values 0 or 1
Outputs:
- path_value: float32 [524288], P(('grp', 'path'))
- state_cot: float32 [32, 524288], P(None, ('grp', 'path'))
- flow_cot: float32 [524288], P(('grp', 'path'))
- greeks: float32 [2, 32], replicated
All inputs are finite; a program needn't handle non-finite values. No bound on the sum of `exercise` on one device may be relied on, other than what follows from the above.
Results may differ from a plain program's by a relative error of at most 0.0003.
Values sent between devices are 32-bit elements; how exact they have to be, the bound alone decides.
No kernel may reach another device: no remote copies, remote signals or barrier semaphores. Data moves between devices by JAX's collectives and lax.ppermute only.
A program may use at most 64 MiB of HBM per device.

v0:
```python
import math

import jax
import jax.numpy as jnp
from jax import lax
from jax.sharding import PartitionSpec as P

expiry_time = 0.5
root_time = math.sqrt(0.5)
inv_root_two = 1.0 / math.sqrt(2.0)
notional = 20.0
soft_width = 0.02


def path_state(normals, spot_today, volatility):
    return spot_today[:, None] * jnp.exp(
        volatility[:, None] * (root_time * normals) - 0.5 * expiry_time * volatility[:, None] ** 2
    )


def basis_rows(state, spot_today, volatility):
    scaled = (state / spot_today[:, None] - 1.0) / (volatility[:, None] * root_time)
    leading = jnp.ones_like(scaled[:1])
    squares = (scaled * scaled - 1.0) * inv_root_two
    neighbour = scaled * jnp.roll(scaled, -1, axis=0)
    bounded = jnp.tanh(scaled[:-1])
    return jnp.concatenate([leading, scaled, squares, neighbour, bounded], axis=0)


def payoff(state, spot_today, weights):
    basket = jnp.sum(weights[:, None] * state, axis=0) / jnp.sum(weights * spot_today)
    return notional * soft_width * jax.nn.softplus((basket - 1.0) / soft_width)


def chol_solve(factor, rhs):
    first = lax.linalg.triangular_solve(factor, rhs, left_side=True, lower=True)
    return lax.linalg.triangular_solve(factor, first, left_side=True, lower=True, transpose_a=True)


def per_device(normals, spot_today, volatility, weights, cash_flows, exercise):
    assets, local_paths = normals.shape
    features = 4 * assets
    block_width = math.gcd(local_paths, 1024)
    block_count = local_paths // block_width
    path_total = local_paths * lax.axis_size("grp") * lax.axis_size("path")
    highest = lax.Precision.HIGHEST
    contract_last = (((1,), (1,)), ((), ()))

    def block_inputs(block_index):
        block_start = block_index * block_width
        draw_block = lax.dynamic_slice_in_dim(normals, block_start, block_width, 1)
        flow_block = lax.dynamic_slice_in_dim(cash_flows, block_start, block_width, 0)
        taken_flag = lax.dynamic_slice_in_dim(exercise, block_start, block_width, 0).astype(
            jnp.float32
        )
        return (draw_block, flow_block, taken_flag)

    def gram_step(block_index, running):
        gram_acc, moment_acc = running
        draw_block, flow_block, taken_flag = block_inputs(block_index)
        basis_block = basis_rows(
            path_state(draw_block, spot_today, volatility), spot_today, volatility
        )
        gram_acc = gram_acc + lax.dot_general(
            basis_block,
            basis_block,
            contract_last,
            precision=highest,
            preferred_element_type=jnp.float32,
        )
        targets = jnp.stack([flow_block, 1.0 - taken_flag])
        moment_acc = moment_acc + lax.dot_general(
            targets,
            basis_block,
            contract_last,
            precision=highest,
            preferred_element_type=jnp.float32,
        )
        return (gram_acc, moment_acc)

    zero_gram = jnp.zeros((features, features), jnp.float32)
    zero_moment = jnp.zeros((2, features), jnp.float32)
    gram_acc, moment_acc = lax.fori_loop(0, block_count, gram_step, (zero_gram, zero_moment))
    gram_sum, moment_sum = lax.psum((gram_acc, moment_acc), ("grp", "path"))
    gram_mean = gram_sum / path_total
    moment_mean = moment_sum / path_total
    factor = jnp.linalg.cholesky(gram_mean)
    coefficients = chol_solve(factor, moment_mean.T)
    regression = coefficients[:, 0]
    multiplier = coefficients[:, 1]
    coef_rows = coefficients.T

    def adjoint_step(block_index, running):
        value_out, state_out, flow_out, greek_acc = running
        draw_block, flow_block, taken_flag = block_inputs(block_index)
        state, path_back = jax.vjp(
            lambda spot_level, spread: path_state(draw_block, spot_level, spread),
            spot_today,
            volatility,
        )
        (basis_block, reward), feature_back = jax.vjp(
            lambda current, spot_level, spread: (
                basis_rows(current, spot_level, spread),
                payoff(current, spot_level, weights),
            ),
            state,
            spot_today,
            volatility,
        )
        fitted = lax.dot_general(
            coef_rows,
            basis_block,
            (((1,), (0,)), ((), ())),
            precision=highest,
            preferred_element_type=jnp.float32,
        )
        continuation = fitted[0]
        lam_phi = fitted[1]
        value_block = taken_flag * reward + (1.0 - taken_flag) * continuation
        rows_bar = (
            multiplier[:, None] * (flow_block - continuation)[None, :]
            + regression[:, None] * (1.0 - taken_flag - lam_phi)[None, :]
        )
        state_bar, spot_bar, spread_bar = feature_back((rows_bar, taken_flag))
        spot_path, spread_path = path_back(state_bar)
        greek_acc = greek_acc + jnp.stack([spot_bar + spot_path, spread_bar + spread_path])
        block_start = block_index * block_width
        value_out = lax.dynamic_update_slice_in_dim(value_out, value_block, block_start, 0)
        state_out = lax.dynamic_update_slice_in_dim(state_out, state_bar, block_start, 1)
        flow_out = lax.dynamic_update_slice_in_dim(flow_out, lam_phi, block_start, 0)
        return (value_out, state_out, flow_out, greek_acc)

    start_outs = (
        jnp.zeros((local_paths,), jnp.float32),
        jnp.zeros((assets, local_paths), jnp.float32),
        jnp.zeros((local_paths,), jnp.float32),
        jnp.zeros((2, assets), jnp.float32),
    )
    path_value, state_cot, flow_cot, greek_acc = lax.fori_loop(
        0, block_count, adjoint_step, start_outs
    )
    greeks = lax.psum(greek_acc, ("grp", "path")) / path_total
    return (path_value, state_cot, flow_cot, greeks)


def solution(mesh):
    in_specs = (P(None, ("grp", "path")), P(), P(), P(), P(("grp", "path")), P(("grp", "path")))
    out_specs = (P(("grp", "path")), P(None, ("grp", "path")), P(("grp", "path")), P())
    return jax.shard_map(
        per_device, mesh=mesh, in_specs=in_specs, out_specs=out_specs, check_vma=False
    )
```

profile of v0, /device:TPU:0, one launch (start us, length us, event | category | flops | bytes accessed | tf_op | source)
XLA Modules:
  0.0 404.8 jit_solution(4931169487659952769)
XLA Ops:
  7.9 80.4 %while.42 = (s32[]{:T(128)}, f32[128,128]{1,0:T(8,128)S(1)}, f32[2,128]{1,0:T(2,128)S(1)}, f32[32]{0:T(128)}, f32[32,16384]{1,0:T(8,128)}, /*index=5*/f32[32]{0:...) while((s32[]{:T(128)}, f32[128,128]{1,0:T(8,128)S(1)}, ...), condition=%wide.region_1.2_spmd.clone, body=%wide.region_0.1_spmd.clone.sunk | while | flops 204870208 | bytes 3562582 | solution.py:83
  9.9 1.0 add_multiply_fusion.5
  20.0 1.0 add_multiply_fusion.5
  45.1 1.0 add_multiply_fusion.5
  55.2 1.0 add_multiply_fusion.5
  60.2 1.0 add_multiply_fusion.5
  65.2 1.0 add_multiply_fusion.5
  70.3 1.0 add_multiply_fusion.5
  80.3 1.0 add_multiply_fusion.5
  89.1 1.3 multiply_bitcast_fusion.2
  91.7 42.0 %psum.22 = f32[2,128]{1,0:T(2,128)S(1)} all-reduce(f32[2,128]{1,0:T(2,128)S(1)} %get-tuple-element.642), channel_id=1, replica_groups=mesh['grp'=2,'path'=16] {'grp','path'}, use_global_device_ids=true, to_apply=%region_5.6 | all-reduce | flops 256 | bytes 2048 | tf_op jit(solution)/shard_map/psum | solution.py:84
  133.7 75.8 %all-reduce.5.cloned.1.call-done = f32[128,128]{0,1:T(8,128)} async-done(((f32[128,128]{0,1:T(8,128)}), f32[128,128]{0,1:T(8,128)}) %all-reduce.5.cloned.1.call-update) | async-done | bytes 65552 | tf_op jit(solution)/shard_map/psum | solution.py:84
  211.4 11.7 %cholesky.15 = f32[128,128]{1,0:T(8,128)S(1)} custom-call(f32[128,128]{1,0:T(8,128)S(1)} %fusion.19), custom_call_target="Cholesky" | custom-call | tf_op jit(solution)/shard_map/jit(cholesky)/cholesky | solution.py:87
  224.4 9.8 %custom-call.8 = f32[1,128,128]{1,2,0:T(8,128)S(1)} custom-call(f32[1,128,128]{2,1,0:T(8,128)S(1)} %fusion.14), custom_call_target="InvertDiagBlocksLowerTriangular" | custom-call | tf_op jit(solution)/shard_map/triangular_solve | solution.py:37
  235.0 121.5 %while.43 = (s32[]{:T(128)}, f32[16384]{0:T(1024)S(1)}, f32[32,16384]{1,0:T(8,128)S(1)}, f32[16384]{0:T(1024)S(1)}, f32[2,32]{1,0:T(2,128)S(1)}, /*index=5*/s32[...) while((s32[]{:T(128)}, f32[16384]{0:T(1024)S(1)}, ...), condition=%wide.region_15.16_spmd.clone, body=%wide.region_7.15_spmd.clone.sunk | while | flops 5333607 | bytes 5730625 | solution.py:139
  235.0 1.0 add_multiply_fusion.6
  237.6 2.0 multiply_reduce_fusion.8
  241.1 1.3 fusion.49
  242.6 1.0 add_multiply_fusion.6
  245.2 2.0 multiply_reduce_fusion.8
  248.7 1.3 fusion.49
  250.2 1.0 add_multiply_fusion.6
  252.8 2.0 multiply_reduce_fusion.8
  256.3 1.3 fusion.49
  257.8 1.0 add_multiply_fusion.6
  260.4 2.0 multiply_reduce_fusion.8
  263.9 1.3 fusion.49
  265.4 1.0 add_multiply_fusion.6
  268.0 2.0 multiply_reduce_fusion.8
  271.5 1.3 fusion.49
  273.0 1.0 add_multiply_fusion.6
  275.6 2.0 multiply_reduce_fusion.8
  279.1 1.3 fusion.49
  280.6 1.0 add_multiply_fusion.6
  283.2 2.0 multiply_reduce_fusion.8
  286.7 1.3 fusion.49
  288.2 1.0 add_multiply_fusion.6
  290.8 2.0 multiply_reduce_fusion.8
  294.3 1.3 fusion.49
  295.8 1.0 add_multiply_fusion.6
  298.3 2.0 multiply_reduce_fusion.8
  301.9 1.3 fusion.49
  303.4 1.0 add_multiply_fusion.6
  305.9 2.0 multiply_reduce_fusion.8
  309.5 1.3 fusion.49
  311.0 1.0 add_multiply_fusion.6
  313.5 2.0 multiply_reduce_fusion.8
  317.1 1.3 fusion.49
  318.6 1.0 add_multiply_fusion.6
  321.1 2.0 multiply_reduce_fusion.8
  324.7 1.3 fusion.49
  326.2 1.0 add_multiply_fusion.6
  328.7 2.0 multiply_reduce_fusion.8
  332.3 1.3 fusion.49
  333.8 1.0 add_multiply_fusion.6
  336.3 2.0 multiply_reduce_fusion.8
  339.9 1.3 fusion.49
  341.4 1.0 add_multiply_fusion.6
  343.9 2.0 multiply_reduce_fusion.8
  347.5 1.3 fusion.49
  349.0 1.0 add_multiply_fusion.6
  351.5 2.0 multiply_reduce_fusion.8
  355.0 1.3 fusion.49
  356.5 40.9 %psum.23 = f32[2,32]{1,0:T(2,128)S(1)} all-reduce(f32[2,32]{1,0:T(2,128)S(1)} %get-tuple-element.646), channel_id=1, replica_groups=mesh['grp'=2,'path'=16] {'grp','path'}, use_global_device_ids=true, to_apply=%region_16.17 | all-reduce | flops 64 | bytes 512 | tf_op jit(solution)/shard_map/psum | solution.py:142
  (520 shorter events, 115.2 us)
Async XLA Ops:
  7.2 202.4 %all-reduce.5.cloned.1.call-start = ((), (), s32[]{:S(2)}) async-start(), calls=%async_computation | async-start | bytes 131072 | tf_op jit(solution)/shard_map/psum | solution.py:84
  7.9 81.2 %copy-start.1 = (f32[32]{0:T(128)S(1)}, f32[32]{0:T(128)}, u32[]{:S(2)}) copy-start(f32[32]{0:T(128)} %param.13) | copy-start | bytes 388
  88.3 146.6 %copy-start.2 = (f32[32]{0:T(128)S(1)}, f32[32]{0:T(128)}, u32[]{:S(2)}) copy-start(f32[32]{0:T(128)} %get-tuple-element.1153) | copy-start | bytes 388
  88.3 146.6 %copy-start.5 = (f32[32]{0:T(128)S(1)}, f32[32]{0:T(128)}, u32[]{:S(2)}) copy-start(f32[32]{0:T(128)} %get-tuple-element.1154) | copy-start | bytes 388
  356.5 41.5 %copy-start = (f32[32,16384]{1,0:T(8,128)}, f32[32,16384]{1,0:T(8,128)S(1)}, u32[]{:S(2)}) copy-start(f32[32,16384]{1,0:T(8,128)S(1)} %get-tuple-element.638) | copy-start | bytes 6291460
  356.5 41.5 %copy-start.3 = (f32[16384]{0:T(1024)}, f32[16384]{0:T(1024)S(1)}, u32[]{:S(2)}) copy-start(f32[16384]{0:T(1024)S(1)} %get-tuple-element.639) | copy-start | bytes 196612
  356.5 41.5 %copy-start.4 = (f32[16384]{0:T(1024)}, f32[16384]{0:T(1024)S(1)}, u32[]{:S(2)}) copy-start(f32[16384]{0:T(1024)S(1)} %get-tuple-element.637) | copy-start | bytes 196612
Sparse Core Ops, SparseCore 0:
  89.2 120.3 all-reduce.4
where the time goes:
time: 408 us; the launch traced here: 405 us
  other arithmetic  151 us (37%)
  blocking collectives  82.9 us (20%)
  waiting for transfers between devices  75.9 us (19%)
  local copies, waits for them, and re-layouts  40.1 us (10%)
  matrix products  24.6 us (6%)
  between operations  15.5 us (4%)
  loops' own time  14.4 us (4%)
    psum x1, waiting for transfers between devices, per_device(): gram_sum, moment_sum = lax.psum((gram_acc, moment_acc), ('grp', 'path'))  75.8 us
    psum x1, blocking collectives, per_device(): gram_sum, moment_sum = lax.psum((gram_acc, moment_acc), ('grp', 'path'))  42 us
    psum x1, blocking collectives, per_device(): greeks = lax.psum(greek_acc, ('grp', 'path')) / path_total  40.9 us
    mul x32, other arithmetic, basis_rows(): squares = (scaled * scaled - 1.0) * inv_root_two  33.1 us
    reduce_sum x16, other arithmetic, payoff(): jnp.sum(weights[:, None] * state, axis=0) / jnp.sum(weights * spot_today)  31.9 us
    concatenate x32, local copies, waits for them, and re-layouts, basis_rows(): jnp.concatenate([leading, scaled, squares, neighbour, bounded], axis=0)  21.9 us
    reduce_sum x16, other arithmetic, path_state(): volatility[:, None] * (root_time * normals)  21.4 us
    another operation x1, loops' own time, per_device(): lax.fori_loop(0, block_count, adjoint_step, start_outs)  12.8 us
  transfers between devices with their start and end apart: 1, of which 1 were waited for; matrix products, arithmetic and copies ran while one was open for 0% of the time, Pallas kernels for 0%

commit v1 on v0

v1 whole, which is shorter than its diff:
```python
import functools
import math

import jax
import jax.numpy as jnp
from jax import lax
from jax.experimental import pallas as pl
from jax.experimental.pallas import tpu as pltpu
from jax.sharding import PartitionSpec as P

root_time = math.sqrt(0.5)
notional = 20.0
soft_width = 0.02
LANES = 128
F32 = jnp.float32
BF16 = jnp.bfloat16
CONTRACT_LAST = (((1,), (1,)), ((), ()))


def column(row, count):
    rows = lax.broadcasted_iota(jnp.int32, (count, count), 0)
    cols = lax.broadcasted_iota(jnp.int32, (count, count), 1)
    wide = jnp.broadcast_to(row, (count, count))
    picked = jnp.sum(jnp.where(rows == cols, wide, 0.0), axis=1, keepdims=True)
    return jnp.broadcast_to(picked, (count, LANES))


def split(x):
    hi = x.astype(BF16)
    lo = (x - hi.astype(F32)).astype(BF16)
    return hi, lo


def sums_kernel(
    assets, width,
    normals, spot, vol, weights, cash, taken,
    scaled_out, bounded_out, value_out, slope_out, gram_out, jac_out,
    coef, rows, jac_hi, jac_lo, gram_acc, jac_acc, jac_low,
):
    step = pl.program_id(0)
    features = 4 * assets

    @pl.when(step == 0)
    def _():
        spread = column(vol[...] * root_time, assets)
        wide = column(weights[...] * spot[...], assets)
        total = jnp.sum(weights[...] * spot[...], axis=1, keepdims=True)
        coef[0] = spread
        coef[1] = 0.5 * spread * spread
        coef[2] = 1.0 / spread
        coef[3] = wide / jnp.broadcast_to(total, (assets, LANES))
        gram_acc[...] = jnp.zeros_like(gram_acc)
        jac_acc[...] = jnp.zeros_like(jac_acc)
        jac_low[...] = jnp.zeros_like(jac_low)

    last = lax.broadcasted_iota(jnp.int32, (assets, LANES), 0) == assets - 1
    slot = lax.broadcasted_iota(jnp.int32, (16, LANES), 0)
    for c in range(width // LANES):
        at = pl.ds(c * LANES, LANES)
        draw = normals[:, at]
        spread = coef[0]
        growth = jnp.exp(spread * draw - coef[1])
        scaled = (growth - 1.0) * coef[2]
        bounded = jnp.where(last, 1.0, jnp.tanh(scaled))
        scaled_out[:, at] = scaled
        bounded_out[:, at] = bounded
        after = pltpu.roll(scaled, assets - 1, 0)
        before = pltpu.roll(scaled, 1, 0)
        basis = jnp.concatenate([scaled, scaled * scaled - 1.0, scaled * after, bounded], axis=0)
        hi, lo = split(basis)
        rows[16 : 16 + features, at] = hi
        rows[16 + features : 16 + 2 * features, at] = lo
        slope = growth * (draw - spread) - scaled
        jac = jnp.concatenate(
            [slope, slope * scaled, slope * after, slope * (1.0 - bounded * bounded), slope * before],
            axis=0,
        )
        hi, lo = split(jac)
        jac_hi[:, at] = hi
        jac_lo[:, at] = lo
        basket = jnp.sum(growth * coef[3], axis=0, keepdims=True)
        x = (basket - 1.0) * (1.0 / soft_width)
        decay = jnp.exp(-jnp.abs(x))
        reward = (notional * soft_width) * (jnp.maximum(x, 0.0) + jnp.log1p(decay))
        inverse = 1.0 / (1.0 + decay)
        sigmoid = jnp.where(x >= 0.0, inverse, decay * inverse)
        flag = taken[:, at].astype(F32)
        flow = cash[:, at]
        pull = notional * flag * sigmoid
        value_out[:, at] = flag * reward
        slope_out[:, at] = pull
        flow_hi = flow.astype(BF16).astype(F32)
        pull_hi = pull.astype(BF16).astype(F32)
        target = jnp.zeros((16, LANES), F32)
        for index, row in enumerate([flow_hi, flow - flow_hi, 1.0 - flag, pull_hi, pull - pull_hi]):
            target = jnp.where(slot == index, jnp.broadcast_to(row, (16, LANES)), target)
        rows[0:16, at] = target.astype(BF16)

    upper = rows[0 : 16 + features, :]
    gram_acc[...] += lax.dot_general(
        upper, rows[16:, :], CONTRACT_LAST, preferred_element_type=F32
    )
    jac_acc[...] += lax.dot_general(rows[...], jac_hi[...], CONTRACT_LAST, preferred_element_type=F32)
    jac_low[...] += lax.dot_general(upper, jac_lo[...], CONTRACT_LAST, preferred_element_type=F32)

    def targets(t):
        pairs = [t[0:1] + t[1:2], t[2:3], t[3:4] + t[4:5], jnp.zeros((5, t.shape[1]), F32)]
        return jnp.concatenate(pairs, axis=0)

    @pl.when(step == pl.num_programs(0) - 1)
    def _():
        high = gram_acc[16:, 0:features]
        half = 0.5 * high + gram_acc[16:, features:]
        gram_out[0:features, :] = half + half.T
        gram_out[features:, :] = targets(gram_acc[0:16, 0:features] + gram_acc[0:16, features:])
        both = jac_acc[16 : 16 + features, :] + jac_acc[16 + features :, :] + jac_low[16:, :]
        aims = targets(jac_acc[0:16, :] + jac_low[0:16, :])
        jac_out[0:features, :] = both[:, 0:features]
        jac_out[features : features + assets, :] = jnp.concatenate(
            [both[assets * g : assets * (g + 1), features:] for g in range(4)], axis=1
        )
        jac_out[features + assets : features + assets + 8, :] = aims[:, 0:features]
        jac_out[features + assets + 8 :, :] = jnp.concatenate(
            [aims[:, features:], jnp.zeros((8, features - assets), F32)], axis=1
        )


def lane(block, index):
    return jnp.broadcast_to(block[:, index : index + 1], block.shape)


def solve_kernel(scale, gram, out, spread):
    features = gram.shape[1]
    blocks = features // 8
    lanes = lax.broadcasted_iota(jnp.int32, (8, features), 1)
    subs = lax.broadcasted_iota(jnp.int32, (8, features), 0)
    mat = [gram[8 * v : 8 * v + 8, :] * scale for v in range(blocks + 1)]
    for k in range(blocks):
        base = 8 * k
        head = mat[k]
        diag = {}
        for j in range(8):
            col = lane(head, base + j)
            spread[0, j] = col
            for i in range(j + 1):
                diag[i, j] = jnp.broadcast_to(spread[0, j, i : i + 1, :], (8, features))
        inside = (lanes >= base) & (lanes < base + 8)
        spread[1, 0] = jnp.where(inside, jnp.where(lanes == base + subs, -1.0, 0.0), head)
        work = [jnp.broadcast_to(spread[1, 0, i : i + 1, :], (8, features)) for i in range(8)]
        inverse, low = [], {}
        for p in range(8):
            inv = 1.0 / diag[p, p]
            inverse.append(inv)
            for j in range(p + 1, 8):
                low[p, j] = diag[p, j] * inv
            for i in range(p + 1, 8):
                for j in range(i, 8):
                    diag[i, j] = diag[i, j] - low[p, i] * diag[p, j]
                work[i] = work[i] - low[p, i] * work[p]
        for i in reversed(range(8)):
            value = work[i] * inverse[i]
            for j in range(i + 1, 8):
                value = value - low[i, j] * work[j]
            work[i] = value
        for v in range(k + 1, blocks + 1):
            new = jnp.where(inside, 0.0, mat[v])
            for c in range(8):
                new = new - lane(mat[v], base + c) * work[c]
            mat[v] = new
    kept = jnp.broadcast_to(gram[features + 2 : features + 3, :], (8, features))
    out[...] = jnp.where(subs == 3, kept, mat[blocks])


def adjoint_kernel(
    assets, width, path_total,
    scaled_in, bounded_in, cash, taken, value_in, pull_in, solved, jac, spot, vol, weights,
    value_out, cot_out, flow_out, greeks_out,
    coef,
):
    step = pl.program_id(0)
    features = 4 * assets

    @pl.when(step == 0)
    def _():
        turned = solved[...].T
        spread = column(vol[...] * root_time, assets)
        base = column(spot[...], assets)
        weight = column(weights[...], assets)
        total = jnp.sum(weights[...] * spot[...], axis=1, keepdims=True)
        gain = 1.0 / (base * spread)
        for which in range(2):
            parts = [
                jnp.broadcast_to(turned[assets * g : assets * (g + 1), which : which + 1], (assets, LANES))
                for g in range(4)
            ]
            at = 9 * which
            for g in range(4):
                coef[at + g] = parts[g]
            coef[at + 4] = parts[0] * gain
            coef[at + 5] = 2.0 * parts[1] * gain
            coef[at + 6] = parts[2] * gain
            coef[at + 7] = pltpu.roll(parts[2], 1, 0) * gain
            coef[at + 8] = parts[3] * gain
            offset = jnp.sum(parts[1], axis=0, keepdims=True)
            coef[19, 8 * which : 8 * which + 8] = jnp.broadcast_to(offset, (8, LANES))
        coef[18] = weight / jnp.broadcast_to(total, (assets, LANES))

    for c in range(width // LANES):
        at = pl.ds(c * LANES, LANES)
        scaled = scaled_in[:, at]
        bounded = bounded_in[:, at]
        after = pltpu.roll(scaled, assets - 1, 0)
        before = pltpu.roll(scaled, 1, 0)
        curve = 1.0 - bounded * bounded
        fitted, tangent = [], []
        for which in range(2):
            k = 9 * which
            inner = coef[k] + coef[k + 1] * scaled + coef[k + 2] * after
            terms = scaled * inner + coef[k + 3] * bounded
            fitted.append(jnp.sum(terms, axis=0, keepdims=True) - coef[19, 8 * which : 8 * which + 1])
            tangent.append(
                coef[k + 4] + coef[k + 5] * scaled + coef[k + 6] * after + coef[k + 7] * before
                + coef[k + 8] * curve
            )
        continuation, lam = fitted
        rest = 1.0 - taken[:, at].astype(F32)
        value_out[:, at] = value_in[:, at] + rest * continuation
        flow_out[:, at] = lam
        miss = cash[:, at] - continuation
        gap = rest - lam
        cot_out[:, at] = miss * tangent[1] + gap * tangent[0] + pull_in[:, at] * coef[18]

    @pl.when(step == pl.num_programs(0) - 1)
    def _():
        turned = solved[...].T
        regression, multiplier = solved[0:1, :], solved[1:2, :]
        group = lax.broadcasted_iota(jnp.int32, (assets, LANES), 1) // assets

        def against(which):
            main = jnp.sum(jac[0:features, :] * turned[:, which : which + 1], axis=0, keepdims=True)
            packed = jnp.zeros((assets, LANES), F32)
            for g in range(4):
                part = turned[assets * g : assets * (g + 1), which : which + 1]
                packed = jnp.where(group == g, jnp.broadcast_to(part, (assets, LANES)), packed)
            side = jnp.sum(jac[features : features + assets, :] * packed, axis=0, keepdims=True)
            side = side + pltpu.roll(side, 2 * assets, 1)
            side = side + pltpu.roll(side, assets, 1)
            return main, side

        aims = features + assets
        main_r, side_r = against(0)
        main_m, side_m = against(1)
        miss, gap = jac[aims : aims + 1, :] - main_r, jac[aims + 1 : aims + 2, :] - main_m
        miss_side = jac[aims + 8 : aims + 9, :] - side_r
        gap_side = jac[aims + 9 : aims + 10, :] - side_m
        lanes = lax.broadcasted_iota(jnp.int32, (1, LANES), 1)
        double = jnp.where((lanes >= assets) & (lanes < 2 * assets), 2.0, 1.0)
        total = double * (multiplier * miss + regression * gap)
        total = total + pltpu.roll(total, 2 * assets, 1)
        total = total + pltpu.roll(total, assets, 1)

        def earlier(row):
            moved = pltpu.roll(row, features - 2 * assets + 1, 1)
            wrapped = pltpu.roll(row, features - 3 * assets + 1, 1)
            return jnp.where(lanes == 0, wrapped, moved)

        total = total + earlier(multiplier) * miss_side + earlier(regression) * gap_side
        vega = total[:, 0:assets] / vol[...]
        pulled_slope = jac[aims + 2 : aims + 3, 0:assets]
        pulled_scaled = solved[3:4, 0:assets]
        pulled = solved[3:4, features - 1 : features]
        value = weights[...] * spot[...]
        whole = jnp.sum(value, axis=1, keepdims=True)
        growth = pulled + vol[...] * root_time * pulled_scaled
        mean = jnp.sum(value * growth, axis=1, keepdims=True) / whole
        delta = weights[...] / whole * (growth - mean)
        vega = vega + value * root_time / whole * (pulled_slope + pulled_scaled)
        greeks_out[...] = jnp.concatenate([delta, vega], axis=0) * (1.0 / path_total)


def add_up(values, axes):
    for axis in axes:
        size = lax.axis_size(axis)
        if size & (size - 1):
            values = [lax.psum(v, axis) for v in values]
            continue
        bit = 1
        while bit < size:
            pairs = [(i, i ^ bit) for i in range(size)]
            values = [v + lax.ppermute(v, axis, pairs) for v in values]
            bit *= 2
    return values


def per_device(normals, spot, vol, weights, cash, taken):
    assets, paths = normals.shape
    features = 4 * assets
    path_total = paths * lax.axis_size("grp") * lax.axis_size("path")
    width = math.gcd(paths, 2048)
    grid = (paths // width,)
    spot, vol, weights = (a.reshape(1, assets) for a in (spot, vol, weights))
    cash, taken = cash.reshape(1, paths), taken.reshape(1, paths)
    whole = pl.BlockSpec((1, assets), lambda i: (0, 0))
    line = pl.BlockSpec((1, width), lambda i: (0, i))
    tile = pl.BlockSpec((assets, width), lambda i: (0, i))
    full = lambda *shape: pl.BlockSpec(shape, lambda i: (0, 0))
    params = pltpu.CompilerParams(vmem_limit_bytes=48 * 1024 * 1024)
    big = jax.ShapeDtypeStruct((assets, paths), F32)
    row = jax.ShapeDtypeStruct((1, paths), F32)
    jac_rows = features + assets + 16
    scaled, bounded, value, pull, gram, jac = pl.pallas_call(
        functools.partial(sums_kernel, assets, width),
        grid=grid,
        in_specs=[tile, whole, whole, whole, line, line],
        out_specs=[tile, tile, line, line, full(features + 8, features), full(jac_rows, features)],
        out_shape=[
            big, big, row, row,
            jax.ShapeDtypeStruct((features + 8, features), F32),
            jax.ShapeDtypeStruct((jac_rows, features), F32),
        ],
        scratch_shapes=[
            pltpu.VMEM((4, assets, LANES), F32),
            pltpu.VMEM((16 + 2 * features, width), BF16),
            pltpu.VMEM((5 * assets, width), BF16),
            pltpu.VMEM((5 * assets, width), BF16),
            pltpu.VMEM((16 + features, 2 * features), F32),
            pltpu.VMEM((16 + 2 * features, 5 * assets), F32),
            pltpu.VMEM((16 + features, 5 * assets), F32),
        ],
        compiler_params=params,
        name="sums",
    )(normals, spot, vol, weights, cash, taken)
    gram, jac = add_up([gram, jac], ("path", "grp"))
    solved = pl.pallas_call(
        functools.partial(solve_kernel, 1.0 / path_total),
        out_shape=jax.ShapeDtypeStruct((8, features), F32),
        scratch_shapes=[pltpu.VMEM((2, 8, 8, features), F32)],
        compiler_params=params,
        name="solve",
    )(gram)
    value, cot, flow, greeks = pl.pallas_call(
        functools.partial(adjoint_kernel, assets, width, path_total),
        grid=grid,
        in_specs=[
            tile, tile, line, line, line, line,
            full(8, features), full(jac_rows, features), whole, whole, whole,
        ],
        out_specs=[line, tile, line, full(2, assets)],
        out_shape=[row, big, row, jax.ShapeDtypeStruct((2, assets), F32)],
        scratch_shapes=[pltpu.VMEM((20, assets, LANES), F32)],
        compiler_params=params,
        name="adjoint",
    )(scaled, bounded, cash, taken, value, pull, solved, jac, spot, vol, weights)
    return value.reshape(paths), cot, flow.reshape(paths), greeks


def solution(mesh):
    in_specs = (P(None, ("grp", "path")), P(), P(), P(), P(("grp", "path")), P(("grp", "path")))
    out_specs = (P(("grp", "path")), P(None, ("grp", "path")), P(("grp", "path")), P())
    return jax.shard_map(
        per_device, mesh=mesh, in_specs=in_specs, out_specs=out_specs, check_vma=False
    )
```

time: 408 us -> 53.1 us (0.13)
  other arithmetic: 151 us -> 0.11 us
  blocking collectives: 82.9 us -> 0 us
  waiting for transfers between devices: 75.9 us -> 11.2 us
  local copies, waits for them, and re-layouts: 40.1 us -> 3.65 us
  matrix products: 24.6 us -> 0 us
  Pallas kernels: 0 us -> 22.6 us
  between operations: 15.5 us -> 0.73 us
  starting transfers between devices: 0.04 us -> 14.5 us
  loops' own time: 14.4 us -> 0 us
    psum x2 -> x0, blocking collectives: 82.9 us -> none  [the longest x1 42 us: per_device(): gram_sum, moment_sum = lax.psum((gram_acc, moment_acc), ('grp', 'path'))]
    psum x1 -> x0, waiting for transfers between devices: 75.8 us -> none  [per_device(): gram_sum, moment_sum = lax.psum((gram_acc, moment_acc), ('grp', 'path'))]
    reduce_sum x32 -> x0, other arithmetic: 53.3 us -> none  [the longest x16 31.9 us: payoff(): jnp.sum(weights[:, None] * state, axis=0) / jnp.sum(weights * spot_today)]
    mul x145 -> x0, other arithmetic: 46.8 us -> none  [the longest x32 33.1 us: basis_rows(): squares = (scaled * scaled - 1.0) * inv_root_two]
    dot_general x48 -> x0, matrix products: 24.2 us -> none  [the longest x16 10.8 us: gram_step(): lax.dot_general(basis_block, basis_block, contract_last, precision=highes...]
    another operation x5 -> x0, other arithmetic: 22.9 us -> none  [the longest x3 12.4 us: per_device(): factor = jnp.linalg.cholesky(gram_mean)]
    pallas_call x0 -> x3, Pallas kernels: none -> 22.6 us  [the longest x1 12.5 us: per_device(): pl.pallas_call(functools.partial(sums_kernel, assets, width), grid=grid,...]
    concatenate x32 -> x0, local copies, waits for them, and re-layouts: 21.9 us -> none  [basis_rows(): jnp.concatenate([leading, scaled, squares, neighbour, bounded], axis=0)]
  transfers between devices with their start and end apart: 1 -> 10, of which waited for: 1 -> 8; matrix products, arithmetic and copies ran while one was open for 0% -> 0% of each run, Pallas kernels for 0% -> 8%
where the time goes in v1:
time: 53.1 us; the launch traced here: 52.8 us
  Pallas kernels  22.6 us (43%)
  starting transfers between devices  14.5 us (27%)
  waiting for transfers between devices  11.2 us (21%)
  local copies, waits for them, and re-layouts  3.65 us (7%)
  between operations  0.73 us (1%)
    ppermute x10, starting transfers between devices, add_up(): values = [v + lax.ppermute(v, axis, pairs) for v in values]  14.5 us
    pallas_call x1, Pallas kernels, per_device(): pl.pallas_call(functools.partial(sums_kernel, assets, width), grid=grid,...  12.5 us
    ppermute x10, waiting for transfers between devices, add_up(): values = [v + lax.ppermute(v, axis, pairs) for v in values]  11.2 us
    pallas_call x1, Pallas kernels, per_device(): pl.pallas_call(functools.partial(adjoint_kernel, assets, width, path_tota...  5.84 us
    pallas_call x1, Pallas kernels, per_device(): pl.pallas_call(functools.partial(solve_kernel, 1.0 / path_total), out_sha...  4.22 us
    unnamed x18, local copies, waits for them, and re-layouts  3.65 us
  transfers between devices with their start and end apart: 10, of which 8 were waited for; matrix products, arithmetic and copies ran while one was open for 0% of the time, Pallas kernels for 8%

profile of v1, /device:TPU:0, one launch (start us, length us, event | category | flops | bytes accessed | tf_op | source)
XLA Modules:
  0.0 52.8 jit_solution(5219271487088730689)
XLA Ops:
  0.6 0.0 copy-start
  0.6 0.8 %copy-done = f32[16384]{0:T(1024)S(1)} copy-done((f32[16384]{0:T(1024)S(1)}, f32[16384]{0:T(1024)}, u32[]{:S(2)}) %copy-start) | copy-done | bytes 65560
  1.5 0.0 copy-start.2
  1.5 0.8 %copy-done.2 = s32[16384]{0:T(1024)S(1)} copy-done((s32[16384]{0:T(1024)S(1)}, s32[16384]{0:T(1024)}, u32[]{:S(2)}) %copy-start.2) | copy-done | bytes 65560
  2.3 0.0 copy-start.3
  2.3 0.7 %copy-done.3 = f32[32]{0:T(128)S(1)} copy-done((f32[32]{0:T(128)S(1)}, f32[32]{0:T(128)}, u32[]{:S(2)}) %copy-start.3) | copy-done | bytes 152
  3.0 0.0 copy-start.5
  3.0 0.7 %copy-done.5 = f32[32]{0:T(128)S(1)} copy-done((f32[32]{0:T(128)S(1)}, f32[32]{0:T(128)}, u32[]{:S(2)}) %copy-start.5) | copy-done | bytes 152
  3.6 0.0 copy-start.7
  3.6 0.7 %copy-done.7 = f32[32]{0:T(128)S(1)} copy-done((f32[32]{0:T(128)S(1)}, f32[32]{0:T(128)}, u32[]{:S(2)}) %copy-start.7) | copy-done | bytes 152
  4.3 0.0 copy-start.1
  4.3 0.0 copy-start.4
  4.3 0.0 copy-start.6
  4.3 0.0 copy-start.8
  4.3 12.5 %sums.1 = (f32[32,16384]{1,0:T(8,128)S(1)}, f32[32,16384]{1,0:T(8,128)S(1)}, f32[1,16384]{1,0:T(1,128)S(1)}, f32[1,16384]{1,0:T(1,128)S(1)}, f32[136,128]{1,0:T(8,128)S(1)}, /*index=5*/f32[176,128]{1,0:T(8,128)S(1)}) custom-call(f32[32,16384]{1,0:T(8,128)} %normals.1, f32[1,32]{1,0:T(1,128)S(1)} %bitcast.11, f32[1,32]{1,0:T(1,128)S(1)} %bitcast.13, ...), custom_call_target="tpu_custom_call" | custom-call | tf_op jit(solution)/shard_map/sums/pallas_call | solution.py:311
  16.8 0.5 collective-permute-start.5
  17.3 0.9 %collective-permute-done.5 = f32[176,128]{1,0:T(8,128)S(1)} collective-permute-done((f32[176,128]{1,0:T(8,128)S(1)}, f32[176,128]{1,0:T(8,128)S(1)}, u32[]{:S(2)}, u32[]{:S(2)}) %collective-permute-start.5) | collective-permute-done | bytes 90144 | tf_op jit(solution)/shard_map/ppermute | solution.py:290
  18.3 2.9 %collective-permute-start.6 = (f32[176,128]{1,0:T(8,128)S(1)}, f32[176,128]{1,0:T(8,128)S(1)}, u32[]{:S(2)}, u32[]{:S(2)}) collective-permute-start(f32[176,128]{1,0:T(8,128)S(1)} %add.35), channel_id=1, source_target_pairs={{0,2},{1,3},{2,0},{3,1},{4,6},{5,7},{6,4},{7,5},{8,10},{9,11},{10,... | collective-permute-start | bytes 270344 | tf_op jit(solution)/shard_map/ppermute | solution.py:290
  21.2 0.0 collective-permute-start
  21.2 1.3 %collective-permute-done = f32[136,128]{1,0:T(8,128)S(1)} collective-permute-done((f32[136,128]{1,0:T(8,128)S(1)}, f32[136,128]{1,0:T(8,128)S(1)}, u32[]{:S(2)}, u32[]{:S(2)}) %collective-permute-start) | collective-permute-done | bytes 69664 | tf_op jit(solution)/shard_map/ppermute | solution.py:290
  22.5 0.1 collective-permute-start.1
  22.6 1.5 %collective-permute-done.6 = f32[176,128]{1,0:T(8,128)S(1)} collective-permute-done((f32[176,128]{1,0:T(8,128)S(1)}, f32[176,128]{1,0:T(8,128)S(1)}, u32[]{:S(2)}, u32[]{:S(2)}) %collective-permute-start.6) | collective-permute-done | bytes 90144 | tf_op jit(solution)/shard_map/ppermute | solution.py:290
  24.2 1.9 %collective-permute-start.7 = (f32[176,128]{1,0:T(8,128)S(1)}, f32[176,128]{1,0:T(8,128)S(1)}, u32[]{:S(2)}, u32[]{:S(2)}) collective-permute-start(f32[176,128]{1,0:T(8,128)S(1)} %add.36), channel_id=1, source_target_pairs={{0,4},{1,5},{2,6},{3,7},{4,0},{5,1},{6,2},{7,3},{8,12},{9,13},{10,... | collective-permute-start | bytes 270344 | tf_op jit(solution)/shard_map/ppermute | solution.py:290
  26.0 0.8 %collective-permute-done.1 = f32[136,128]{1,0:T(8,128)S(1)} collective-permute-done((f32[136,128]{1,0:T(8,128)S(1)}, f32[136,128]{1,0:T(8,128)S(1)}, u32[]{:S(2)}, u32[]{:S(2)}) %collective-permute-start.1) | collective-permute-done | bytes 69664 | tf_op jit(solution)/shard_map/ppermute | solution.py:290
  26.9 1.6 %collective-permute-start.2 = (f32[136,128]{1,0:T(8,128)S(1)}, f32[136,128]{1,0:T(8,128)S(1)}, u32[]{:S(2)}, u32[]{:S(2)}) collective-permute-start(f32[136,128]{1,0:T(8,128)S(1)} %add.31), channel_id=1, source_target_pairs={{0,4},{1,5},{2,6},{3,7},{4,0},{5,1},{6,2},{7,3},{8,12},{9,13},{10,... | collective-permute-start | bytes 208904 | tf_op jit(solution)/shard_map/ppermute | solution.py:290
  28.5 0.5 collective-permute-done.7
  29.0 3.1 %collective-permute-start.8 = (f32[176,128]{1,0:T(8,128)S(1)}, f32[176,128]{1,0:T(8,128)S(1)}, u32[]{:S(2)}, u32[]{:S(2)}) collective-permute-start(f32[176,128]{1,0:T(8,128)S(1)} %add.37), channel_id=1, source_target_pairs={{0,8},{1,9},{2,10},{3,11},{4,12},{5,13},{6,14},{7,15},{8,0},{9,1},... | collective-permute-start | bytes 270344 | tf_op jit(solution)/shard_map/ppermute | solution.py:290
  32.2 0.1 collective-permute-done.2
  32.2 1.9 %collective-permute-start.3 = (f32[136,128]{1,0:T(8,128)S(1)}, f32[136,128]{1,0:T(8,128)S(1)}, u32[]{:S(2)}, u32[]{:S(2)}) collective-permute-start(f32[136,128]{1,0:T(8,128)S(1)} %add.32), channel_id=1, source_target_pairs={{0,8},{1,9},{2,10},{3,11},{4,12},{5,13},{6,14},{7,15},{8,0},{9,1},... | collective-permute-start | bytes 208904 | tf_op jit(solution)/shard_map/ppermute | solution.py:290
  34.1 2.5 %collective-permute-done.8 = f32[176,128]{1,0:T(8,128)S(1)} collective-permute-done((f32[176,128]{1,0:T(8,128)S(1)}, f32[176,128]{1,0:T(8,128)S(1)}, u32[]{:S(2)}, u32[]{:S(2)}) %collective-permute-start.8) | collective-permute-done | bytes 90144 | tf_op jit(solution)/shard_map/ppermute | solution.py:290
  36.7 1.6 %collective-permute-start.9 = (f32[176,128]{1,0:T(8,128)S(1)}, f32[176,128]{1,0:T(8,128)S(1)}, u32[]{:S(2)}, u32[]{:S(2)}) collective-permute-start(f32[176,128]{1,0:T(8,128)S(1)} %add.38), channel_id=1, source_target_pairs={{0,16},{16,0},{1,17},{17,1},{2,18},{18,2},{3,19},{19,3},{4,20},{20... | collective-permute-start | bytes 270344 | tf_op jit(solution)/shard_map/ppermute | solution.py:290
  38.3 0.0 collective-permute-done.3
  38.3 0.8 %collective-permute-start.4 = (f32[136,128]{1,0:T(8,128)S(1)}, f32[136,128]{1,0:T(8,128)S(1)}, u32[]{:S(2)}, u32[]{:S(2)}) collective-permute-start(f32[136,128]{1,0:T(8,128)S(1)} %add.33), channel_id=1, source_target_pairs={{0,16},{16,0},{1,17},{17,1},{2,18},{18,2},{3,19},{19,3},{4,20},{20... | collective-permute-start | bytes 208904 | tf_op jit(solution)/shard_map/ppermute | solution.py:290
  39.1 3.6 %collective-permute-done.4 = f32[136,128]{1,0:T(8,128)S(1)} collective-permute-done((f32[136,128]{1,0:T(8,128)S(1)}, f32[136,128]{1,0:T(8,128)S(1)}, u32[]{:S(2)}, u32[]{:S(2)}) %collective-permute-start.4) | collective-permute-done | bytes 69664 | tf_op jit(solution)/shard_map/ppermute | solution.py:290
  42.7 4.2 %solve.1.solved = f32[8,128]{1,0:T(8,128)S(1)} custom-call(f32[136,128]{1,0:T(8,128)S(1)} %add.34.gram), custom_call_target="tpu_custom_call" | custom-call | tf_op jit(solution)/shard_map/solve/pallas_call | solution.py:334
  46.9 0.0 collective-permute-done.9
  46.9 0.0 copy-done.1
  47.0 0.0 copy-done.4
  47.0 0.0 copy-done.6
  47.0 0.0 copy-done.8
  47.0 5.8 %adjoint.1 = (f32[1,16384]{1,0:T(1,128)}, f32[32,16384]{1,0:T(8,128)}, f32[1,16384]{1,0:T(1,128)}, f32[2,32]{1,0:T(2,128)}) custom-call(f32[32,16384]{1,0:T(8,128)S(1)} %get-tuple-element.14.scaled_in, f32[32,16384]{1,0:T(8,128)S(1)} %get-tuple-element.15.bounded_in, f32[1,16384]{1,0:T(1,128)S(1)} %bitcast.8, s32[1,16384]{1,0:T(1,128)S(1)} %bitcast.10, ...), custom_call_target="tpu_custom_call" | custom-call | tf_op jit(solution)/shard_map/adjoint/pallas_call | solution.py:341
  (10 shorter events, 0.1 us)
Async XLA Ops:
  0.6 0.8 %copy-start = (f32[16384]{0:T(1024)S(1)}, f32[16384]{0:T(1024)}, u32[]{:S(2)}) copy-start(f32[16384]{0:T(1024)} %param.10) | copy-start | bytes 196612
  1.5 0.8 %copy-start.2 = (s32[16384]{0:T(1024)S(1)}, s32[16384]{0:T(1024)}, u32[]{:S(2)}) copy-start(s32[16384]{0:T(1024)} %param.11) | copy-start | bytes 196612
  2.3 0.7 %copy-start.3 = (f32[32]{0:T(128)S(1)}, f32[32]{0:T(128)}, u32[]{:S(2)}) copy-start(f32[32]{0:T(128)} %param.7) | copy-start | bytes 388
  3.0 0.7 %copy-start.5 = (f32[32]{0:T(128)S(1)}, f32[32]{0:T(128)}, u32[]{:S(2)}) copy-start(f32[32]{0:T(128)} %param.8) | copy-start | bytes 388
  3.6 0.7 %copy-start.7 = (f32[32]{0:T(128)S(1)}, f32[32]{0:T(128)}, u32[]{:S(2)}) copy-start(f32[32]{0:T(128)} %param.9) | copy-start | bytes 388
  4.3 42.7 %copy-start.1 = (f32[16384]{0:T(1024)S(1)}, f32[16384]{0:T(1024)}, u32[]{:S(2)}) copy-start(f32[16384]{0:T(1024)} %param.10) | copy-start | bytes 196612
  4.3 42.7 %copy-start.4 = (f32[32]{0:T(128)S(1)}, f32[32]{0:T(128)}, u32[]{:S(2)}) copy-start(f32[32]{0:T(128)} %param.7) | copy-start | bytes 388
  4.3 42.7 %copy-start.6 = (f32[32]{0:T(128)S(1)}, f32[32]{0:T(128)}, u32[]{:S(2)}) copy-start(f32[32]{0:T(128)} %param.8) | copy-start | bytes 388
  4.3 42.7 %copy-start.8 = (f32[32]{0:T(128)S(1)}, f32[32]{0:T(128)}, u32[]{:S(2)}) copy-start(f32[32]{0:T(128)} %param.9) | copy-start | bytes 388
  16.8 1.5 %collective-permute-start.5 = (f32[176,128]{1,0:T(8,128)S(1)}, f32[176,128]{1,0:T(8,128)S(1)}, u32[]{:S(2)}, u32[]{:S(2)}) collective-permute-start(f32[176,128]{1,0:T(8,128)S(1)} %get-tuple-element.19), channel_id=1, source_target_pairs={{0,1},{1,0},{2,3},{3,2},{4,5},{5,4},{6,7},{7,6},{8,9},{9,8},{10,11... | collective-permute-start | bytes 270344 | tf_op jit(solution)/shard_map/ppermute | solution.py:290
  18.3 5.9 %collective-permute-start.6 = (f32[176,128]{1,0:T(8,128)S(1)}, f32[176,128]{1,0:T(8,128)S(1)}, u32[]{:S(2)}, u32[]{:S(2)}) collective-permute-start(f32[176,128]{1,0:T(8,128)S(1)} %add.35), channel_id=1, source_target_pairs={{0,2},{1,3},{2,0},{3,1},{4,6},{5,7},{6,4},{7,5},{8,10},{9,11},{10,... | collective-permute-start | bytes 270344 | tf_op jit(solution)/shard_map/ppermute | solution.py:290
  21.2 1.3 %collective-permute-start = (f32[136,128]{1,0:T(8,128)S(1)}, f32[136,128]{1,0:T(8,128)S(1)}, u32[]{:S(2)}, u32[]{:S(2)}) collective-permute-start(f32[136,128]{1,0:T(8,128)S(1)} %get-tuple-element.18), channel_id=1, source_target_pairs={{0,1},{1,0},{2,3},{3,2},{4,5},{5,4},{6,7},{7,6},{8,9},{9,8},{10,11... | collective-permute-start | bytes 208904 | tf_op jit(solution)/shard_map/ppermute | solution.py:290
  22.5 4.4 %collective-permute-start.1 = (f32[136,128]{1,0:T(8,128)S(1)}, f32[136,128]{1,0:T(8,128)S(1)}, u32[]{:S(2)}, u32[]{:S(2)}) collective-permute-start(f32[136,128]{1,0:T(8,128)S(1)} %add.30), channel_id=1, source_target_pairs={{0,2},{1,3},{2,0},{3,1},{4,6},{5,7},{6,4},{7,5},{8,10},{9,11},{10,... | collective-permute-start | bytes 208904 | tf_op jit(solution)/shard_map/ppermute | solution.py:290
  24.2 4.9 %collective-permute-start.7 = (f32[176,128]{1,0:T(8,128)S(1)}, f32[176,128]{1,0:T(8,128)S(1)}, u32[]{:S(2)}, u32[]{:S(2)}) collective-permute-start(f32[176,128]{1,0:T(8,128)S(1)} %add.36), channel_id=1, source_target_pairs={{0,4},{1,5},{2,6},{3,7},{4,0},{5,1},{6,2},{7,3},{8,12},{9,13},{10,... | collective-permute-start | bytes 270344 | tf_op jit(solution)/shard_map/ppermute | solution.py:290
  26.9 5.3 %collective-permute-start.2 = (f32[136,128]{1,0:T(8,128)S(1)}, f32[136,128]{1,0:T(8,128)S(1)}, u32[]{:S(2)}, u32[]{:S(2)}) collective-permute-start(f32[136,128]{1,0:T(8,128)S(1)} %add.31), channel_id=1, source_target_pairs={{0,4},{1,5},{2,6},{3,7},{4,0},{5,1},{6,2},{7,3},{8,12},{9,13},{10,... | collective-permute-start | bytes 208904 | tf_op jit(solution)/shard_map/ppermute | solution.py:290
  29.0 7.6 %collective-permute-start.8 = (f32[176,128]{1,0:T(8,128)S(1)}, f32[176,128]{1,0:T(8,128)S(1)}, u32[]{:S(2)}, u32[]{:S(2)}) collective-permute-start(f32[176,128]{1,0:T(8,128)S(1)} %add.37), channel_id=1, source_target_pairs={{0,8},{1,9},{2,10},{3,11},{4,12},{5,13},{6,14},{7,15},{8,0},{9,1},... | collective-permute-start | bytes 270344 | tf_op jit(solution)/shard_map/ppermute | solution.py:290
  32.2 6.1 %collective-permute-start.3 = (f32[136,128]{1,0:T(8,128)S(1)}, f32[136,128]{1,0:T(8,128)S(1)}, u32[]{:S(2)}, u32[]{:S(2)}) collective-permute-start(f32[136,128]{1,0:T(8,128)S(1)} %add.32), channel_id=1, source_target_pairs={{0,8},{1,9},{2,10},{3,11},{4,12},{5,13},{6,14},{7,15},{8,0},{9,1},... | collective-permute-start | bytes 208904 | tf_op jit(solution)/shard_map/ppermute | solution.py:290
  36.7 10.3 %collective-permute-start.9 = (f32[176,128]{1,0:T(8,128)S(1)}, f32[176,128]{1,0:T(8,128)S(1)}, u32[]{:S(2)}, u32[]{:S(2)}) collective-permute-start(f32[176,128]{1,0:T(8,128)S(1)} %add.38), channel_id=1, source_target_pairs={{0,16},{16,0},{1,17},{17,1},{2,18},{18,2},{3,19},{19,3},{4,20},{20... | collective-permute-start | bytes 270344 | tf_op jit(solution)/shard_map/ppermute | solution.py:290
  38.3 4.4 %collective-permute-start.4 = (f32[136,128]{1,0:T(8,128)S(1)}, f32[136,128]{1,0:T(8,128)S(1)}, u32[]{:S(2)}, u32[]{:S(2)}) collective-permute-start(f32[136,128]{1,0:T(8,128)S(1)} %add.33), channel_id=1, source_target_pairs={{0,16},{16,0},{1,17},{17,1},{2,18},{18,2},{3,19},{19,3},{4,20},{20... | collective-permute-start | bytes 208904 | tf_op jit(solution)/shard_map/ppermute | solution.py:290

commit v2 on v0

v2 whole, which is shorter than its diff:
```python
import functools
import math

import jax
import jax.numpy as jnp
from jax import lax
from jax.experimental import pallas as pl
from jax.experimental.pallas import tpu as pltpu
from jax.sharding import PartitionSpec as P

root_time = math.sqrt(0.5)
notional = 20.0
soft_width = 0.02
LANES = 128
F32 = jnp.float32
BF16 = jnp.bfloat16
AXES = ("grp", "path")
CONTRACT_LAST = (((1,), (1,)), ((), ()))


def column(row, count):
    rows = lax.broadcasted_iota(jnp.int32, (count, count), 0)
    cols = lax.broadcasted_iota(jnp.int32, (count, count), 1)
    wide = jnp.broadcast_to(row, (count, count))
    picked = jnp.sum(jnp.where(rows == cols, wide, 0.0), axis=1, keepdims=True)
    return jnp.broadcast_to(picked, (count, LANES))


def split(x):
    hi = x.astype(BF16)
    lo = (x - hi.astype(F32)).astype(BF16)
    return hi, lo


def halves(rows):
    odd = lax.axis_index("path") & 1
    at = lambda index: pl.ds(pl.multiple_of(index * rows, 8), rows)
    return at(odd), at(1 - odd)


def sums_kernel(
    assets, width, spot, vol, weights, cash, taken, normals,
    scaled_out, bounded_out, value_out, pull_out, gram_out, jac_keep, jac_give,
    small, flows, flags, draws, coef, part, target,
    scaled_all, bounded_all, rows_a, tilts_a, rows_b, tilts_b, gram_acc, jac_acc, jac_low, jac, sems, sent,
):
    features = 4 * assets
    paths = draws.shape[1]
    chunks = width // LANES
    blocks = paths // width
    copies = [
        pltpu.make_async_copy(spot, small.at[0:1, :], sems.at[0]),
        pltpu.make_async_copy(vol, small.at[1:2, :], sems.at[1]),
        pltpu.make_async_copy(weights, small.at[2:3, :], sems.at[2]),
        pltpu.make_async_copy(cash, flows, sems.at[3]),
        pltpu.make_async_copy(taken, flags, sems.at[4]),
    ]

    def pair(index):
        at = pl.ds(pl.multiple_of(index * (2 * width), 2 * width), 2 * width)
        return pltpu.make_async_copy(normals.at[:, at], draws.at[:, at], sems.at[5 + index])

    def leave(index):
        at = pl.ds(pl.multiple_of(index * (2 * width), 2 * width), 2 * width)
        return [
            pltpu.make_async_copy(scaled_all.at[:, at], scaled_out.at[:, at], sent.at[0, index]),
            pltpu.make_async_copy(bounded_all.at[:, at], bounded_out.at[:, at], sent.at[1, index]),
        ]

    for copy in copies[:3]:
        copy.start()
    for index in range(blocks // 2):
        pair(index).start()
        if index == 0:
            for copy in copies[3:]:
                copy.start()
    gram_acc[...] = jnp.zeros_like(gram_acc)
    jac_acc[...] = jnp.zeros_like(jac_acc)
    jac_low[...] = jnp.zeros_like(jac_low)
    rows_b[...] = jnp.zeros_like(rows_b)
    tilts_b[...] = jnp.zeros_like(tilts_b)
    target[...] = jnp.zeros_like(target)
    for copy in copies[:3]:
        copy.wait()
    spread = column(small[1:2, :] * root_time, assets)
    value = small[2:3, :] * small[0:1, :]
    total = jnp.sum(value, axis=1, keepdims=True)
    coef[0] = spread
    coef[1] = 0.5 * spread * spread
    coef[2] = 1.0 / spread
    coef[3] = column(value, assets) / jnp.broadcast_to(total, (assets, LANES))
    for copy in copies[3:]:
        copy.wait()

    last = lax.broadcasted_iota(jnp.int32, (assets, LANES), 0) == assets - 1

    def fill(block, rows, tilts):
        for c in range(chunks):
            at = pl.ds(pl.multiple_of(block * width, width) + c * LANES, LANES)
            here = pl.ds(c * LANES, LANES)
            draw = draws[:, at]
            spread = coef[0]
            growth = jnp.exp(spread * draw - coef[1])
            weighted = growth * coef[3]
            part[8 * c : 8 * c + 8, :] = sum(weighted[8 * g : 8 * g + 8] for g in range(assets // 8))
            scaled = (growth - 1.0) * coef[2]
            bounded = jnp.where(last, 1.0, jnp.tanh(scaled))
            scaled_all[:, at] = scaled
            bounded_all[:, at] = bounded
            after = pltpu.roll(scaled, assets - 1, 0)
            before = pltpu.roll(scaled, 1, 0)
            basis = jnp.concatenate(
                [scaled, scaled * scaled - 1.0, scaled * after, bounded], axis=0
            )
            hi, lo = split(basis)
            rows[16 : 16 + features, here] = hi
            rows[16 + features : 16 + 2 * features, here] = lo
            slope = growth * (draw - spread) - scaled
            curve = 1.0 - bounded * bounded
            hi, lo = split(
                jnp.concatenate(
                    [slope, slope * scaled, slope * after, slope * curve, slope * before], axis=0
                )
            )
            tilts[0 : 5 * assets, here] = hi
            tilts[5 * assets : 10 * assets, here] = lo
        line = pl.ds(pl.multiple_of(block * chunks, chunks), chunks)
        basket = sum(part[pl.ds(i, chunks, stride=8), :] for i in range(8))
        x = (basket - 1.0) * (1.0 / soft_width)
        decay = jnp.exp(-jnp.abs(x))
        reward = (notional * soft_width) * (jnp.maximum(x, 0.0) + jnp.log1p(decay))
        inverse = 1.0 / (1.0 + decay)
        sigmoid = jnp.where(x >= 0.0, inverse, decay * inverse)
        flag = flags[line, :].astype(F32)
        flow = flows[line, :]
        pull = notional * flag * sigmoid
        value_out[line, :] = flag * reward
        pull_out[line, :] = pull
        flow_hi = flow.astype(BF16).astype(F32)
        pull_hi = pull.astype(BF16).astype(F32)
        for c in range(chunks):
            here = pl.ds(c * LANES, LANES)
            for index, row in enumerate(
                [flow_hi, flow - flow_hi, 1.0 - flag, pull_hi, pull - pull_hi]
            ):
                target[index : index + 1, here] = row[c : c + 1, :]
        rows[0:16, :] = target[...].astype(BF16)

    def multiply(rows, tilts):
        upper = rows[0 : 16 + features, :]
        gram_acc[...] += lax.dot_general(
            upper, rows[16:, :], CONTRACT_LAST, preferred_element_type=F32
        )
        jac_acc[...] += lax.dot_general(
            rows[...], tilts[0 : 5 * assets, :], CONTRACT_LAST, preferred_element_type=F32
        )
        jac_low[...] += lax.dot_general(
            upper, tilts[5 * assets :, :], CONTRACT_LAST, preferred_element_type=F32
        )

    def both(index, carry):
        pair(index).wait()
        multiply(rows_b, tilts_b)
        fill(2 * index, rows_a, tilts_a)
        multiply(rows_a, tilts_a)
        fill(2 * index + 1, rows_b, tilts_b)
        for copy in leave(index):
            copy.start()
        return carry

    lax.fori_loop(0, blocks // 2, both, 0)
    multiply(rows_b, tilts_b)

    def targets(t):
        pairs = [t[0:1] + t[1:2], t[2:3], t[3:4] + t[4:5], jnp.zeros((5, t.shape[1]), F32)]
        return jnp.concatenate(pairs, axis=0)

    mid = features // 2
    high = gram_acc[16:, 0:features]
    half = 0.5 * high + gram_acc[16:, features:]
    gram = half + half.T
    turned = pltpu.roll(gram[mid:, :], mid, 1)
    lanes = lax.broadcasted_iota(jnp.int32, (mid, features), 1)
    subs = lax.broadcasted_iota(jnp.int32, (mid, features), 0)
    gram_out[0:mid, :] = jnp.where(lanes >= subs, gram[0:mid, :], turned)
    corner = jnp.sum(jnp.where(lanes == subs, turned, 0.0), axis=0, keepdims=True)
    aims = targets(gram_acc[0:16, 0:features] + gram_acc[0:16, features:])
    rank = lax.broadcasted_iota(jnp.int32, (8, features), 0)
    gram_out[mid:, :] = jnp.where(rank == 3, jnp.broadcast_to(corner, (8, features)), aims)
    full = jac_acc[16 : 16 + features, :] + jac_acc[16 + features :, :] + jac_low[16:, :]
    aims = targets(jac_acc[0:16, :] + jac_low[0:16, :])
    jac[0:features, :] = full[:, 0:features]
    jac[features : features + assets, :] = jnp.concatenate(
        [full[assets * g : assets * (g + 1), features:] for g in range(4)], axis=1
    )
    jac[features + assets : features + assets + 8, :] = aims[:, 0:features]
    jac[features + assets + 8 :, :] = jnp.concatenate(
        [aims[:, features:], jnp.zeros((8, features - assets), F32)], axis=1
    )
    mine, other = halves(jac_keep.shape[0])
    jac_keep[...] = jac[mine, :]
    jac_give[...] = jac[other, :]
    for index in range(blocks // 2):
        for copy in leave(index):
            copy.wait()


def lane(block, index):
    return jnp.broadcast_to(block[:, index : index + 1], block.shape)


def solve_kernel(packed, out, spread):
    features = packed.shape[1]
    blocks = features // 8
    mid = features // 2
    lanes = lax.broadcasted_iota(jnp.int32, (mid, features), 1)
    subs = lax.broadcasted_iota(jnp.int32, (mid, features), 0)
    upper = packed[0:mid, :]
    aims = packed[mid:, :]
    corner = jnp.broadcast_to(aims[3:4], (mid, features))
    lower = jnp.where(lanes < subs, upper, jnp.where(lanes == subs, 0.5 * corner, 0.0))
    half = jnp.concatenate(
        [
            jnp.where(lanes == subs, 0.5 * upper, jnp.where(lanes > subs, upper, 0.0)),
            pltpu.roll(lower, mid, 1),
        ],
        axis=0,
    )
    gram = half + half.T
    lanes = lax.broadcasted_iota(jnp.int32, (8, features), 1)
    subs = lax.broadcasted_iota(jnp.int32, (8, features), 0)
    mat = [gram[8 * v : 8 * v + 8, :] for v in range(blocks)] + [aims]
    for k in range(blocks):
        base = 8 * k
        head = mat[k]
        diag = {}
        for j in range(8):
            col = lane(head, base + j)
            spread[0, j] = col
            for i in range(j + 1):
                diag[i, j] = jnp.broadcast_to(spread[0, j, i : i + 1, :], (8, features))
        inside = (lanes >= base) & (lanes < base + 8)
        spread[1, 0] = jnp.where(inside, jnp.where(lanes == base + subs, -1.0, 0.0), head)
        work = [jnp.broadcast_to(spread[1, 0, i : i + 1, :], (8, features)) for i in range(8)]
        inverse, low = [], {}
        for p in range(8):
            inv = 1.0 / diag[p, p]
            inverse.append(inv)
            for j in range(p + 1, 8):
                low[p, j] = diag[p, j] * inv
            for i in range(p + 1, 8):
                for j in range(i, 8):
                    diag[i, j] = diag[i, j] - low[p, i] * diag[p, j]
                work[i] = work[i] - low[p, i] * work[p]
        for i in reversed(range(8)):
            value = work[i] * inverse[i]
            for j in range(i + 1, 8):
                value = value - low[i, j] * work[j]
            work[i] = value
        for v in range(k + 1, blocks + 1):
            new = jnp.where(inside, 0.0, mat[v])
            for c in range(8):
                new = new - lane(mat[v], base + c) * work[c]
            mat[v] = new
    kept = jnp.broadcast_to(aims[2:3], (8, features))
    out[...] = jnp.where(subs == 3, kept, mat[blocks])


def adjoint_kernel(
    assets, width,
    solved, jac_mine, jac_other, spot, vol, weights, cash, taken,
    value_in, pull_in, scaled_in, bounded_in,
    value_out, flow_out, greeks_out, cot_out,
    coef, part, line, tangents, cot, jac, sent,
):
    features = 4 * assets
    paths = scaled_in.shape[1]
    chunks = width // LANES
    turned = solved[...].T
    spread = column(vol[...] * root_time, assets)
    base = column(spot[...], assets)
    weight = column(weights[...], assets)
    total = jnp.sum(weights[...] * spot[...], axis=1, keepdims=True)
    offsets = []
    for which in range(2):
        parts = [
            jnp.broadcast_to(turned[assets * g : assets * (g + 1), which : which + 1], (assets, LANES))
            for g in range(4)
        ]
        for g in range(4):
            coef[5 * which + g] = parts[g]
        coef[5 * which + 4] = pltpu.roll(parts[2], 1, 0)
        offsets.append(jnp.sum(parts[1], axis=0, keepdims=True))
    coef[10] = 1.0 / (base * spread)
    coef[11] = weight / jnp.broadcast_to(total, (assets, LANES))

    def leave(index):
        at = pl.ds(pl.multiple_of(index * (2 * width), 2 * width), 2 * width)
        return pltpu.make_async_copy(cot.at[:, at], cot_out.at[:, at], sent.at[index])

    def block(index, slot):
        for c in range(chunks):
            at = pl.ds(pl.multiple_of(index * width, width) + c * LANES, LANES)
            here = pl.ds(c * LANES, LANES)
            scaled = scaled_in[:, at]
            bounded = bounded_in[:, at]
            after = pltpu.roll(scaled, assets - 1, 0)
            before = pltpu.roll(scaled, 1, 0)
            curve = 1.0 - bounded * bounded
            for which in range(2):
                k = 5 * which
                bend = coef[k + 1] * scaled
                inner = coef[k] + bend + coef[k + 2] * after
                terms = scaled * inner + coef[k + 3] * bounded
                part[slot, which, 8 * c : 8 * c + 8, :] = sum(
                    terms[8 * g : 8 * g + 8] for g in range(assets // 8)
                )
                tangents[slot, which, :, here] = (
                    inner + bend + coef[k + 4] * before + coef[k + 3] * curve
                )
        at = pl.ds(pl.multiple_of(index * chunks, chunks), chunks)
        fitted = [
            sum(part[slot, which, pl.ds(i, chunks, stride=8), :] for i in range(8)) - offsets[which]
            for which in range(2)
        ]
        rest = 1.0 - taken[at, :].astype(F32)
        value_out[at, :] = value_in[at, :] + rest * fitted[0]
        flow_out[at, :] = fitted[1]
        line[slot, 0] = cash[at, :] - fitted[0]
        line[slot, 1] = rest - fitted[1]
        line[slot, 2] = pull_in[at, :]
        for c in range(chunks):
            at = pl.ds(pl.multiple_of(index * width, width) + c * LANES, LANES)
            here = pl.ds(c * LANES, LANES)
            miss, gap, pull = (
                jnp.broadcast_to(line[slot, i, c : c + 1, :], (assets, LANES)) for i in range(3)
            )
            cot[:, at] = (
                miss * tangents[slot, 1, :, here] + gap * tangents[slot, 0, :, here]
            ) * coef[10] + pull * coef[11]

    def both(index, carry):
        block(2 * index, 0)
        block(2 * index + 1, 1)
        leave(index).start()
        return carry

    lax.fori_loop(0, paths // (2 * width), both, 0)

    mine, other = halves(jac_mine.shape[0])
    jac[mine, :] = jac_mine[...]
    jac[other, :] = jac_other[...]
    regression, multiplier = solved[0:1, :], solved[1:2, :]
    group = lax.broadcasted_iota(jnp.int32, (assets, LANES), 1) // assets

    def against(which):
        main = jnp.sum(jac[0:features, :] * turned[:, which : which + 1], axis=0, keepdims=True)
        packed = jnp.zeros((assets, LANES), F32)
        for g in range(4):
            part = turned[assets * g : assets * (g + 1), which : which + 1]
            packed = jnp.where(group == g, jnp.broadcast_to(part, (assets, LANES)), packed)
        side = jnp.sum(jac[features : features + assets, :] * packed, axis=0, keepdims=True)
        side = side + pltpu.roll(side, 2 * assets, 1)
        side = side + pltpu.roll(side, assets, 1)
        return main, side

    aims = features + assets
    main_r, side_r = against(0)
    main_m, side_m = against(1)
    miss, gap = jac[aims : aims + 1, :] - main_r, jac[aims + 1 : aims + 2, :] - main_m
    miss_side = jac[aims + 8 : aims + 9, :] - side_r
    gap_side = jac[aims + 9 : aims + 10, :] - side_m
    lanes = lax.broadcasted_iota(jnp.int32, (1, LANES), 1)
    double = jnp.where((lanes >= assets) & (lanes < 2 * assets), 2.0, 1.0)
    total = double * (multiplier * miss + regression * gap)
    total = total + pltpu.roll(total, 2 * assets, 1)
    total = total + pltpu.roll(total, assets, 1)

    def earlier(row):
        moved = pltpu.roll(row, features - 2 * assets + 1, 1)
        wrapped = pltpu.roll(row, features - 3 * assets + 1, 1)
        return jnp.where(lanes == 0, wrapped, moved)

    total = total + earlier(multiplier) * miss_side + earlier(regression) * gap_side
    vega = total[:, 0:assets] / vol[...]
    pulled_slope = jac[aims + 2 : aims + 3, 0:assets]
    pulled_scaled = solved[3:4, 0:assets]
    pulled = solved[3:4, features - 1 : features]
    value = weights[...] * spot[...]
    whole = jnp.sum(value, axis=1, keepdims=True)
    growth = pulled + vol[...] * root_time * pulled_scaled
    mean = jnp.sum(value * growth, axis=1, keepdims=True) / whole
    delta = weights[...] / whole * (growth - mean)
    vega = vega + value * root_time / whole * (pulled_slope + pulled_scaled)
    greeks_out[...] = jnp.concatenate([delta, vega], axis=0)
    for index in range(paths // (2 * width)):
        leave(index).wait()


def swap(value, mask):
    count = math.prod(lax.axis_size(axis) for axis in AXES)
    return lax.ppermute(value, AXES, [(i, i ^ mask) for i in range(count)])


def gather_sum(value, masks):
    combos = [0]
    for mask in masks:
        combos = combos + [c ^ mask for c in combos]
    terms = [value] + [swap(value, c) for c in combos[1:]]
    while len(terms) > 1:
        terms = [a + b for a, b in zip(terms[::2], terms[1::2])]
    return terms[0]


def per_device(normals, spot, vol, weights, cash, taken):
    assets, paths = normals.shape
    features = 4 * assets
    path_total = paths * lax.axis_size("grp") * lax.axis_size("path")
    spot, vol, weights = (a.reshape(1, assets) for a in (spot, vol, weights))
    params = pltpu.CompilerParams(vmem_limit_bytes=16 * 1024 * 1024)
    big = jax.ShapeDtypeStruct((assets, paths), F32)
    jac_rows = features + assets + 16
    half = jax.ShapeDtypeStruct((jac_rows // 2, features), F32)
    compact = (paths // LANES, LANES)
    block = 8 * LANES
    remote = pl.BlockSpec(memory_space=pltpu.HBM)
    local = pl.BlockSpec(memory_space=pltpu.VMEM)
    short = jax.ShapeDtypeStruct(compact, F32)
    buffers = [
        pltpu.VMEM((16 + 2 * features, block), BF16),
        pltpu.VMEM((10 * assets, block), BF16),
    ]
    scaled, bounded, value, pull, gram, jac_keep, jac_give = pl.pallas_call(
        functools.partial(sums_kernel, assets, block),
        in_specs=[remote] * 6,
        out_specs=[remote] * 2 + [local] * 5,
        out_shape=[
            big, big, short, short,
            jax.ShapeDtypeStruct((features // 2 + 8, features), F32),
            half, half,
        ],
        scratch_shapes=[
            pltpu.VMEM((8, assets), F32),
            pltpu.VMEM(compact, F32),
            pltpu.VMEM(compact, jnp.int32),
            pltpu.VMEM((assets, paths), F32),
            pltpu.VMEM((4, assets, LANES), F32),
            pltpu.VMEM((64, LANES), F32),
            pltpu.VMEM((16, block), F32),
            pltpu.VMEM((assets, paths), F32),
            pltpu.VMEM((assets, paths), F32),
            *buffers, *buffers,
            pltpu.VMEM((16 + features, 2 * features), F32),
            pltpu.VMEM((16 + 2 * features, 5 * assets), F32),
            pltpu.VMEM((16 + features, 5 * assets), F32),
            pltpu.VMEM((jac_rows, features), F32),
            pltpu.SemaphoreType.DMA((5 + paths // (2 * block),)),
            pltpu.SemaphoreType.DMA((2, paths // (2 * block))),
        ],
        compiler_params=pltpu.CompilerParams(vmem_limit_bytes=60 * 1024 * 1024),
        name="sums",
    )(spot, vol, weights, cash.reshape(compact), taken.reshape(compact), normals)
    sizes = [lax.axis_size(axis) for axis in AXES]
    masks = [1 << bit for bit in range(math.prod(sizes).bit_length() - 1)]
    assert math.prod(sizes) == 1 << len(masks)
    scale = 1.0 / path_total
    gram = lax.optimization_barrier(gram * scale) + swap(gram, masks[0]) * scale
    jac_mine = lax.optimization_barrier(jac_keep * scale) + swap(jac_give, masks[0]) * scale
    packed = jnp.concatenate([gram, jac_mine], axis=0)
    later = masks[2:] + masks[1:2]
    for index in range(0, len(later), 2):
        packed = gather_sum(packed, later[index : index + 2])
    gram, jac_mine = packed[: gram.shape[0]], packed[gram.shape[0] :]
    jac_other = swap(jac_mine, masks[0])
    solved = pl.pallas_call(
        solve_kernel,
        out_shape=jax.ShapeDtypeStruct((8, features), F32),
        scratch_shapes=[pltpu.VMEM((2, 8, 8, features), F32)],
        compiler_params=params,
        cost_estimate=pl.CostEstimate(
            flops=4 * 10**9, bytes_accessed=15 * 10**6, transcendentals=features
        ),
        name="solve",
    )(gram)
    value, flow, greeks, cot = pl.pallas_call(
        functools.partial(adjoint_kernel, assets, block),
        in_specs=[local] * 12,
        out_specs=[local] * 3 + [remote],
        out_shape=[short, short, jax.ShapeDtypeStruct((2, assets), F32), big],
        scratch_shapes=[
            pltpu.VMEM((12, assets, LANES), F32),
            pltpu.VMEM((2, 2, 64, LANES), F32),
            pltpu.VMEM((2, 3, 8, LANES), F32),
            pltpu.VMEM((2, 2, assets, block), F32),
            pltpu.VMEM((assets, paths), F32),
            pltpu.VMEM((jac_rows, features), F32),
            pltpu.SemaphoreType.DMA((paths // (2 * block),)),
        ],
        compiler_params=params,
        name="adjoint",
    )(
        solved, jac_mine, jac_other, spot, vol, weights, cash.reshape(compact), taken.reshape(compact),
        value, pull, scaled, bounded,
    )
    return value.reshape(paths), cot, flow.reshape(paths), greeks


def solution(mesh):
    in_specs = (P(None, ("grp", "path")), P(), P(), P(), P(("grp", "path")), P(("grp", "path")))
    out_specs = (P(("grp", "path")), P(None, ("grp", "path")), P(("grp", "path")), P())
    return jax.shard_map(
        per_device, mesh=mesh, in_specs=in_specs, out_specs=out_specs, check_vma=False
    )
```

time: 408 us -> 44.5 us (0.11)
  other arithmetic: 151 us -> 1.63 us
  blocking collectives: 82.9 us -> 0 us
  waiting for transfers between devices: 75.9 us -> 9.98 us
  local copies, waits for them, and re-layouts: 40.1 us -> 0.06 us
  matrix products: 24.6 us -> 0 us
  Pallas kernels: 0 us -> 21.8 us
  between operations: 15.5 us -> 0.86 us
  loops' own time: 14.4 us -> 0 us
  starting transfers between devices: 0.04 us -> 9.88 us
    psum x2 -> x0, blocking collectives: 82.9 us -> none  [the longest x1 42 us: per_device(): gram_sum, moment_sum = lax.psum((gram_acc, moment_acc), ('grp', 'path'))]
    psum x1 -> x0, waiting for transfers between devices: 75.8 us -> none  [per_device(): gram_sum, moment_sum = lax.psum((gram_acc, moment_acc), ('grp', 'path'))]
    reduce_sum x32 -> x0, other arithmetic: 53.3 us -> none  [the longest x16 31.9 us: payoff(): jnp.sum(weights[:, None] * state, axis=0) / jnp.sum(weights * spot_today)]
    mul x145 -> x2, other arithmetic: 46.8 us -> 1.56 us  [the longest x1 0.79 us: per_device(): jac_keep * scale]
    dot_general x48 -> x0, matrix products: 24.2 us -> none  [the longest x16 10.8 us: gram_step(): lax.dot_general(basis_block, basis_block, contract_last, precision=highes...]
    another operation x5 -> x0, other arithmetic: 22.9 us -> none  [the longest x3 12.4 us: per_device(): factor = jnp.linalg.cholesky(gram_mean)]
    concatenate x32 -> x0, local copies, waits for them, and re-layouts: 21.9 us -> none  [basis_rows(): jnp.concatenate([leading, scaled, squares, neighbour, bounded], axis=0)]
    pallas_call x0 -> x3, Pallas kernels: none -> 21.8 us  [the longest x1 12.7 us: per_device(): pl.pallas_call(functools.partial(sums_kernel, assets, block), in_specs=[r...]
  transfers between devices with their start and end apart: 1 -> 9, of which waited for: 1 -> 6; matrix products, arithmetic and copies ran while one was open for 0% -> 4% of each run, Pallas kernels for 0% -> 10%
where the time goes in v2:
time: 44.5 us; the launch traced here: 44.2 us
  Pallas kernels  21.8 us (49%)
  waiting for transfers between devices  9.98 us (22%)
  starting transfers between devices  9.88 us (22%)
  other arithmetic  1.63 us (4%)
  between operations  0.86 us (2%)
    pallas_call x1, Pallas kernels, per_device(): pl.pallas_call(functools.partial(sums_kernel, assets, block), in_specs=[r...  12.7 us
    ppermute x9, waiting for transfers between devices, swap(): return lax.ppermute(value, AXES, [(i, i ^ mask) for i in range(count)])  9.98 us
    ppermute x9, starting transfers between devices, swap(): return lax.ppermute(value, AXES, [(i, i ^ mask) for i in range(count)])  9.88 us
    pallas_call x1, Pallas kernels, per_device(): pl.pallas_call(functools.partial(adjoint_kernel, assets, block), in_specs...  4.75 us
    pallas_call x1, Pallas kernels, per_device(): pl.pallas_call(solve_kernel, out_shape=jax.ShapeDtypeStruct((8, features)...  4.33 us
  transfers between devices with their start and end apart: 9, of which 6 were waited for; matrix products, arithmetic and copies ran while one was open for 4% of the time, Pallas kernels for 10%

profile of v2, /device:TPU:0, one launch (start us, length us, event | category | flops | bytes accessed | tf_op | source)
XLA Modules:
  0.0 44.2 jit_solution(8180866821582879584)
XLA Ops:
  0.6 12.7 %sums.1 = (f32[32,16384]{1,0:T(8,128)}, f32[32,16384]{1,0:T(8,128)}, f32[128,128]{1,0:T(8,128)}, f32[128,128]{1,0:T(8,128)}, f32[72,128]{1,0:T(8,128)}, /*index=5*/f32[88,128]{1,0:T(8,128)}, f32[88,128]{1,0:T(8,128)}) custom-call(f32[1,32]{1,0:T(1,128)} %bitcast.11, f32[1,32]{1,0:T(1,128)} %bitcast.13, f32[1,32]{1,0:T(1,128)} %bitcast.15, ...), custom_call_target="tpu_custom_call" | custom-call | tf_op jit(solution)/shard_map/sums/pallas_call | solution.py:433
  13.3 0.5 %collective-permute-start = (f32[72,128]{1,0:T(8,128)}, f32[72,128]{1,0:T(8,128)S(1)}, u32[]{:S(2)}, u32[]{:S(2)}) collective-permute-start(f32[72,128]{1,0:T(8,128)} %get-tuple-element.15), channel_id=1, source_target_pairs={{0,1},{1,0},{2,3},{3,2},{4,5},{5,4},{6,7},{7,6},{8,9},{9,8},{10,11... | collective-permute-start | bytes 110600 | tf_op jit(solution)/shard_map/ppermute | solution.py:402
  13.9 0.1 collective-permute-start.1
  13.9 0.8 %broadcast_multiply_fusion = f32[88,128]{1,0:T(8,128)S(1)} fusion(f32[88,128]{1,0:T(8,128)} %get-tuple-element.16), kind=kLoop, calls=%fused_computation.5 | loop fusion | flops 11264 | bytes 90112 | tf_op jit(solution)/shard_map/mul | solution.py:468
  14.7 0.8 %broadcast_multiply_fusion.1 = f32[72,128]{1,0:T(8,128)S(1)} fusion(f32[72,128]{1,0:T(8,128)} %get-tuple-element.15), kind=kLoop, calls=%fused_computation.6 | loop fusion | flops 9216 | bytes 73728 | tf_op jit(solution)/shard_map/mul | solution.py:467
  15.5 0.0 collective-permute-done
  15.5 0.0 collective-permute-done.1
  15.6 4.1 %collective-permute-start.3 = (f32[160,128]{1,0:T(8,128)S(1)}, f32[160,128]{1,0:T(8,128)S(1)}, u32[]{:S(2)}, u32[]{:S(2)}) collective-permute-start(f32[160,128]{1,0:T(8,128)S(1)} %pad_maximum_fusion), channel_id=1, source_target_pairs={{0,8},{1,9},{2,10},{3,11},{4,12},{5,13},{6,14},{7,15},{8,0},{9,1},... | collective-permute-start | bytes 245768 | tf_op jit(solution)/shard_map/ppermute | solution.py:402
  19.6 1.3 %collective-permute-start.4 = (f32[160,128]{1,0:T(8,128)S(1)}, f32[160,128]{1,0:T(8,128)S(1)}, u32[]{:S(2)}, u32[]{:S(2)}) collective-permute-start(f32[160,128]{1,0:T(8,128)S(1)} %pad_maximum_fusion), channel_id=1, source_target_pairs={{0,12},{1,13},{2,14},{3,15},{4,8},{5,9},{6,10},{7,11},{8,4},{9,5},... | collective-permute-start | bytes 245768 | tf_op jit(solution)/shard_map/ppermute | solution.py:402
  21.0 0.2 collective-permute-start.2
  21.2 4.8 %collective-permute-done.3 = f32[160,128]{1,0:T(8,128)S(1)} collective-permute-done((f32[160,128]{1,0:T(8,128)S(1)}, f32[160,128]{1,0:T(8,128)S(1)}, u32[]{:S(2)}, u32[]{:S(2)}) %collective-permute-start.3) | collective-permute-done | bytes 81952 | tf_op jit(solution)/shard_map/ppermute | solution.py:402
  26.0 0.5 %collective-permute-done.4 = f32[160,128]{1,0:T(8,128)S(1)} collective-permute-done((f32[160,128]{1,0:T(8,128)S(1)}, f32[160,128]{1,0:T(8,128)S(1)}, u32[]{:S(2)}, u32[]{:S(2)}) %collective-permute-start.4) | collective-permute-done | bytes 81952 | tf_op jit(solution)/shard_map/ppermute | solution.py:402
  26.5 0.7 %collective-permute-done.2 = f32[160,128]{1,0:T(8,128)S(1)} collective-permute-done((f32[160,128]{1,0:T(8,128)S(1)}, f32[160,128]{1,0:T(8,128)S(1)}, u32[]{:S(2)}, u32[]{:S(2)}) %collective-permute-start.2) | collective-permute-done | bytes 81952 | tf_op jit(solution)/shard_map/ppermute | solution.py:402
  27.2 2.6 %collective-permute-start.7 = (f32[160,128]{1,0:T(8,128)S(1)}, f32[160,128]{1,0:T(8,128)S(1)}, u32[]{:S(2)}, u32[]{:S(2)}) collective-permute-start(f32[160,128]{1,0:T(8,128)S(1)} %add_add_fusion.1), channel_id=1, source_target_pairs={{0,18},{1,19},{2,16},{3,17},{4,22},{5,23},{6,20},{7,21},{8,26},{9,... | collective-permute-start | bytes 245768 | tf_op jit(solution)/shard_map/ppermute | solution.py:402
  29.8 0.5 %collective-permute-start.6 = (f32[160,128]{1,0:T(8,128)S(1)}, f32[160,128]{1,0:T(8,128)S(1)}, u32[]{:S(2)}, u32[]{:S(2)}) collective-permute-start(f32[160,128]{1,0:T(8,128)S(1)} %add_add_fusion.1), channel_id=1, source_target_pairs={{0,2},{1,3},{2,0},{3,1},{4,6},{5,7},{6,4},{7,5},{8,10},{9,11},{10,... | collective-permute-start | bytes 245768 | tf_op jit(solution)/shard_map/ppermute | solution.py:402
  30.3 0.5 %collective-permute-start.5 = (f32[160,128]{1,0:T(8,128)S(1)}, f32[160,128]{1,0:T(8,128)S(1)}, u32[]{:S(2)}, u32[]{:S(2)}) collective-permute-start(f32[160,128]{1,0:T(8,128)S(1)} %add_add_fusion.1), channel_id=1, source_target_pairs={{0,16},{1,17},{2,18},{3,19},{4,20},{5,21},{6,22},{7,23},{8,24},{9,... | collective-permute-start | bytes 245768 | tf_op jit(solution)/shard_map/ppermute | solution.py:402
  30.8 2.0 %collective-permute-done.7 = f32[160,128]{1,0:T(8,128)S(1)} collective-permute-done((f32[160,128]{1,0:T(8,128)S(1)}, f32[160,128]{1,0:T(8,128)S(1)}, u32[]{:S(2)}, u32[]{:S(2)}) %collective-permute-start.7) | collective-permute-done | bytes 81952 | tf_op jit(solution)/shard_map/ppermute | solution.py:402
  32.8 1.5 %collective-permute-done.6 = f32[160,128]{1,0:T(8,128)S(1)} collective-permute-done((f32[160,128]{1,0:T(8,128)S(1)}, f32[160,128]{1,0:T(8,128)S(1)}, u32[]{:S(2)}, u32[]{:S(2)}) %collective-permute-start.6) | collective-permute-done | bytes 81952 | tf_op jit(solution)/shard_map/ppermute | solution.py:402
  34.3 0.5 %collective-permute-done.5 = f32[160,128]{1,0:T(8,128)S(1)} collective-permute-done((f32[160,128]{1,0:T(8,128)S(1)}, f32[160,128]{1,0:T(8,128)S(1)}, u32[]{:S(2)}, u32[]{:S(2)}) %collective-permute-start.5) | collective-permute-done | bytes 81952 | tf_op jit(solution)/shard_map/ppermute | solution.py:402
  34.8 0.0 copy-start
  34.8 0.0 copy-start.1
  34.8 0.0 copy-start.2
  34.9 0.0 copy-start.3
  34.9 0.0 copy-start.4
  34.9 0.0 copy-start.5
  34.9 0.0 copy-start.6
  34.9 0.0 copy-start.7
  34.9 0.0 copy-start.8
  34.9 0.1 collective-permute-start.8
  35.0 4.3 %solve.1.solved = f32[8,128]{1,0:T(8,128)S(1)} custom-call(f32[72,128]{1,0:T(8,128)S(1)} %slice.8.packed), custom_call_target="tpu_custom_call" | custom-call | flops 4000000000 | bytes 15000000 | tf_op jit(solution)/shard_map/solve/pallas_call | solution.py:475
  39.3 0.0 collective-permute-done.8.jac_other
  39.3 0.0 copy-done
  39.4 0.0 copy-done.1
  39.4 0.0 copy-done.2
  39.4 0.0 copy-done.3
  39.4 0.0 copy-done.4
  39.4 0.0 copy-done.5
  39.4 0.0 copy-done.6
  39.4 0.0 copy-done.7
  39.4 0.0 copy-done.8
  39.4 4.8 %adjoint.1 = (f32[128,128]{1,0:T(8,128)}, f32[128,128]{1,0:T(8,128)}, f32[2,32]{1,0:T(2,128)}, f32[32,16384]{1,0:T(8,128)}) custom-call(f32[8,128]{1,0:T(8,128)S(1)} %solve.1.solved, f32[88,128]{1,0:T(8,128)S(1)} %slice.9.jac_mine, f32[88,128]{1,0:T(8,128)S(1)} %collective-permute-done.8.jac_other, f32[1,32]{1,0:T(1,128)S(1)} %bitcast.12, ...), custom_call_target="tpu_custom_call" | custom-call | tf_op jit(solution)/shard_map/adjoint/pallas_call | solution.py:485
  (7 shorter events, 0.1 us)
Async XLA Ops:
  13.3 2.2 %collective-permute-start = (f32[72,128]{1,0:T(8,128)}, f32[72,128]{1,0:T(8,128)S(1)}, u32[]{:S(2)}, u32[]{:S(2)}) collective-permute-start(f32[72,128]{1,0:T(8,128)} %get-tuple-element.15), channel_id=1, source_target_pairs={{0,1},{1,0},{2,3},{3,2},{4,5},{5,4},{6,7},{7,6},{8,9},{9,8},{10,11... | collective-permute-start | bytes 110600 | tf_op jit(solution)/shard_map/ppermute | solution.py:402
  13.9 1.7 %collective-permute-start.1 = (f32[88,128]{1,0:T(8,128)}, f32[88,128]{1,0:T(8,128)S(1)}, u32[]{:S(2)}, u32[]{:S(2)}) collective-permute-start(f32[88,128]{1,0:T(8,128)} %get-tuple-element.17), channel_id=1, source_target_pairs={{0,1},{1,0},{2,3},{3,2},{4,5},{5,4},{6,7},{7,6},{8,9},{9,8},{10,11... | collective-permute-start | bytes 135176 | tf_op jit(solution)/shard_map/ppermute | solution.py:402
  15.6 10.4 %collective-permute-start.3 = (f32[160,128]{1,0:T(8,128)S(1)}, f32[160,128]{1,0:T(8,128)S(1)}, u32[]{:S(2)}, u32[]{:S(2)}) collective-permute-start(f32[160,128]{1,0:T(8,128)S(1)} %pad_maximum_fusion), channel_id=1, source_target_pairs={{0,8},{1,9},{2,10},{3,11},{4,12},{5,13},{6,14},{7,15},{8,0},{9,1},... | collective-permute-start | bytes 245768 | tf_op jit(solution)/shard_map/ppermute | solution.py:402
  19.6 6.9 %collective-permute-start.4 = (f32[160,128]{1,0:T(8,128)S(1)}, f32[160,128]{1,0:T(8,128)S(1)}, u32[]{:S(2)}, u32[]{:S(2)}) collective-permute-start(f32[160,128]{1,0:T(8,128)S(1)} %pad_maximum_fusion), channel_id=1, source_target_pairs={{0,12},{1,13},{2,14},{3,15},{4,8},{5,9},{6,10},{7,11},{8,4},{9,5},... | collective-permute-start | bytes 245768 | tf_op jit(solution)/shard_map/ppermute | solution.py:402
  21.0 6.2 %collective-permute-start.2 = (f32[160,128]{1,0:T(8,128)S(1)}, f32[160,128]{1,0:T(8,128)S(1)}, u32[]{:S(2)}, u32[]{:S(2)}) collective-permute-start(f32[160,128]{1,0:T(8,128)S(1)} %pad_maximum_fusion), channel_id=1, source_target_pairs={{0,4},{1,5},{2,6},{3,7},{4,0},{5,1},{6,2},{7,3},{8,12},{9,13},{10,... | collective-permute-start | bytes 245768 | tf_op jit(solution)/shard_map/ppermute | solution.py:402
  27.2 5.5 %collective-permute-start.7 = (f32[160,128]{1,0:T(8,128)S(1)}, f32[160,128]{1,0:T(8,128)S(1)}, u32[]{:S(2)}, u32[]{:S(2)}) collective-permute-start(f32[160,128]{1,0:T(8,128)S(1)} %add_add_fusion.1), channel_id=1, source_target_pairs={{0,18},{1,19},{2,16},{3,17},{4,22},{5,23},{6,20},{7,21},{8,26},{9,... | collective-permute-start | bytes 245768 | tf_op jit(solution)/shard_map/ppermute | solution.py:402
  29.8 4.4 %collective-permute-start.6 = (f32[160,128]{1,0:T(8,128)S(1)}, f32[160,128]{1,0:T(8,128)S(1)}, u32[]{:S(2)}, u32[]{:S(2)}) collective-permute-start(f32[160,128]{1,0:T(8,128)S(1)} %add_add_fusion.1), channel_id=1, source_target_pairs={{0,2},{1,3},{2,0},{3,1},{4,6},{5,7},{6,4},{7,5},{8,10},{9,11},{10,... | collective-permute-start | bytes 245768 | tf_op jit(solution)/shard_map/ppermute | solution.py:402
  30.3 4.4 %collective-permute-start.5 = (f32[160,128]{1,0:T(8,128)S(1)}, f32[160,128]{1,0:T(8,128)S(1)}, u32[]{:S(2)}, u32[]{:S(2)}) collective-permute-start(f32[160,128]{1,0:T(8,128)S(1)} %add_add_fusion.1), channel_id=1, source_target_pairs={{0,16},{1,17},{2,18},{3,19},{4,20},{5,21},{6,22},{7,23},{8,24},{9,... | collective-permute-start | bytes 245768 | tf_op jit(solution)/shard_map/ppermute | solution.py:402
  34.8 4.5 %copy-start = (f32[32,16384]{1,0:T(8,128)S(1)}, f32[32,16384]{1,0:T(8,128)}, u32[]{:S(2)}) copy-start(f32[32,16384]{1,0:T(8,128)} %get-tuple-element.20.scaled_in) | copy-start | bytes 6291460
  34.8 4.5 %copy-start.1 = (f32[32,16384]{1,0:T(8,128)S(1)}, f32[32,16384]{1,0:T(8,128)}, u32[]{:S(2)}) copy-start(f32[32,16384]{1,0:T(8,128)} %get-tuple-element.21.bounded_in) | copy-start | bytes 6291460
  34.8 4.5 %copy-start.2 = (f32[16384]{0:T(1024)S(1)}, f32[16384]{0:T(1024)}, u32[]{:S(2)}) copy-start(f32[16384]{0:T(1024)} %param.10) | copy-start | bytes 196612
  34.9 4.5 %copy-start.3 = (s32[16384]{0:T(1024)S(1)}, s32[16384]{0:T(1024)}, u32[]{:S(2)}) copy-start(s32[16384]{0:T(1024)} %param.11) | copy-start | bytes 196612
  34.9 4.5 %copy-start.4 = (f32[128,128]{1,0:T(8,128)S(1)}, f32[128,128]{1,0:T(8,128)}, u32[]{:S(2)}) copy-start(f32[128,128]{1,0:T(8,128)} %get-tuple-element.18.value_in) | copy-start | bytes 196612
  34.9 4.5 %copy-start.5 = (f32[128,128]{1,0:T(8,128)S(1)}, f32[128,128]{1,0:T(8,128)}, u32[]{:S(2)}) copy-start(f32[128,128]{1,0:T(8,128)} %get-tuple-element.19.pull_in) | copy-start | bytes 196612
  34.9 4.5 %copy-start.6 = (f32[32]{0:T(128)S(1)}, f32[32]{0:T(128)}, u32[]{:S(2)}) copy-start(f32[32]{0:T(128)} %param.7) | copy-start | bytes 388
  34.9 4.5 %copy-start.7 = (f32[32]{0:T(128)S(1)}, f32[32]{0:T(128)}, u32[]{:S(2)}) copy-start(f32[32]{0:T(128)} %param.8) | copy-start | bytes 388
  34.9 4.5 %copy-start.8 = (f32[32]{0:T(128)S(1)}, f32[32]{0:T(128)}, u32[]{:S(2)}) copy-start(f32[32]{0:T(128)} %param.9) | copy-start | bytes 388
  34.9 4.4 %collective-permute-start.8 = (f32[88,128]{1,0:T(8,128)S(1)}, f32[88,128]{1,0:T(8,128)S(1)}, u32[]{:S(2)}, u32[]{:S(2)}) collective-permute-start(f32[88,128]{1,0:T(8,128)S(1)} %slice.9.jac_mine), channel_id=1, source_target_pairs={{0,1},{1,0},{2,3},{3,2},{4,5},{5,4},{6,7},{7,6},{8,9},{9,8},{10,11... | collective-permute-start | bytes 135176 | tf_op jit(solution)/shard_map/ppermute | solution.py:402

commit v3 on v2

--- a/solution.py
+++ b/solution.py
@@ -40,9 +40,9 @@
 
 def sums_kernel(
     assets, width, spot, vol, weights, cash, taken, normals,
-    scaled_out, bounded_out, value_out, pull_out, gram_out, jac_keep, jac_give,
+    scaled_out, bounded_out, value_out, pull_out, keep, give,
     small, flows, flags, draws, coef, part, target,
-    scaled_all, bounded_all, rows_a, tilts_a, rows_b, tilts_b, gram_acc, jac_acc, jac_low, jac, sems, sent,
+    scaled_all, bounded_all, slopes, rows_a, rows_b, acc, flow_acc, pull_acc, jac, sems, sent,
 ):
     features = 4 * assets
     paths = draws.shape[1]
@@ -74,11 +74,10 @@
         if index == 0:
             for copy in copies[3:]:
                 copy.start()
-    gram_acc[...] = jnp.zeros_like(gram_acc)
-    jac_acc[...] = jnp.zeros_like(jac_acc)
-    jac_low[...] = jnp.zeros_like(jac_low)
+    acc[...] = jnp.zeros_like(acc)
+    flow_acc[...] = jnp.zeros_like(flow_acc)
+    pull_acc[...] = jnp.zeros_like(pull_acc)
     rows_b[...] = jnp.zeros_like(rows_b)
-    tilts_b[...] = jnp.zeros_like(tilts_b)
     target[...] = jnp.zeros_like(target)
     for copy in copies[:3]:
         copy.wait()
@@ -93,9 +92,16 @@
         copy.wait()
 
     last = lax.broadcasted_iota(jnp.int32, (assets, LANES), 0) == assets - 1
-
-    def fill(block, rows, tilts):
-        for c in range(chunks):
+    tail = lax.broadcasted_iota(jnp.int32, (16, LANES), 0) == 15
+    aim, base, low = 10 * assets, 10 * assets + 16, 10 * assets + 16 + features
+
+    def fill(block, rows, half):
+        line = pl.ds(pl.multiple_of(block * chunks, chunks), chunks)
+        flag = flags[line, :].astype(F32)
+        flow = flows[line, :]
+        rest = 1.0 - flag
+        flow_sum = 0.0
+        for c in range(half * chunks // 2, (half + 1) * chunks // 2):
             at = pl.ds(pl.multiple_of(block * width, width) + c * LANES, LANES)
             here = pl.ds(c * LANES, LANES)
             draw = draws[:, at]
@@ -113,93 +119,113 @@
                 [scaled, scaled * scaled - 1.0, scaled * after, bounded], axis=0
             )
             hi, lo = split(basis)
-            rows[16 : 16 + features, here] = hi
-            rows[16 + features : 16 + 2 * features, here] = lo
+            rows[base : base + features, here] = hi
+            rows[low : low + features - 16, here] = lo[: features - 16]
+            ends = (basis - hi.astype(F32))[features - 16 :]
+            kept = jnp.broadcast_to(rest[c : c + 1, :], (16, LANES))
+            rows[low + features - 16 :, here] = jnp.where(tail, kept, ends).astype(BF16)
             slope = growth * (draw - spread) - scaled
             curve = 1.0 - bounded * bounded
-            hi, lo = split(
-                jnp.concatenate(
-                    [slope, slope * scaled, slope * after, slope * curve, slope * before], axis=0
-                )
+            tilt = jnp.concatenate(
+                [slope, slope * scaled, slope * after, slope * curve, slope * before], axis=0
             )
-            tilts[0 : 5 * assets, here] = hi
-            tilts[5 * assets : 10 * assets, here] = lo
-        line = pl.ds(pl.multiple_of(block * chunks, chunks), chunks)
+            hi, lo = split(tilt)
+            rows[0 : 5 * assets, here] = hi
+            rows[5 * assets : 10 * assets, here] = lo
+            flow_sum = flow_sum + tilt * jnp.broadcast_to(flow[c : c + 1, :], tilt.shape)
+            slopes[:, here] = slope
+        flow_acc[...] += flow_sum
+        if half == 0:
+            return
         basket = sum(part[pl.ds(i, chunks, stride=8), :] for i in range(8))
         x = (basket - 1.0) * (1.0 / soft_width)
         decay = jnp.exp(-jnp.abs(x))
         reward = (notional * soft_width) * (jnp.maximum(x, 0.0) + jnp.log1p(decay))
         inverse = 1.0 / (1.0 + decay)
         sigmoid = jnp.where(x >= 0.0, inverse, decay * inverse)
-        flag = flags[line, :].astype(F32)
-        flow = flows[line, :]
         pull = notional * flag * sigmoid
         value_out[line, :] = flag * reward
         pull_out[line, :] = pull
         flow_hi = flow.astype(BF16).astype(F32)
         pull_hi = pull.astype(BF16).astype(F32)
+        pull_sum = 0.0
         for c in range(chunks):
             here = pl.ds(c * LANES, LANES)
-            for index, row in enumerate(
-                [flow_hi, flow - flow_hi, 1.0 - flag, pull_hi, pull - pull_hi]
-            ):
+            for index, row in enumerate([flow_hi, flow - flow_hi, rest, pull_hi, pull - pull_hi]):
                 target[index : index + 1, here] = row[c : c + 1, :]
-        rows[0:16, :] = target[...].astype(BF16)
-
-    def multiply(rows, tilts):
-        upper = rows[0 : 16 + features, :]
-        gram_acc[...] += lax.dot_general(
-            upper, rows[16:, :], CONTRACT_LAST, preferred_element_type=F32
-        )
-        jac_acc[...] += lax.dot_general(
-            rows[...], tilts[0 : 5 * assets, :], CONTRACT_LAST, preferred_element_type=F32
-        )
-        jac_low[...] += lax.dot_general(
-            upper, tilts[5 * assets :, :], CONTRACT_LAST, preferred_element_type=F32
+            pull_sum = pull_sum + slopes[:, here] * jnp.broadcast_to(pull[c : c + 1, :], (assets, LANES))
+        pull_acc[...] += pull_sum
+        rows[aim : aim + 16, :] = target[...].astype(BF16)
+
+    cut = 16 * ((low // 16 + 1) // 2)
+
+    def multiply(rows, part):
+        at = slice(0, cut) if part == 0 else slice(cut, low)
+        acc[at, :] += lax.dot_general(
+            rows[at, :], rows[base:, :], CONTRACT_LAST, preferred_element_type=F32
         )
 
     def both(index, carry):
         pair(index).wait()
-        multiply(rows_b, tilts_b)
-        fill(2 * index, rows_a, tilts_a)
-        multiply(rows_a, tilts_a)
-        fill(2 * index + 1, rows_b, tilts_b)
+        for part in range(2):
+            multiply(rows_b, part)
+            fill(2 * index, rows_a, part)
+        for part in range(2):
+            multiply(rows_a, part)
+            fill(2 * index + 1, rows_b, part)
         for copy in leave(index):
             copy.start()
         return carry
 
     lax.fori_loop(0, blocks // 2, both, 0)
-    multiply(rows_b, tilts_b)
-
-    def targets(t):
-        pairs = [t[0:1] + t[1:2], t[2:3], t[3:4] + t[4:5], jnp.zeros((5, t.shape[1]), F32)]
-        return jnp.concatenate(pairs, axis=0)
+    multiply(rows_b, 0)
+    multiply(rows_b, 1)
 
     mid = features // 2
-    high = gram_acc[16:, 0:features]
-    half = 0.5 * high + gram_acc[16:, features:]
+    high = acc[base:low, 0:features]
+    cross = acc[base:low, features:]
+    edge = lax.broadcasted_iota(jnp.int32, (features, features), 1) == features - 1
+    half = 0.5 * high + jnp.where(edge, 0.0, cross)
     gram = half + half.T
     turned = pltpu.roll(gram[mid:, :], mid, 1)
     lanes = lax.broadcasted_iota(jnp.int32, (mid, features), 1)
     subs = lax.broadcasted_iota(jnp.int32, (mid, features), 0)
-    gram_out[0:mid, :] = jnp.where(lanes >= subs, gram[0:mid, :], turned)
+    packed = jnp.where(lanes >= subs, gram[0:mid, :], turned)
+    keep[0:mid, :] = packed
+    give[0:mid, :] = packed
     corner = jnp.sum(jnp.where(lanes == subs, turned, 0.0), axis=0, keepdims=True)
-    aims = targets(gram_acc[0:16, 0:features] + gram_acc[0:16, features:])
+    aimed = acc[aim : aim + 8, 0:features] + jnp.where(edge[0:8], 0.0, acc[aim : aim + 8, features:])
+    aims = jnp.concatenate(
+        [
+            aimed[0:1] + aimed[1:2], aimed[2:3], aimed[3:4] + aimed[4:5],
+            jnp.zeros((5, features), F32),
+        ],
+        axis=0,
+    )
     rank = lax.broadcasted_iota(jnp.int32, (8, features), 0)
-    gram_out[mid:, :] = jnp.where(rank == 3, jnp.broadcast_to(corner, (8, features)), aims)
-    full = jac_acc[16 : 16 + features, :] + jac_acc[16 + features :, :] + jac_low[16:, :]
-    aims = targets(jac_acc[0:16, :] + jac_low[0:16, :])
-    jac[0:features, :] = full[:, 0:features]
-    jac[features : features + assets, :] = jnp.concatenate(
-        [full[assets * g : assets * (g + 1), features:] for g in range(4)], axis=1
+    packed = jnp.where(rank == 3, jnp.broadcast_to(corner, (8, features)), aims)
+    keep[mid : mid + 8, :] = packed
+    give[mid : mid + 8, :] = packed
+    five = 5 * assets
+    edge = edge[0:1]
+    leaned = acc[0:five, features:]
+    full = acc[0:five, 0:features] + acc[five:aim, 0:features] + jnp.where(edge, 0.0, leaned)
+    rest = jnp.sum(jnp.where(edge, leaned + acc[five:aim, features:], 0.0), axis=1, keepdims=True)
+    flow = jnp.sum(flow_acc[...], axis=1, keepdims=True)
+    pull = jnp.sum(pull_acc[...], axis=1, keepdims=True)
+    jac[0:five, :] = full
+    slots = lax.broadcasted_iota(jnp.int32, (five, features), 1)
+    pull = jnp.concatenate([pull, jnp.zeros((4 * assets, 1), F32)], axis=0)
+    sides = jnp.where(
+        slots == 0, flow, jnp.where(slots == 1, rest, jnp.where(slots == 2, pull, 0.0))
+    ).T
+    jac[five : five + 8, :] = sides[0:8, 0:features]
+    jac[five + 8 : five + 16, :] = jnp.concatenate(
+        [sides[0:8, features:], jnp.zeros((8, features - assets), F32)], axis=1
     )
-    jac[features + assets : features + assets + 8, :] = aims[:, 0:features]
-    jac[features + assets + 8 :, :] = jnp.concatenate(
-        [aims[:, features:], jnp.zeros((8, features - assets), F32)], axis=1
-    )
-    mine, other = halves(jac_keep.shape[0])
-    jac_keep[...] = jac[mine, :]
-    jac_give[...] = jac[other, :]
+    mine, other = halves(jac.shape[0] // 2)
+    keep[mid + 8 :, :] = jac[mine, :]
+    give[mid + 8 :, :] = jac[other, :]
     for index in range(blocks // 2):
         for copy in leave(index):
             copy.wait()
@@ -242,24 +268,34 @@
         inside = (lanes >= base) & (lanes < base + 8)
         spread[1, 0] = jnp.where(inside, jnp.where(lanes == base + subs, -1.0, 0.0), head)
         work = [jnp.broadcast_to(spread[1, 0, i : i + 1, :], (8, features)) for i in range(8)]
-        inverse, low = [], {}
-        for p in range(8):
-            inv = 1.0 / diag[p, p]
-            inverse.append(inv)
-            for j in range(p + 1, 8):
-                low[p, j] = diag[p, j] * inv
-            for i in range(p + 1, 8):
+        inverse, low = {}, {}
+        for p in range(0, 8, 2):
+            q = p + 1
+            one, off, two = diag[p, p], diag[p, q], diag[q, q]
+            inv = 1.0 / (one * two - off * off)
+            inverse[p] = (two * inv, off * inv, one * inv)
+            lift = {}
+            for j in range(q + 1, 8):
+                first, second = diag[p, j], diag[q, j]
+                lift[j] = (two * first - off * second, one * second - off * first)
+                low[p, j], low[q, j] = lift[j][0] * inv, lift[j][1] * inv
+            for i in range(q + 1, 8):
                 for j in range(i, 8):
-                    diag[i, j] = diag[i, j] - low[p, i] * diag[p, j]
-                work[i] = work[i] - low[p, i] * work[p]
-        for i in reversed(range(8)):
-            value = work[i] * inverse[i]
-            for j in range(i + 1, 8):
-                value = value - low[i, j] * work[j]
-            work[i] = value
+                    drop = lift[i][0] * diag[p, j] + lift[i][1] * diag[q, j]
+                    diag[i, j] = diag[i, j] - drop * inv
+                work[i] = work[i] - (low[p, i] * work[p] + low[q, i] * work[q])
+        for p in (6, 4, 2, 0):
+            q = p + 1
+            one, off, two = inverse[p]
+            first = one * work[p] - off * work[q]
+            second = two * work[q] - off * work[p]
+            for j in reversed(range(q + 1, 8)):
+                first = first - low[p, j] * work[j]
+                second = second - low[q, j] * work[j]
+            work[p], work[q] = first, second
         for v in range(k + 1, blocks + 1):
             new = jnp.where(inside, 0.0, mat[v])
-            for c in range(8):
+            for c in reversed(range(8)):
                 new = new - lane(mat[v], base + c) * work[c]
             mat[v] = new
     kept = jnp.broadcast_to(aims[2:3], (8, features))
@@ -351,25 +387,15 @@
     jac[mine, :] = jac_mine[...]
     jac[other, :] = jac_other[...]
     regression, multiplier = solved[0:1, :], solved[1:2, :]
-    group = lax.broadcasted_iota(jnp.int32, (assets, LANES), 1) // assets
-
-    def against(which):
-        main = jnp.sum(jac[0:features, :] * turned[:, which : which + 1], axis=0, keepdims=True)
-        packed = jnp.zeros((assets, LANES), F32)
-        for g in range(4):
-            part = turned[assets * g : assets * (g + 1), which : which + 1]
-            packed = jnp.where(group == g, jnp.broadcast_to(part, (assets, LANES)), packed)
-        side = jnp.sum(jac[features : features + assets, :] * packed, axis=0, keepdims=True)
-        side = side + pltpu.roll(side, 2 * assets, 1)
-        side = side + pltpu.roll(side, assets, 1)
-        return main, side
-
     aims = features + assets
-    main_r, side_r = against(0)
-    main_m, side_m = against(1)
-    miss, gap = jac[aims : aims + 1, :] - main_r, jac[aims + 1 : aims + 2, :] - main_m
-    miss_side = jac[aims + 8 : aims + 9, :] - side_r
-    gap_side = jac[aims + 9 : aims + 10, :] - side_m
+    against = lax.dot_general(
+        solved[...], jac[0:aims, :], CONTRACT_LAST,
+        precision=lax.Precision.HIGHEST, preferred_element_type=F32,
+    )
+    miss = jac[aims : aims + 1, :] - against[0:1, 0:features]
+    gap = jac[aims + 1 : aims + 2, :] - against[1:2, 0:features]
+    miss_side = jac[aims + 8 : aims + 9, 0:assets] - against[0:1, features:]
+    gap_side = jac[aims + 9 : aims + 10, 0:assets] - against[1:2, features:]
     lanes = lax.broadcasted_iota(jnp.int32, (1, LANES), 1)
     double = jnp.where((lanes >= assets) & (lanes < 2 * assets), 2.0, 1.0)
     total = double * (multiplier * miss + regression * gap)
@@ -381,8 +407,8 @@
         wrapped = pltpu.roll(row, features - 3 * assets + 1, 1)
         return jnp.where(lanes == 0, wrapped, moved)
 
-    total = total + earlier(multiplier) * miss_side + earlier(regression) * gap_side
-    vega = total[:, 0:assets] / vol[...]
+    side = earlier(multiplier)[:, 0:assets] * miss_side + earlier(regression)[:, 0:assets] * gap_side
+    vega = (total[:, 0:assets] + side) / vol[...]
     pulled_slope = jac[aims + 2 : aims + 3, 0:assets]
     pulled_scaled = solved[3:4, 0:assets]
     pulled = solved[3:4, features - 1 : features]
@@ -420,24 +446,21 @@
     params = pltpu.CompilerParams(vmem_limit_bytes=16 * 1024 * 1024)
     big = jax.ShapeDtypeStruct((assets, paths), F32)
     jac_rows = features + assets + 16
-    half = jax.ShapeDtypeStruct((jac_rows // 2, features), F32)
+    gram_rows = features // 2 + 8
+    sent = jax.ShapeDtypeStruct((gram_rows + jac_rows // 2, features), F32)
     compact = (paths // LANES, LANES)
     block = 8 * LANES
     remote = pl.BlockSpec(memory_space=pltpu.HBM)
     local = pl.BlockSpec(memory_space=pltpu.VMEM)
     short = jax.ShapeDtypeStruct(compact, F32)
-    buffers = [
-        pltpu.VMEM((16 + 2 * features, block), BF16),
-        pltpu.VMEM((10 * assets, block), BF16),
-    ]
-    scaled, bounded, value, pull, gram, jac_keep, jac_give = pl.pallas_call(
+    rows = pltpu.VMEM((10 * assets + 16 + 2 * features, block), BF16)
+    scaled, bounded, value, pull, keep, give = pl.pallas_call(
         functools.partial(sums_kernel, assets, block),
         in_specs=[remote] * 6,
-        out_specs=[remote] * 2 + [local] * 5,
+        out_specs=[remote] * 2 + [local] * 4,
         out_shape=[
             big, big, short, short,
-            jax.ShapeDtypeStruct((features // 2 + 8, features), F32),
-            half, half,
+            sent, sent,
         ],
         scratch_shapes=[
             pltpu.VMEM((8, assets), F32),
@@ -449,10 +472,11 @@
             pltpu.VMEM((16, block), F32),
             pltpu.VMEM((assets, paths), F32),
             pltpu.VMEM((assets, paths), F32),
-            *buffers, *buffers,
-            pltpu.VMEM((16 + features, 2 * features), F32),
-            pltpu.VMEM((16 + 2 * features, 5 * assets), F32),
-            pltpu.VMEM((16 + features, 5 * assets), F32),
+            pltpu.VMEM((assets, block), F32),
+            rows, rows,
+            pltpu.VMEM((10 * assets + 16 + features, 2 * features), F32),
+            pltpu.VMEM((5 * assets, LANES), F32),
+            pltpu.VMEM((assets, LANES), F32),
             pltpu.VMEM((jac_rows, features), F32),
             pltpu.SemaphoreType.DMA((5 + paths // (2 * block),)),
             pltpu.SemaphoreType.DMA((2, paths // (2 * block))),
@@ -464,13 +488,10 @@
     masks = [1 << bit for bit in range(math.prod(sizes).bit_length() - 1)]
     assert math.prod(sizes) == 1 << len(masks)
     scale = 1.0 / path_total
-    gram = lax.optimization_barrier(gram * scale) + swap(gram, masks[0]) * scale
-    jac_mine = lax.optimization_barrier(jac_keep * scale) + swap(jac_give, masks[0]) * scale
-    packed = jnp.concatenate([gram, jac_mine], axis=0)
-    later = masks[2:] + masks[1:2]
-    for index in range(0, len(later), 2):
-        packed = gather_sum(packed, later[index : index + 2])
-    gram, jac_mine = packed[: gram.shape[0]], packed[gram.shape[0] :]
+    packed = lax.optimization_barrier(keep * scale) + swap(give, masks[0]) * scale
+    for group in [[masks[1], masks[-1]]] + [[mask] for mask in masks[2:-1]]:
+        packed = gather_sum(packed, group)
+    gram, jac_mine = packed[:gram_rows], packed[gram_rows:]
     jac_other = swap(jac_mine, masks[0])
     solved = pl.pallas_call(
         solve_kernel,

time: 44.5 us -> 41.8 us (0.939)
  Pallas kernels: 21.8 us -> 20.2 us
  other arithmetic: 1.63 us -> 0.94 us
  starting transfers between devices: 9.88 us -> 9.39 us
    pallas_call x1, Pallas kernels: 4.33 us -> 3.21 us  [per_device(): pl.pallas_call(solve_kernel, out_shape=jax.ShapeDtypeStruct((8, features)...]
    mul x2 -> x1, other arithmetic: 1.56 us -> 0.89 us  [per_device(): keep * scale]
    pallas_call x1, Pallas kernels: 12.7 us -> 12.2 us  [per_device(): pl.pallas_call(functools.partial(sums_kernel, assets, block), in_specs=[r...]
    ppermute x9 -> x7, starting transfers between devices: 9.88 us -> 9.39 us  [swap(): return lax.ppermute(value, AXES, [(i, i ^ mask) for i in range(count)])]
    ppermute x9 -> x7, waiting for transfers between devices: 9.98 us -> 10.2 us  [swap(): return lax.ppermute(value, AXES, [(i, i ^ mask) for i in range(count)])]
  transfers between devices with their start and end apart: 9 -> 7, of which waited for: 6 -> 6; matrix products, arithmetic and copies ran while one was open for 4% -> 2% of each run, Pallas kernels for 10% -> 8%
where the time goes in v3:
time: 41.8 us; the launch traced here: 41.6 us
  Pallas kernels  20.2 us (48%)
  waiting for transfers between devices  10.2 us (24%)
  starting transfers between devices  9.39 us (22%)
  other arithmetic  0.94 us (2%)
  between operations  0.83 us (2%)
    pallas_call x1, Pallas kernels, per_device(): pl.pallas_call(functools.partial(sums_kernel, assets, block), in_specs=[r...  12.2 us
    ppermute x7, waiting for transfers between devices, swap(): return lax.ppermute(value, AXES, [(i, i ^ mask) for i in range(count)])  10.2 us
    ppermute x7, starting transfers between devices, swap(): return lax.ppermute(value, AXES, [(i, i ^ mask) for i in range(count)])  9.39 us
    pallas_call x1, Pallas kernels, per_device(): pl.pallas_call(functools.partial(adjoint_kernel, assets, block), in_specs...  4.75 us
    pallas_call x1, Pallas kernels, per_device(): pl.pallas_call(solve_kernel, out_shape=jax.ShapeDtypeStruct((8, features)...  3.21 us
    mul x1, other arithmetic, per_device(): keep * scale  0.89 us
  transfers between devices with their start and end apart: 7, of which 6 were waited for; matrix products, arithmetic and copies ran while one was open for 2% of the time, Pallas kernels for 8%

profile of v3, /device:TPU:0, one launch (start us, length us, event | category | flops | bytes accessed | tf_op | source)
XLA Modules:
  0.0 41.6 jit_solution(11715075909990329169)
XLA Ops:
  0.6 12.2 %sums.1 = (f32[32,16384]{1,0:T(8,128)}, f32[32,16384]{1,0:T(8,128)}, f32[128,128]{1,0:T(8,128)}, f32[128,128]{1,0:T(8,128)}, f32[160,128]{1,0:T(8,128)}, /*index=5*/f32[160,128]{1,0:T(8,128)}) custom-call(f32[1,32]{1,0:T(1,128)} %bitcast.11, f32[1,32]{1,0:T(1,128)} %bitcast.13, f32[1,32]{1,0:T(1,128)} %bitcast.15, f32[128,128]{1,0:T(8,128)} %bitcast.7, ...), custom_call_target="tpu_custom_call" | custom-call | tf_op jit(solution)/shard_map/sums/pallas_call | solution.py:457
  12.8 0.5 %collective-permute-start = (f32[160,128]{1,0:T(8,128)}, f32[160,128]{1,0:T(8,128)S(1)}, u32[]{:S(2)}, u32[]{:S(2)}) collective-permute-start(f32[160,128]{1,0:T(8,128)} %get-tuple-element.15), channel_id=1, source_target_pairs={{0,1},{1,0},{2,3},{3,2},{4,5},{5,4},{6,7},{7,6},{8,9},{9,8},{10,11... | collective-permute-start | bytes 245768 | tf_op jit(solution)/shard_map/ppermute | solution.py:428
  13.4 0.9 %broadcast_multiply_fusion = f32[160,128]{1,0:T(8,128)S(1)} fusion(f32[160,128]{1,0:T(8,128)} %get-tuple-element.14), kind=kLoop, calls=%fused_computation.2 | loop fusion | flops 20480 | bytes 163840 | tf_op jit(solution)/shard_map/mul | solution.py:491
  14.3 0.2 collective-permute-done
  14.5 3.9 %collective-permute-start.3 = (f32[160,128]{1,0:T(8,128)S(1)}, f32[160,128]{1,0:T(8,128)S(1)}, u32[]{:S(2)}, u32[]{:S(2)}) collective-permute-start(f32[160,128]{1,0:T(8,128)S(1)} %multiply_add_fusion), channel_id=1, source_target_pairs={{0,18},{1,19},{2,16},{3,17},{4,22},{5,23},{6,20},{7,21},{8,26},{9,... | collective-permute-start | bytes 245768 | tf_op jit(solution)/shard_map/ppermute | solution.py:428
  18.4 0.5 %collective-permute-start.2 = (f32[160,128]{1,0:T(8,128)S(1)}, f32[160,128]{1,0:T(8,128)S(1)}, u32[]{:S(2)}, u32[]{:S(2)}) collective-permute-start(f32[160,128]{1,0:T(8,128)S(1)} %multiply_add_fusion), channel_id=1, source_target_pairs={{0,16},{1,17},{2,18},{3,19},{4,20},{5,21},{6,22},{7,23},{8,24},{9,... | collective-permute-start | bytes 245768 | tf_op jit(solution)/shard_map/ppermute | solution.py:428
  18.9 0.1 collective-permute-start.1
  19.0 2.5 %collective-permute-done.3 = f32[160,128]{1,0:T(8,128)S(1)} collective-permute-done((f32[160,128]{1,0:T(8,128)S(1)}, f32[160,128]{1,0:T(8,128)S(1)}, u32[]{:S(2)}, u32[]{:S(2)}) %collective-permute-start.3) | collective-permute-done | bytes 81952 | tf_op jit(solution)/shard_map/ppermute | solution.py:428
  21.5 1.6 %collective-permute-done.2 = f32[160,128]{1,0:T(8,128)S(1)} collective-permute-done((f32[160,128]{1,0:T(8,128)S(1)}, f32[160,128]{1,0:T(8,128)S(1)}, u32[]{:S(2)}, u32[]{:S(2)}) %collective-permute-start.2) | collective-permute-done | bytes 81952 | tf_op jit(solution)/shard_map/ppermute | solution.py:428
  23.1 0.2 collective-permute-done.1
  23.4 1.6 %collective-permute-start.4 = (f32[160,128]{1,0:T(8,128)S(1)}, f32[160,128]{1,0:T(8,128)S(1)}, u32[]{:S(2)}, u32[]{:S(2)}) collective-permute-start(f32[160,128]{1,0:T(8,128)S(1)} %add_add_fusion), channel_id=1, source_target_pairs={{0,4},{1,5},{2,6},{3,7},{4,0},{5,1},{6,2},{7,3},{8,12},{9,13},{10,... | collective-permute-start | bytes 245768 | tf_op jit(solution)/shard_map/ppermute | solution.py:428
  25.0 2.9 %collective-permute-done.4 = f32[160,128]{1,0:T(8,128)S(1)} collective-permute-done((f32[160,128]{1,0:T(8,128)S(1)}, f32[160,128]{1,0:T(8,128)S(1)}, u32[]{:S(2)}, u32[]{:S(2)}) %collective-permute-start.4) | collective-permute-done | bytes 81952 | tf_op jit(solution)/shard_map/ppermute | solution.py:428
  27.9 2.7 %collective-permute-start.5 = (f32[160,128]{1,0:T(8,128)S(1)}, f32[160,128]{1,0:T(8,128)S(1)}, u32[]{:S(2)}, u32[]{:S(2)}) collective-permute-start(f32[160,128]{1,0:T(8,128)S(1)} %add.22), channel_id=1, source_target_pairs={{0,8},{1,9},{2,10},{3,11},{4,12},{5,13},{6,14},{7,15},{8,0},{9,1},... | collective-permute-start | bytes 245768 | tf_op jit(solution)/shard_map/ppermute | solution.py:428
  30.5 2.7 %collective-permute-done.5 = f32[160,128]{1,0:T(8,128)S(1)} collective-permute-done((f32[160,128]{1,0:T(8,128)S(1)}, f32[160,128]{1,0:T(8,128)S(1)}, u32[]{:S(2)}, u32[]{:S(2)}) %collective-permute-start.5) | collective-permute-done | bytes 81952 | tf_op jit(solution)/shard_map/ppermute | solution.py:428
  33.3 0.0 copy-start
  33.3 0.0 copy-start.1
  33.4 0.0 copy-start.2
  33.4 0.0 copy-start.3
  33.4 0.0 copy-start.4
  33.4 0.0 copy-start.5
  33.4 0.0 copy-start.6
  33.4 0.0 copy-start.7
  33.4 0.0 copy-start.8
  33.4 0.1 collective-permute-start.6
  33.5 3.2 %solve.1.solved = f32[8,128]{1,0:T(8,128)S(1)} custom-call(f32[72,128]{1,0:T(8,128)S(1)} %slice.8.packed), custom_call_target="tpu_custom_call" | custom-call | flops 4000000000 | bytes 15000000 | tf_op jit(solution)/shard_map/solve/pallas_call | solution.py:496
  36.7 0.0 collective-permute-done.6.jac_other
  36.7 0.0 copy-done
  36.7 0.0 copy-done.1
  36.8 0.0 copy-done.2
  36.8 0.0 copy-done.3
  36.8 0.0 copy-done.4
  36.8 0.0 copy-done.5
  36.8 0.0 copy-done.6
  36.8 0.0 copy-done.7
  36.8 0.0 copy-done.8
  36.8 4.8 %adjoint.1 = (f32[128,128]{1,0:T(8,128)}, f32[128,128]{1,0:T(8,128)}, f32[2,32]{1,0:T(2,128)}, f32[32,16384]{1,0:T(8,128)}) custom-call(f32[8,128]{1,0:T(8,128)S(1)} %solve.1.solved, f32[88,128]{1,0:T(8,128)S(1)} %slice.9.jac_mine, f32[88,128]{1,0:T(8,128)S(1)} %collective-permute-done.6.jac_other, f32[1,32]{1,0:T(1,128)S(1)} %bitcast.12, ...), custom_call_target="tpu_custom_call" | custom-call | tf_op jit(solution)/shard_map/adjoint/pallas_call | solution.py:506
  (6 shorter events, 0.1 us)
Async XLA Ops:
  12.8 1.7 %collective-permute-start = (f32[160,128]{1,0:T(8,128)}, f32[160,128]{1,0:T(8,128)S(1)}, u32[]{:S(2)}, u32[]{:S(2)}) collective-permute-start(f32[160,128]{1,0:T(8,128)} %get-tuple-element.15), channel_id=1, source_target_pairs={{0,1},{1,0},{2,3},{3,2},{4,5},{5,4},{6,7},{7,6},{8,9},{9,8},{10,11... | collective-permute-start | bytes 245768 | tf_op jit(solution)/shard_map/ppermute | solution.py:428
  14.5 7.0 %collective-permute-start.3 = (f32[160,128]{1,0:T(8,128)S(1)}, f32[160,128]{1,0:T(8,128)S(1)}, u32[]{:S(2)}, u32[]{:S(2)}) collective-permute-start(f32[160,128]{1,0:T(8,128)S(1)} %multiply_add_fusion), channel_id=1, source_target_pairs={{0,18},{1,19},{2,16},{3,17},{4,22},{5,23},{6,20},{7,21},{8,26},{9,... | collective-permute-start | bytes 245768 | tf_op jit(solution)/shard_map/ppermute | solution.py:428
  18.4 4.8 %collective-permute-start.2 = (f32[160,128]{1,0:T(8,128)S(1)}, f32[160,128]{1,0:T(8,128)S(1)}, u32[]{:S(2)}, u32[]{:S(2)}) collective-permute-start(f32[160,128]{1,0:T(8,128)S(1)} %multiply_add_fusion), channel_id=1, source_target_pairs={{0,16},{1,17},{2,18},{3,19},{4,20},{5,21},{6,22},{7,23},{8,24},{9,... | collective-permute-start | bytes 245768 | tf_op jit(solution)/shard_map/ppermute | solution.py:428
  18.9 4.4 %collective-permute-start.1 = (f32[160,128]{1,0:T(8,128)S(1)}, f32[160,128]{1,0:T(8,128)S(1)}, u32[]{:S(2)}, u32[]{:S(2)}) collective-permute-start(f32[160,128]{1,0:T(8,128)S(1)} %multiply_add_fusion), channel_id=1, source_target_pairs={{0,2},{1,3},{2,0},{3,1},{4,6},{5,7},{6,4},{7,5},{8,10},{9,11},{10,... | collective-permute-start | bytes 245768 | tf_op jit(solution)/shard_map/ppermute | solution.py:428
  23.4 4.5 %collective-permute-start.4 = (f32[160,128]{1,0:T(8,128)S(1)}, f32[160,128]{1,0:T(8,128)S(1)}, u32[]{:S(2)}, u32[]{:S(2)}) collective-permute-start(f32[160,128]{1,0:T(8,128)S(1)} %add_add_fusion), channel_id=1, source_target_pairs={{0,4},{1,5},{2,6},{3,7},{4,0},{5,1},{6,2},{7,3},{8,12},{9,13},{10,... | collective-permute-start | bytes 245768 | tf_op jit(solution)/shard_map/ppermute | solution.py:428
  27.9 5.4 %collective-permute-start.5 = (f32[160,128]{1,0:T(8,128)S(1)}, f32[160,128]{1,0:T(8,128)S(1)}, u32[]{:S(2)}, u32[]{:S(2)}) collective-permute-start(f32[160,128]{1,0:T(8,128)S(1)} %add.22), channel_id=1, source_target_pairs={{0,8},{1,9},{2,10},{3,11},{4,12},{5,13},{6,14},{7,15},{8,0},{9,1},... | collective-permute-start | bytes 245768 | tf_op jit(solution)/shard_map/ppermute | solution.py:428
  33.3 3.4 %copy-start = (f32[32,16384]{1,0:T(8,128)S(1)}, f32[32,16384]{1,0:T(8,128)}, u32[]{:S(2)}) copy-start(f32[32,16384]{1,0:T(8,128)} %get-tuple-element.18.scaled_in) | copy-start | bytes 6291460
  33.3 3.4 %copy-start.1 = (f32[32,16384]{1,0:T(8,128)S(1)}, f32[32,16384]{1,0:T(8,128)}, u32[]{:S(2)}) copy-start(f32[32,16384]{1,0:T(8,128)} %get-tuple-element.19.bounded_in) | copy-start | bytes 6291460
  33.4 3.4 %copy-start.2 = (f32[16384]{0:T(1024)S(1)}, f32[16384]{0:T(1024)}, u32[]{:S(2)}) copy-start(f32[16384]{0:T(1024)} %param.10) | copy-start | bytes 196612
  33.4 3.4 %copy-start.3 = (s32[16384]{0:T(1024)S(1)}, s32[16384]{0:T(1024)}, u32[]{:S(2)}) copy-start(s32[16384]{0:T(1024)} %param.11) | copy-start | bytes 196612
  33.4 3.4 %copy-start.4 = (f32[128,128]{1,0:T(8,128)S(1)}, f32[128,128]{1,0:T(8,128)}, u32[]{:S(2)}) copy-start(f32[128,128]{1,0:T(8,128)} %get-tuple-element.16.value_in) | copy-start | bytes 196612
  33.4 3.4 %copy-start.5 = (f32[128,128]{1,0:T(8,128)S(1)}, f32[128,128]{1,0:T(8,128)}, u32[]{:S(2)}) copy-start(f32[128,128]{1,0:T(8,128)} %get-tuple-element.17.pull_in) | copy-start | bytes 196612
  33.4 3.4 %copy-start.6 = (f32[32]{0:T(128)S(1)}, f32[32]{0:T(128)}, u32[]{:S(2)}) copy-start(f32[32]{0:T(128)} %param.7) | copy-start | bytes 388
  33.4 3.4 %copy-start.7 = (f32[32]{0:T(128)S(1)}, f32[32]{0:T(128)}, u32[]{:S(2)}) copy-start(f32[32]{0:T(128)} %param.8) | copy-start | bytes 388
  33.4 3.4 %copy-start.8 = (f32[32]{0:T(128)S(1)}, f32[32]{0:T(128)}, u32[]{:S(2)}) copy-start(f32[32]{0:T(128)} %param.9) | copy-start | bytes 388
  33.4 3.3 %collective-permute-start.6 = (f32[88,128]{1,0:T(8,128)S(1)}, f32[88,128]{1,0:T(8,128)S(1)}, u32[]{:S(2)}, u32[]{:S(2)}) collective-permute-start(f32[88,128]{1,0:T(8,128)S(1)} %slice.9.jac_mine), channel_id=1, source_target_pairs={{0,1},{1,0},{2,3},{3,2},{4,5},{5,4},{6,7},{7,6},{8,9},{9,8},{10,11... | collective-permute-start | bytes 135176 | tf_op jit(solution)/shard_map/ppermute | solution.py:428

commit v4 on v3

--- a/solution.py
+++ b/solution.py
@@ -453,9 +453,10 @@
     remote = pl.BlockSpec(memory_space=pltpu.HBM)
     local = pl.BlockSpec(memory_space=pltpu.VMEM)
     short = jax.ShapeDtypeStruct(compact, F32)
-    rows = pltpu.VMEM((10 * assets + 16 + 2 * features, block), BF16)
+    wide = 16 * LANES
+    rows = pltpu.VMEM((10 * assets + 16 + 2 * features, wide), BF16)
     scaled, bounded, value, pull, keep, give = pl.pallas_call(
-        functools.partial(sums_kernel, assets, block),
+        functools.partial(sums_kernel, assets, wide),
         in_specs=[remote] * 6,
         out_specs=[remote] * 2 + [local] * 4,
         out_shape=[
@@ -468,18 +469,18 @@
             pltpu.VMEM(compact, jnp.int32),
             pltpu.VMEM((assets, paths), F32),
             pltpu.VMEM((4, assets, LANES), F32),
-            pltpu.VMEM((64, LANES), F32),
-            pltpu.VMEM((16, block), F32),
+            pltpu.VMEM((wide // 16, LANES), F32),
+            pltpu.VMEM((16, wide), F32),
             pltpu.VMEM((assets, paths), F32),
             pltpu.VMEM((assets, paths), F32),
-            pltpu.VMEM((assets, block), F32),
+            pltpu.VMEM((assets, wide), F32),
             rows, rows,
             pltpu.VMEM((10 * assets + 16 + features, 2 * features), F32),
             pltpu.VMEM((5 * assets, LANES), F32),
             pltpu.VMEM((assets, LANES), F32),
             pltpu.VMEM((jac_rows, features), F32),
-            pltpu.SemaphoreType.DMA((5 + paths // (2 * block),)),
-            pltpu.SemaphoreType.DMA((2, paths // (2 * block))),
+            pltpu.SemaphoreType.DMA((5 + paths // (2 * wide),)),
+            pltpu.SemaphoreType.DMA((2, paths // (2 * wide))),
         ],
         compiler_params=pltpu.CompilerParams(vmem_limit_bytes=60 * 1024 * 1024),
         name="sums",
@@ -510,8 +511,8 @@
         out_shape=[short, short, jax.ShapeDtypeStruct((2, assets), F32), big],
         scratch_shapes=[
             pltpu.VMEM((12, assets, LANES), F32),
-            pltpu.VMEM((2, 2, 64, LANES), F32),
-            pltpu.VMEM((2, 3, 8, LANES), F32),
+            pltpu.VMEM((2, 2, block // 16, LANES), F32),
+            pltpu.VMEM((2, 3, block // LANES, LANES), F32),
             pltpu.VMEM((2, 2, assets, block), F32),
             pltpu.VMEM((assets, paths), F32),
             pltpu.VMEM((jac_rows, features), F32),

time: 41.8 us -> 41.3 us (0.988)
  Pallas kernels: 20.2 us -> 19.7 us
    pallas_call x1, Pallas kernels: 12.2 us -> 11.7 us  [per_device(): pl.pallas_call(functools.partial(sums_kernel, assets, wide), in_specs=[re...]
where the time goes in v4:
time: 41.3 us; the launch traced here: 41.1 us
  Pallas kernels  19.7 us (48%)
  waiting for transfers between devices  10.2 us (25%)
  starting transfers between devices  9.37 us (23%)
  other arithmetic  0.94 us (2%)
  between operations  0.83 us (2%)
    pallas_call x1, Pallas kernels, per_device(): pl.pallas_call(functools.partial(sums_kernel, assets, wide), in_specs=[re...  11.7 us
    ppermute x7, waiting for transfers between devices, swap(): return lax.ppermute(value, AXES, [(i, i ^ mask) for i in range(count)])  10.2 us
    ppermute x7, starting transfers between devices, swap(): return lax.ppermute(value, AXES, [(i, i ^ mask) for i in range(count)])  9.37 us
    pallas_call x1, Pallas kernels, per_device(): pl.pallas_call(functools.partial(adjoint_kernel, assets, block), in_specs...  4.75 us
    pallas_call x1, Pallas kernels, per_device(): pl.pallas_call(solve_kernel, out_shape=jax.ShapeDtypeStruct((8, features)...  3.21 us
    mul x1, other arithmetic, per_device(): keep * scale  0.89 us
  transfers between devices with their start and end apart: 7, of which 6 were waited for; matrix products, arithmetic and copies ran while one was open for 2% of the time, Pallas kernels for 8%

profile of v4, /device:TPU:0, one launch (start us, length us, event | category | flops | bytes accessed | tf_op | source)
XLA Modules:
  0.0 41.1 jit_solution(778352436140002461)
XLA Ops:
  0.6 11.7 %sums.1 = (f32[32,16384]{1,0:T(8,128)}, f32[32,16384]{1,0:T(8,128)}, f32[128,128]{1,0:T(8,128)}, f32[128,128]{1,0:T(8,128)}, f32[160,128]{1,0:T(8,128)}, /*index=5*/f32[160,128]{1,0:T(8,128)}) custom-call(f32[1,32]{1,0:T(1,128)} %bitcast.11, f32[1,32]{1,0:T(1,128)} %bitcast.13, f32[1,32]{1,0:T(1,128)} %bitcast.15, f32[128,128]{1,0:T(8,128)} %bitcast.7, ...), custom_call_target="tpu_custom_call" | custom-call | tf_op jit(solution)/shard_map/sums/pallas_call | solution.py:458
  12.4 0.5 %collective-permute-start = (f32[160,128]{1,0:T(8,128)}, f32[160,128]{1,0:T(8,128)S(1)}, u32[]{:S(2)}, u32[]{:S(2)}) collective-permute-start(f32[160,128]{1,0:T(8,128)} %get-tuple-element.15), channel_id=1, source_target_pairs={{0,1},{1,0},{2,3},{3,2},{4,5},{5,4},{6,7},{7,6},{8,9},{9,8},{10,11... | collective-permute-start | bytes 245768 | tf_op jit(solution)/shard_map/ppermute | solution.py:428
  12.9 0.9 %broadcast_multiply_fusion = f32[160,128]{1,0:T(8,128)S(1)} fusion(f32[160,128]{1,0:T(8,128)} %get-tuple-element.14), kind=kLoop, calls=%fused_computation.2 | loop fusion | flops 20480 | bytes 163840 | tf_op jit(solution)/shard_map/mul | solution.py:492
  13.8 0.2 collective-permute-done
  14.0 3.9 %collective-permute-start.3 = (f32[160,128]{1,0:T(8,128)S(1)}, f32[160,128]{1,0:T(8,128)S(1)}, u32[]{:S(2)}, u32[]{:S(2)}) collective-permute-start(f32[160,128]{1,0:T(8,128)S(1)} %multiply_add_fusion), channel_id=1, source_target_pairs={{0,18},{1,19},{2,16},{3,17},{4,22},{5,23},{6,20},{7,21},{8,26},{9,... | collective-permute-start | bytes 245768 | tf_op jit(solution)/shard_map/ppermute | solution.py:428
  17.9 0.5 %collective-permute-start.2 = (f32[160,128]{1,0:T(8,128)S(1)}, f32[160,128]{1,0:T(8,128)S(1)}, u32[]{:S(2)}, u32[]{:S(2)}) collective-permute-start(f32[160,128]{1,0:T(8,128)S(1)} %multiply_add_fusion), channel_id=1, source_target_pairs={{0,16},{1,17},{2,18},{3,19},{4,20},{5,21},{6,22},{7,23},{8,24},{9,... | collective-permute-start | bytes 245768 | tf_op jit(solution)/shard_map/ppermute | solution.py:428
  18.4 0.1 collective-permute-start.1
  18.5 2.5 %collective-permute-done.3 = f32[160,128]{1,0:T(8,128)S(1)} collective-permute-done((f32[160,128]{1,0:T(8,128)S(1)}, f32[160,128]{1,0:T(8,128)S(1)}, u32[]{:S(2)}, u32[]{:S(2)}) %collective-permute-start.3) | collective-permute-done | bytes 81952 | tf_op jit(solution)/shard_map/ppermute | solution.py:428
  21.0 1.6 %collective-permute-done.2 = f32[160,128]{1,0:T(8,128)S(1)} collective-permute-done((f32[160,128]{1,0:T(8,128)S(1)}, f32[160,128]{1,0:T(8,128)S(1)}, u32[]{:S(2)}, u32[]{:S(2)}) %collective-permute-start.2) | collective-permute-done | bytes 81952 | tf_op jit(solution)/shard_map/ppermute | solution.py:428
  22.7 0.2 collective-permute-done.1
  22.9 1.6 %collective-permute-start.4 = (f32[160,128]{1,0:T(8,128)S(1)}, f32[160,128]{1,0:T(8,128)S(1)}, u32[]{:S(2)}, u32[]{:S(2)}) collective-permute-start(f32[160,128]{1,0:T(8,128)S(1)} %add_add_fusion), channel_id=1, source_target_pairs={{0,4},{1,5},{2,6},{3,7},{4,0},{5,1},{6,2},{7,3},{8,12},{9,13},{10,... | collective-permute-start | bytes 245768 | tf_op jit(solution)/shard_map/ppermute | solution.py:428
  24.5 2.9 %collective-permute-done.4 = f32[160,128]{1,0:T(8,128)S(1)} collective-permute-done((f32[160,128]{1,0:T(8,128)S(1)}, f32[160,128]{1,0:T(8,128)S(1)}, u32[]{:S(2)}, u32[]{:S(2)}) %collective-permute-start.4) | collective-permute-done | bytes 81952 | tf_op jit(solution)/shard_map/ppermute | solution.py:428
  27.4 2.6 %collective-permute-start.5 = (f32[160,128]{1,0:T(8,128)S(1)}, f32[160,128]{1,0:T(8,128)S(1)}, u32[]{:S(2)}, u32[]{:S(2)}) collective-permute-start(f32[160,128]{1,0:T(8,128)S(1)} %add.22), channel_id=1, source_target_pairs={{0,8},{1,9},{2,10},{3,11},{4,12},{5,13},{6,14},{7,15},{8,0},{9,1},... | collective-permute-start | bytes 245768 | tf_op jit(solution)/shard_map/ppermute | solution.py:428
  30.1 2.8 %collective-permute-done.5 = f32[160,128]{1,0:T(8,128)S(1)} collective-permute-done((f32[160,128]{1,0:T(8,128)S(1)}, f32[160,128]{1,0:T(8,128)S(1)}, u32[]{:S(2)}, u32[]{:S(2)}) %collective-permute-start.5) | collective-permute-done | bytes 81952 | tf_op jit(solution)/shard_map/ppermute | solution.py:428
  32.9 0.0 copy-start
  32.9 0.0 copy-start.1
  32.9 0.0 copy-start.2
  32.9 0.0 copy-start.3
  32.9 0.0 copy-start.4
  32.9 0.0 copy-start.5
  32.9 0.0 copy-start.6
  32.9 0.0 copy-start.7
  32.9 0.0 copy-start.8
  33.0 0.1 collective-permute-start.6
  33.0 3.2 %solve.1.solved = f32[8,128]{1,0:T(8,128)S(1)} custom-call(f32[72,128]{1,0:T(8,128)S(1)} %slice.8.packed), custom_call_target="tpu_custom_call" | custom-call | flops 4000000000 | bytes 15000000 | tf_op jit(solution)/shard_map/solve/pallas_call | solution.py:497
  36.2 0.0 collective-permute-done.6.jac_other
  36.3 0.0 copy-done
  36.3 0.0 copy-done.1
  36.3 0.0 copy-done.2
  36.3 0.0 copy-done.3
  36.3 0.0 copy-done.4
  36.3 0.0 copy-done.5
  36.3 0.0 copy-done.6
  36.3 0.0 copy-done.7
  36.3 0.0 copy-done.8
  36.3 4.8 %adjoint.1 = (f32[128,128]{1,0:T(8,128)}, f32[128,128]{1,0:T(8,128)}, f32[2,32]{1,0:T(2,128)}, f32[32,16384]{1,0:T(8,128)}) custom-call(f32[8,128]{1,0:T(8,128)S(1)} %solve.1.solved, f32[88,128]{1,0:T(8,128)S(1)} %slice.9.jac_mine, f32[88,128]{1,0:T(8,128)S(1)} %collective-permute-done.6.jac_other, f32[1,32]{1,0:T(1,128)S(1)} %bitcast.12, ...), custom_call_target="tpu_custom_call" | custom-call | tf_op jit(solution)/shard_map/adjoint/pallas_call | solution.py:507
  (6 shorter events, 0.1 us)
Async XLA Ops:
  12.4 1.7 %collective-permute-start = (f32[160,128]{1,0:T(8,128)}, f32[160,128]{1,0:T(8,128)S(1)}, u32[]{:S(2)}, u32[]{:S(2)}) collective-permute-start(f32[160,128]{1,0:T(8,128)} %get-tuple-element.15), channel_id=1, source_target_pairs={{0,1},{1,0},{2,3},{3,2},{4,5},{5,4},{6,7},{7,6},{8,9},{9,8},{10,11... | collective-permute-start | bytes 245768 | tf_op jit(solution)/shard_map/ppermute | solution.py:428
  14.0 7.0 %collective-permute-start.3 = (f32[160,128]{1,0:T(8,128)S(1)}, f32[160,128]{1,0:T(8,128)S(1)}, u32[]{:S(2)}, u32[]{:S(2)}) collective-permute-start(f32[160,128]{1,0:T(8,128)S(1)} %multiply_add_fusion), channel_id=1, source_target_pairs={{0,18},{1,19},{2,16},{3,17},{4,22},{5,23},{6,20},{7,21},{8,26},{9,... | collective-permute-start | bytes 245768 | tf_op jit(solution)/shard_map/ppermute | solution.py:428
  17.9 4.8 %collective-permute-start.2 = (f32[160,128]{1,0:T(8,128)S(1)}, f32[160,128]{1,0:T(8,128)S(1)}, u32[]{:S(2)}, u32[]{:S(2)}) collective-permute-start(f32[160,128]{1,0:T(8,128)S(1)} %multiply_add_fusion), channel_id=1, source_target_pairs={{0,16},{1,17},{2,18},{3,19},{4,20},{5,21},{6,22},{7,23},{8,24},{9,... | collective-permute-start | bytes 245768 | tf_op jit(solution)/shard_map/ppermute | solution.py:428
  18.4 4.4 %collective-permute-start.1 = (f32[160,128]{1,0:T(8,128)S(1)}, f32[160,128]{1,0:T(8,128)S(1)}, u32[]{:S(2)}, u32[]{:S(2)}) collective-permute-start(f32[160,128]{1,0:T(8,128)S(1)} %multiply_add_fusion), channel_id=1, source_target_pairs={{0,2},{1,3},{2,0},{3,1},{4,6},{5,7},{6,4},{7,5},{8,10},{9,11},{10,... | collective-permute-start | bytes 245768 | tf_op jit(solution)/shard_map/ppermute | solution.py:428
  22.9 4.5 %collective-permute-start.4 = (f32[160,128]{1,0:T(8,128)S(1)}, f32[160,128]{1,0:T(8,128)S(1)}, u32[]{:S(2)}, u32[]{:S(2)}) collective-permute-start(f32[160,128]{1,0:T(8,128)S(1)} %add_add_fusion), channel_id=1, source_target_pairs={{0,4},{1,5},{2,6},{3,7},{4,0},{5,1},{6,2},{7,3},{8,12},{9,13},{10,... | collective-permute-start | bytes 245768 | tf_op jit(solution)/shard_map/ppermute | solution.py:428
  27.4 5.4 %collective-permute-start.5 = (f32[160,128]{1,0:T(8,128)S(1)}, f32[160,128]{1,0:T(8,128)S(1)}, u32[]{:S(2)}, u32[]{:S(2)}) collective-permute-start(f32[160,128]{1,0:T(8,128)S(1)} %add.22), channel_id=1, source_target_pairs={{0,8},{1,9},{2,10},{3,11},{4,12},{5,13},{6,14},{7,15},{8,0},{9,1},... | collective-permute-start | bytes 245768 | tf_op jit(solution)/shard_map/ppermute | solution.py:428
  32.9 3.4 %copy-start = (f32[32,16384]{1,0:T(8,128)S(1)}, f32[32,16384]{1,0:T(8,128)}, u32[]{:S(2)}) copy-start(f32[32,16384]{1,0:T(8,128)} %get-tuple-element.18.scaled_in) | copy-start | bytes 6291460
  32.9 3.4 %copy-start.1 = (f32[32,16384]{1,0:T(8,128)S(1)}, f32[32,16384]{1,0:T(8,128)}, u32[]{:S(2)}) copy-start(f32[32,16384]{1,0:T(8,128)} %get-tuple-element.19.bounded_in) | copy-start | bytes 6291460
  32.9 3.4 %copy-start.2 = (f32[16384]{0:T(1024)S(1)}, f32[16384]{0:T(1024)}, u32[]{:S(2)}) copy-start(f32[16384]{0:T(1024)} %param.10) | copy-start | bytes 196612
  32.9 3.4 %copy-start.3 = (s32[16384]{0:T(1024)S(1)}, s32[16384]{0:T(1024)}, u32[]{:S(2)}) copy-start(s32[16384]{0:T(1024)} %param.11) | copy-start | bytes 196612
  32.9 3.4 %copy-start.4 = (f32[128,128]{1,0:T(8,128)S(1)}, f32[128,128]{1,0:T(8,128)}, u32[]{:S(2)}) copy-start(f32[128,128]{1,0:T(8,128)} %get-tuple-element.16.value_in) | copy-start | bytes 196612
  32.9 3.4 %copy-start.5 = (f32[128,128]{1,0:T(8,128)S(1)}, f32[128,128]{1,0:T(8,128)}, u32[]{:S(2)}) copy-start(f32[128,128]{1,0:T(8,128)} %get-tuple-element.17.pull_in) | copy-start | bytes 196612
  32.9 3.4 %copy-start.6 = (f32[32]{0:T(128)S(1)}, f32[32]{0:T(128)}, u32[]{:S(2)}) copy-start(f32[32]{0:T(128)} %param.7) | copy-start | bytes 388
  32.9 3.4 %copy-start.7 = (f32[32]{0:T(128)S(1)}, f32[32]{0:T(128)}, u32[]{:S(2)}) copy-start(f32[32]{0:T(128)} %param.8) | copy-start | bytes 388
  32.9 3.4 %copy-start.8 = (f32[32]{0:T(128)S(1)}, f32[32]{0:T(128)}, u32[]{:S(2)}) copy-start(f32[32]{0:T(128)} %param.9) | copy-start | bytes 388
  33.0 3.3 %collective-permute-start.6 = (f32[88,128]{1,0:T(8,128)S(1)}, f32[88,128]{1,0:T(8,128)S(1)}, u32[]{:S(2)}, u32[]{:S(2)}) collective-permute-start(f32[88,128]{1,0:T(8,128)S(1)} %slice.9.jac_mine), channel_id=1, source_target_pairs={{0,1},{1,0},{2,3},{3,2},{4,5},{5,4},{6,7},{7,6},{8,9},{9,8},{10,11... | collective-permute-start | bytes 135176 | tf_op jit(solution)/shard_map/ppermute | solution.py:428

commit v5 on v4

--- a/solution.py
+++ b/solution.py
@@ -40,9 +40,9 @@
 
 def sums_kernel(
     assets, width, spot, vol, weights, cash, taken, normals,
-    scaled_out, bounded_out, value_out, pull_out, keep, give,
+    scaled_out, bounded_out, value_out, pull_out, keep_out, give_out,
     small, flows, flags, draws, coef, part, target,
-    scaled_all, bounded_all, slopes, rows_a, rows_b, acc, flow_acc, pull_acc, jac, sems, sent,
+    scaled_all, bounded_all, value_all, pull_all, keep, give, slopes, rows_a, rows_b, acc, flow_acc, pull_acc, jac, sems, sent,
 ):
     features = 4 * assets
     paths = draws.shape[1]
@@ -62,9 +62,12 @@
 
     def leave(index):
         at = pl.ds(pl.multiple_of(index * (2 * width), 2 * width), 2 * width)
+        line = pl.ds(pl.multiple_of(index * (2 * chunks), 2 * chunks), 2 * chunks)
         return [
             pltpu.make_async_copy(scaled_all.at[:, at], scaled_out.at[:, at], sent.at[0, index]),
             pltpu.make_async_copy(bounded_all.at[:, at], bounded_out.at[:, at], sent.at[1, index]),
+            pltpu.make_async_copy(value_all.at[line, :], value_out.at[line, :], sent.at[2, index]),
+            pltpu.make_async_copy(pull_all.at[line, :], pull_out.at[line, :], sent.at[3, index]),
         ]
 
     for copy in copies[:3]:
@@ -92,7 +95,6 @@
         copy.wait()
 
     last = lax.broadcasted_iota(jnp.int32, (assets, LANES), 0) == assets - 1
-    tail = lax.broadcasted_iota(jnp.int32, (16, LANES), 0) == 15
     aim, base, low = 10 * assets, 10 * assets + 16, 10 * assets + 16 + features
 
     def fill(block, rows, half):
@@ -100,7 +102,6 @@
         flag = flags[line, :].astype(F32)
         flow = flows[line, :]
         rest = 1.0 - flag
-        flow_sum = 0.0
         for c in range(half * chunks // 2, (half + 1) * chunks // 2):
             at = pl.ds(pl.multiple_of(block * width, width) + c * LANES, LANES)
             here = pl.ds(c * LANES, LANES)
@@ -115,26 +116,31 @@
             bounded_all[:, at] = bounded
             after = pltpu.roll(scaled, assets - 1, 0)
             before = pltpu.roll(scaled, 1, 0)
-            basis = jnp.concatenate(
-                [scaled, scaled * scaled - 1.0, scaled * after, bounded], axis=0
-            )
-            hi, lo = split(basis)
-            rows[base : base + features, here] = hi
-            rows[low : low + features - 16, here] = lo[: features - 16]
-            ends = (basis - hi.astype(F32))[features - 16 :]
-            kept = jnp.broadcast_to(rest[c : c + 1, :], (16, LANES))
-            rows[low + features - 16 :, here] = jnp.where(tail, kept, ends).astype(BF16)
+            kept = jnp.broadcast_to(rest[c : c + 1, :], (assets, LANES))
+            for g, make in enumerate(
+                [lambda: scaled, lambda: scaled * scaled - 1.0, lambda: scaled * after, lambda: bounded]
+            ):
+                wide = make()
+                high = wide.astype(BF16)
+                less = wide - high.astype(F32)
+                if g == 3:
+                    less = jnp.where(last, kept, less)
+                rows[base + assets * g : base + assets * (g + 1), here] = high
+                rows[low + assets * g : low + assets * (g + 1), here] = less.astype(BF16)
             slope = growth * (draw - spread) - scaled
-            curve = 1.0 - bounded * bounded
-            tilt = jnp.concatenate(
-                [slope, slope * scaled, slope * after, slope * curve, slope * before], axis=0
-            )
-            hi, lo = split(tilt)
-            rows[0 : 5 * assets, here] = hi
-            rows[5 * assets : 10 * assets, here] = lo
-            flow_sum = flow_sum + tilt * jnp.broadcast_to(flow[c : c + 1, :], tilt.shape)
+            paid = jnp.broadcast_to(flow[c : c + 1, :], (assets, LANES))
+            for g, make in enumerate(
+                [
+                    lambda: slope, lambda: slope * scaled, lambda: slope * after,
+                    lambda: slope * (1.0 - bounded * bounded), lambda: slope * before,
+                ]
+            ):
+                wide = make()
+                high, less = split(wide)
+                rows[assets * g : assets * (g + 1), here] = high
+                rows[assets * (5 + g) : assets * (6 + g), here] = less
+                flow_acc[assets * g : assets * (g + 1), :] += wide * paid
             slopes[:, here] = slope
-        flow_acc[...] += flow_sum
         if half == 0:
             return
         basket = sum(part[pl.ds(i, chunks, stride=8), :] for i in range(8))
@@ -144,8 +150,8 @@
         inverse = 1.0 / (1.0 + decay)
         sigmoid = jnp.where(x >= 0.0, inverse, decay * inverse)
         pull = notional * flag * sigmoid
-        value_out[line, :] = flag * reward
-        pull_out[line, :] = pull
+        value_all[line, :] = flag * reward
+        pull_all[line, :] = pull
         flow_hi = flow.astype(BF16).astype(F32)
         pull_hi = pull.astype(BF16).astype(F32)
         pull_sum = 0.0
@@ -168,11 +174,11 @@
     def both(index, carry):
         pair(index).wait()
         for part in range(2):
+            fill(2 * index, rows_a, part)
             multiply(rows_b, part)
-            fill(2 * index, rows_a, part)
         for part in range(2):
+            fill(2 * index + 1, rows_b, part)
             multiply(rows_a, part)
-            fill(2 * index + 1, rows_b, part)
         for copy in leave(index):
             copy.start()
         return carry
@@ -226,6 +232,14 @@
     mine, other = halves(jac.shape[0] // 2)
     keep[mid + 8 :, :] = jac[mine, :]
     give[mid + 8 :, :] = jac[other, :]
+    last_copies = [
+        pltpu.make_async_copy(give, give_out, sems.at[0]),
+        pltpu.make_async_copy(keep, keep_out, sems.at[1]),
+    ]
+    for copy in last_copies:
+        copy.start()
+    for copy in last_copies:
+        copy.wait()
     for index in range(blocks // 2):
         for copy in leave(index):
             copy.wait()
@@ -307,7 +321,7 @@
     solved, jac_mine, jac_other, spot, vol, weights, cash, taken,
     value_in, pull_in, scaled_in, bounded_in,
     value_out, flow_out, greeks_out, cot_out,
-    coef, part, line, tangents, cot, jac, sent,
+    coef, part, line, tangents, cot, jac, values, flows, greeks, sent,
 ):
     features = 4 * assets
     paths = scaled_in.shape[1]
@@ -332,7 +346,12 @@
 
     def leave(index):
         at = pl.ds(pl.multiple_of(index * (2 * width), 2 * width), 2 * width)
-        return pltpu.make_async_copy(cot.at[:, at], cot_out.at[:, at], sent.at[index])
+        rows = pl.ds(pl.multiple_of(index * (2 * chunks), 2 * chunks), 2 * chunks)
+        return [
+            pltpu.make_async_copy(cot.at[:, at], cot_out.at[:, at], sent.at[0, index]),
+            pltpu.make_async_copy(values.at[rows, :], value_out.at[rows, :], sent.at[1, index]),
+            pltpu.make_async_copy(flows.at[rows, :], flow_out.at[rows, :], sent.at[2, index]),
+        ]
 
     def block(index, slot):
         for c in range(chunks):
@@ -360,8 +379,8 @@
             for which in range(2)
         ]
         rest = 1.0 - taken[at, :].astype(F32)
-        value_out[at, :] = value_in[at, :] + rest * fitted[0]
-        flow_out[at, :] = fitted[1]
+        values[at, :] = value_in[at, :] + rest * fitted[0]
+        flows[at, :] = fitted[1]
         line[slot, 0] = cash[at, :] - fitted[0]
         line[slot, 1] = rest - fitted[1]
         line[slot, 2] = pull_in[at, :]
@@ -378,10 +397,9 @@
     def both(index, carry):
         block(2 * index, 0)
         block(2 * index + 1, 1)
-        leave(index).start()
+        for copy in leave(index):
+            copy.start()
         return carry
-
-    lax.fori_loop(0, paths // (2 * width), both, 0)
 
     mine, other = halves(jac_mine.shape[0])
     jac[mine, :] = jac_mine[...]
@@ -418,9 +436,14 @@
     mean = jnp.sum(value * growth, axis=1, keepdims=True) / whole
     delta = weights[...] / whole * (growth - mean)
     vega = vega + value * root_time / whole * (pulled_slope + pulled_scaled)
-    greeks_out[...] = jnp.concatenate([delta, vega], axis=0)
+    greeks[...] = jnp.concatenate([delta, vega], axis=0)
+    whole_copy = pltpu.make_async_copy(greeks, greeks_out, sent.at[3, 0])
+    whole_copy.start()
+    lax.fori_loop(0, paths // (2 * width), both, 0)
+    whole_copy.wait()
     for index in range(paths // (2 * width)):
-        leave(index).wait()
+        for copy in leave(index):
+            copy.wait()
 
 
 def swap(value, mask):
@@ -458,7 +481,7 @@
     scaled, bounded, value, pull, keep, give = pl.pallas_call(
         functools.partial(sums_kernel, assets, wide),
         in_specs=[remote] * 6,
-        out_specs=[remote] * 2 + [local] * 4,
+        out_specs=[remote] * 6,
         out_shape=[
             big, big, short, short,
             sent, sent,
@@ -473,6 +496,10 @@
             pltpu.VMEM((16, wide), F32),
             pltpu.VMEM((assets, paths), F32),
             pltpu.VMEM((assets, paths), F32),
+            pltpu.VMEM(compact, F32),
+            pltpu.VMEM(compact, F32),
+            pltpu.VMEM(sent.shape, F32),
+            pltpu.VMEM(sent.shape, F32),
             pltpu.VMEM((assets, wide), F32),
             rows, rows,
             pltpu.VMEM((10 * assets + 16 + features, 2 * features), F32),
@@ -480,7 +507,7 @@
             pltpu.VMEM((assets, LANES), F32),
             pltpu.VMEM((jac_rows, features), F32),
             pltpu.SemaphoreType.DMA((5 + paths // (2 * wide),)),
-            pltpu.SemaphoreType.DMA((2, paths // (2 * wide))),
+            pltpu.SemaphoreType.DMA((4, paths // (2 * wide))),
         ],
         compiler_params=pltpu.CompilerParams(vmem_limit_bytes=60 * 1024 * 1024),
         name="sums",
@@ -507,7 +534,7 @@
     value, flow, greeks, cot = pl.pallas_call(
         functools.partial(adjoint_kernel, assets, block),
         in_specs=[local] * 12,
-        out_specs=[local] * 3 + [remote],
+        out_specs=[remote] * 4,
         out_shape=[short, short, jax.ShapeDtypeStruct((2, assets), F32), big],
         scratch_shapes=[
             pltpu.VMEM((12, assets, LANES), F32),
@@ -516,7 +543,10 @@
             pltpu.VMEM((2, 2, assets, block), F32),
             pltpu.VMEM((assets, paths), F32),
             pltpu.VMEM((jac_rows, features), F32),
-            pltpu.SemaphoreType.DMA((paths // (2 * block),)),
+            pltpu.VMEM(compact, F32),
+            pltpu.VMEM(compact, F32),
+            pltpu.VMEM((2, assets), F32),
+            pltpu.SemaphoreType.DMA((4, paths // (2 * block))),
         ],
         compiler_params=params,
         name="adjoint",

time: 41.3 us -> 41 us (level)
  no operation moved by 1% of the time
where the time goes in v5:
time: 41 us; the launch traced here: 40.8 us
  Pallas kernels  19.3 us (47%)
  waiting for transfers between devices  10.2 us (25%)
  starting transfers between devices  9.4 us (23%)
  other arithmetic  0.94 us (2%)
  between operations  0.83 us (2%)
    pallas_call x1, Pallas kernels, per_device(): pl.pallas_call(functools.partial(sums_kernel, assets, wide), in_specs=[re...  11.6 us
    ppermute x7, waiting for transfers between devices, swap(): return lax.ppermute(value, AXES, [(i, i ^ mask) for i in range(count)])  10.2 us
    ppermute x7, starting transfers between devices, swap(): return lax.ppermute(value, AXES, [(i, i ^ mask) for i in range(count)])  9.4 us
    pallas_call x1, Pallas kernels, per_device(): pl.pallas_call(functools.partial(adjoint_kernel, assets, block), in_specs...  4.53 us
    pallas_call x1, Pallas kernels, per_device(): pl.pallas_call(solve_kernel, out_shape=jax.ShapeDtypeStruct((8, features)...  3.21 us
    mul x1, other arithmetic, per_device(): keep * scale  0.89 us
  transfers between devices with their start and end apart: 7, of which 6 were waited for; matrix products, arithmetic and copies ran while one was open for 2% of the time, Pallas kernels for 8%

profile of v5, /device:TPU:0, one launch (start us, length us, event | category | flops | bytes accessed | tf_op | source)
XLA Modules:
  0.0 40.8 jit_solution(2057039641882938019)
XLA Ops:
  0.6 11.6 %sums.1 = (f32[32,16384]{1,0:T(8,128)}, f32[32,16384]{1,0:T(8,128)}, f32[128,128]{1,0:T(8,128)}, f32[128,128]{1,0:T(8,128)}, f32[160,128]{1,0:T(8,128)}, /*index=5*/f32[160,128]{1,0:T(8,128)}) custom-call(f32[1,32]{1,0:T(1,128)} %bitcast.11, f32[1,32]{1,0:T(1,128)} %bitcast.13, f32[1,32]{1,0:T(1,128)} %bitcast.15, f32[128,128]{1,0:T(8,128)} %bitcast.7, ...), custom_call_target="tpu_custom_call" | custom-call | tf_op jit(solution)/shard_map/sums/pallas_call | solution.py:481
  12.3 0.5 %collective-permute-start = (f32[160,128]{1,0:T(8,128)}, f32[160,128]{1,0:T(8,128)S(1)}, u32[]{:S(2)}, u32[]{:S(2)}) collective-permute-start(f32[160,128]{1,0:T(8,128)} %get-tuple-element.15), channel_id=1, source_target_pairs={{0,1},{1,0},{2,3},{3,2},{4,5},{5,4},{6,7},{7,6},{8,9},{9,8},{10,11... | collective-permute-start | bytes 245768 | tf_op jit(solution)/shard_map/ppermute | solution.py:451
  12.8 0.9 %broadcast_multiply_fusion = f32[160,128]{1,0:T(8,128)S(1)} fusion(f32[160,128]{1,0:T(8,128)} %get-tuple-element.14), kind=kLoop, calls=%fused_computation.2 | loop fusion | flops 20480 | bytes 163840 | tf_op jit(solution)/shard_map/mul | solution.py:519
  13.7 0.2 collective-permute-done
  13.9 3.9 %collective-permute-start.3 = (f32[160,128]{1,0:T(8,128)S(1)}, f32[160,128]{1,0:T(8,128)S(1)}, u32[]{:S(2)}, u32[]{:S(2)}) collective-permute-start(f32[160,128]{1,0:T(8,128)S(1)} %multiply_add_fusion), channel_id=1, source_target_pairs={{0,18},{1,19},{2,16},{3,17},{4,22},{5,23},{6,20},{7,21},{8,26},{9,... | collective-permute-start | bytes 245768 | tf_op jit(solution)/shard_map/ppermute | solution.py:451
  17.8 0.5 %collective-permute-start.2 = (f32[160,128]{1,0:T(8,128)S(1)}, f32[160,128]{1,0:T(8,128)S(1)}, u32[]{:S(2)}, u32[]{:S(2)}) collective-permute-start(f32[160,128]{1,0:T(8,128)S(1)} %multiply_add_fusion), channel_id=1, source_target_pairs={{0,16},{1,17},{2,18},{3,19},{4,20},{5,21},{6,22},{7,23},{8,24},{9,... | collective-permute-start | bytes 245768 | tf_op jit(solution)/shard_map/ppermute | solution.py:451
  18.3 0.1 collective-permute-start.1
  18.4 2.5 %collective-permute-done.3 = f32[160,128]{1,0:T(8,128)S(1)} collective-permute-done((f32[160,128]{1,0:T(8,128)S(1)}, f32[160,128]{1,0:T(8,128)S(1)}, u32[]{:S(2)}, u32[]{:S(2)}) %collective-permute-start.3) | collective-permute-done | bytes 81952 | tf_op jit(solution)/shard_map/ppermute | solution.py:451
  20.9 1.6 %collective-permute-done.2 = f32[160,128]{1,0:T(8,128)S(1)} collective-permute-done((f32[160,128]{1,0:T(8,128)S(1)}, f32[160,128]{1,0:T(8,128)S(1)}, u32[]{:S(2)}, u32[]{:S(2)}) %collective-permute-start.2) | collective-permute-done | bytes 81952 | tf_op jit(solution)/shard_map/ppermute | solution.py:451
  22.6 0.2 collective-permute-done.1
  22.8 1.6 %collective-permute-start.4 = (f32[160,128]{1,0:T(8,128)S(1)}, f32[160,128]{1,0:T(8,128)S(1)}, u32[]{:S(2)}, u32[]{:S(2)}) collective-permute-start(f32[160,128]{1,0:T(8,128)S(1)} %add_add_fusion), channel_id=1, source_target_pairs={{0,4},{1,5},{2,6},{3,7},{4,0},{5,1},{6,2},{7,3},{8,12},{9,13},{10,... | collective-permute-start | bytes 245768 | tf_op jit(solution)/shard_map/ppermute | solution.py:451
  24.4 2.9 %collective-permute-done.4 = f32[160,128]{1,0:T(8,128)S(1)} collective-permute-done((f32[160,128]{1,0:T(8,128)S(1)}, f32[160,128]{1,0:T(8,128)S(1)}, u32[]{:S(2)}, u32[]{:S(2)}) %collective-permute-start.4) | collective-permute-done | bytes 81952 | tf_op jit(solution)/shard_map/ppermute | solution.py:451
  27.3 2.7 %collective-permute-start.5 = (f32[160,128]{1,0:T(8,128)S(1)}, f32[160,128]{1,0:T(8,128)S(1)}, u32[]{:S(2)}, u32[]{:S(2)}) collective-permute-start(f32[160,128]{1,0:T(8,128)S(1)} %add.22), channel_id=1, source_target_pairs={{0,8},{1,9},{2,10},{3,11},{4,12},{5,13},{6,14},{7,15},{8,0},{9,1},... | collective-permute-start | bytes 245768 | tf_op jit(solution)/shard_map/ppermute | solution.py:451
  30.0 2.7 %collective-permute-done.5 = f32[160,128]{1,0:T(8,128)S(1)} collective-permute-done((f32[160,128]{1,0:T(8,128)S(1)}, f32[160,128]{1,0:T(8,128)S(1)}, u32[]{:S(2)}, u32[]{:S(2)}) %collective-permute-start.5) | collective-permute-done | bytes 81952 | tf_op jit(solution)/shard_map/ppermute | solution.py:451
  32.7 0.0 copy-start
  32.8 0.0 copy-start.1
  32.8 0.0 copy-start.2
  32.8 0.0 copy-start.3
  32.8 0.0 copy-start.4
  32.8 0.0 copy-start.5
  32.8 0.0 copy-start.6
  32.8 0.0 copy-start.7
  32.8 0.0 copy-start.8
  32.9 0.1 collective-permute-start.6
  32.9 3.2 %solve.1.solved = f32[8,128]{1,0:T(8,128)S(1)} custom-call(f32[72,128]{1,0:T(8,128)S(1)} %slice.8.packed), custom_call_target="tpu_custom_call" | custom-call | flops 4000000000 | bytes 15000000 | tf_op jit(solution)/shard_map/solve/pallas_call | solution.py:524
  36.1 0.0 collective-permute-done.6.jac_other
  36.1 0.0 copy-done
  36.2 0.0 copy-done.1
  36.2 0.0 copy-done.2
  36.2 0.0 copy-done.3
  36.2 0.0 copy-done.4
  36.2 0.0 copy-done.5
  36.2 0.0 copy-done.6
  36.2 0.0 copy-done.7
  36.2 0.0 copy-done.8
  36.2 4.5 %adjoint.1 = (f32[128,128]{1,0:T(8,128)}, f32[128,128]{1,0:T(8,128)}, f32[2,32]{1,0:T(2,128)}, f32[32,16384]{1,0:T(8,128)}) custom-call(f32[8,128]{1,0:T(8,128)S(1)} %solve.1.solved, f32[88,128]{1,0:T(8,128)S(1)} %slice.9.jac_mine, f32[88,128]{1,0:T(8,128)S(1)} %collective-permute-done.6.jac_other, f32[1,32]{1,0:T(1,128)S(1)} %bitcast.12, ...), custom_call_target="tpu_custom_call" | custom-call | tf_op jit(solution)/shard_map/adjoint/pallas_call | solution.py:534
  (6 shorter events, 0.1 us)
Async XLA Ops:
  12.3 1.7 %collective-permute-start = (f32[160,128]{1,0:T(8,128)}, f32[160,128]{1,0:T(8,128)S(1)}, u32[]{:S(2)}, u32[]{:S(2)}) collective-permute-start(f32[160,128]{1,0:T(8,128)} %get-tuple-element.15), channel_id=1, source_target_pairs={{0,1},{1,0},{2,3},{3,2},{4,5},{5,4},{6,7},{7,6},{8,9},{9,8},{10,11... | collective-permute-start | bytes 245768 | tf_op jit(solution)/shard_map/ppermute | solution.py:451
  13.9 7.0 %collective-permute-start.3 = (f32[160,128]{1,0:T(8,128)S(1)}, f32[160,128]{1,0:T(8,128)S(1)}, u32[]{:S(2)}, u32[]{:S(2)}) collective-permute-start(f32[160,128]{1,0:T(8,128)S(1)} %multiply_add_fusion), channel_id=1, source_target_pairs={{0,18},{1,19},{2,16},{3,17},{4,22},{5,23},{6,20},{7,21},{8,26},{9,... | collective-permute-start | bytes 245768 | tf_op jit(solution)/shard_map/ppermute | solution.py:451
  17.8 4.8 %collective-permute-start.2 = (f32[160,128]{1,0:T(8,128)S(1)}, f32[160,128]{1,0:T(8,128)S(1)}, u32[]{:S(2)}, u32[]{:S(2)}) collective-permute-start(f32[160,128]{1,0:T(8,128)S(1)} %multiply_add_fusion), channel_id=1, source_target_pairs={{0,16},{1,17},{2,18},{3,19},{4,20},{5,21},{6,22},{7,23},{8,24},{9,... | collective-permute-start | bytes 245768 | tf_op jit(solution)/shard_map/ppermute | solution.py:451
  18.3 4.4 %collective-permute-start.1 = (f32[160,128]{1,0:T(8,128)S(1)}, f32[160,128]{1,0:T(8,128)S(1)}, u32[]{:S(2)}, u32[]{:S(2)}) collective-permute-start(f32[160,128]{1,0:T(8,128)S(1)} %multiply_add_fusion), channel_id=1, source_target_pairs={{0,2},{1,3},{2,0},{3,1},{4,6},{5,7},{6,4},{7,5},{8,10},{9,11},{10,... | collective-permute-start | bytes 245768 | tf_op jit(solution)/shard_map/ppermute | solution.py:451
  22.8 4.5 %collective-permute-start.4 = (f32[160,128]{1,0:T(8,128)S(1)}, f32[160,128]{1,0:T(8,128)S(1)}, u32[]{:S(2)}, u32[]{:S(2)}) collective-permute-start(f32[160,128]{1,0:T(8,128)S(1)} %add_add_fusion), channel_id=1, source_target_pairs={{0,4},{1,5},{2,6},{3,7},{4,0},{5,1},{6,2},{7,3},{8,12},{9,13},{10,... | collective-permute-start | bytes 245768 | tf_op jit(solution)/shard_map/ppermute | solution.py:451
  27.3 5.4 %collective-permute-start.5 = (f32[160,128]{1,0:T(8,128)S(1)}, f32[160,128]{1,0:T(8,128)S(1)}, u32[]{:S(2)}, u32[]{:S(2)}) collective-permute-start(f32[160,128]{1,0:T(8,128)S(1)} %add.22), channel_id=1, source_target_pairs={{0,8},{1,9},{2,10},{3,11},{4,12},{5,13},{6,14},{7,15},{8,0},{9,1},... | collective-permute-start | bytes 245768 | tf_op jit(solution)/shard_map/ppermute | solution.py:451
  32.7 3.4 %copy-start = (f32[32,16384]{1,0:T(8,128)S(1)}, f32[32,16384]{1,0:T(8,128)}, u32[]{:S(2)}) copy-start(f32[32,16384]{1,0:T(8,128)} %get-tuple-element.18.scaled_in) | copy-start | bytes 6291460
  32.8 3.4 %copy-start.1 = (f32[32,16384]{1,0:T(8,128)S(1)}, f32[32,16384]{1,0:T(8,128)}, u32[]{:S(2)}) copy-start(f32[32,16384]{1,0:T(8,128)} %get-tuple-element.19.bounded_in) | copy-start | bytes 6291460
  32.8 3.4 %copy-start.2 = (f32[16384]{0:T(1024)S(1)}, f32[16384]{0:T(1024)}, u32[]{:S(2)}) copy-start(f32[16384]{0:T(1024)} %param.10) | copy-start | bytes 196612
  32.8 3.4 %copy-start.3 = (s32[16384]{0:T(1024)S(1)}, s32[16384]{0:T(1024)}, u32[]{:S(2)}) copy-start(s32[16384]{0:T(1024)} %param.11) | copy-start | bytes 196612
  32.8 3.4 %copy-start.4 = (f32[128,128]{1,0:T(8,128)S(1)}, f32[128,128]{1,0:T(8,128)}, u32[]{:S(2)}) copy-start(f32[128,128]{1,0:T(8,128)} %get-tuple-element.16.value_in) | copy-start | bytes 196612
  32.8 3.4 %copy-start.5 = (f32[128,128]{1,0:T(8,128)S(1)}, f32[128,128]{1,0:T(8,128)}, u32[]{:S(2)}) copy-start(f32[128,128]{1,0:T(8,128)} %get-tuple-element.17.pull_in) | copy-start | bytes 196612
  32.8 3.4 %copy-start.6 = (f32[32]{0:T(128)S(1)}, f32[32]{0:T(128)}, u32[]{:S(2)}) copy-start(f32[32]{0:T(128)} %param.7) | copy-start | bytes 388
  32.8 3.4 %copy-start.7 = (f32[32]{0:T(128)S(1)}, f32[32]{0:T(128)}, u32[]{:S(2)}) copy-start(f32[32]{0:T(128)} %param.8) | copy-start | bytes 388
  32.8 3.4 %copy-start.8 = (f32[32]{0:T(128)S(1)}, f32[32]{0:T(128)}, u32[]{:S(2)}) copy-start(f32[32]{0:T(128)} %param.9) | copy-start | bytes 388
  32.9 3.3 %collective-permute-start.6 = (f32[88,128]{1,0:T(8,128)S(1)}, f32[88,128]{1,0:T(8,128)S(1)}, u32[]{:S(2)}, u32[]{:S(2)}) collective-permute-start(f32[88,128]{1,0:T(8,128)S(1)} %slice.9.jac_mine), channel_id=1, source_target_pairs={{0,1},{1,0},{2,3},{3,2},{4,5},{5,4},{6,7},{7,6},{8,9},{9,8},{10,11... | collective-permute-start | bytes 135176 | tf_op jit(solution)/shard_map/ppermute | solution.py:451

commit v6 on v5

--- a/solution.py
+++ b/solution.py
@@ -163,7 +163,7 @@
         pull_acc[...] += pull_sum
         rows[aim : aim + 16, :] = target[...].astype(BF16)
 
-    cut = 16 * ((low // 16 + 1) // 2)
+    cut = 2 * features
 
     def multiply(rows, part):
         at = slice(0, cut) if part == 0 else slice(cut, low)
@@ -532,21 +532,21 @@
         name="solve",
     )(gram)
     value, flow, greeks, cot = pl.pallas_call(
-        functools.partial(adjoint_kernel, assets, block),
+        functools.partial(adjoint_kernel, assets, wide),
         in_specs=[local] * 12,
         out_specs=[remote] * 4,
         out_shape=[short, short, jax.ShapeDtypeStruct((2, assets), F32), big],
         scratch_shapes=[
             pltpu.VMEM((12, assets, LANES), F32),
-            pltpu.VMEM((2, 2, block // 16, LANES), F32),
-            pltpu.VMEM((2, 3, block // LANES, LANES), F32),
-            pltpu.VMEM((2, 2, assets, block), F32),
+            pltpu.VMEM((2, 2, wide // 16, LANES), F32),
+            pltpu.VMEM((2, 3, wide // LANES, LANES), F32),
+            pltpu.VMEM((2, 2, assets, wide), F32),
             pltpu.VMEM((assets, paths), F32),
             pltpu.VMEM((jac_rows, features), F32),
             pltpu.VMEM(compact, F32),
             pltpu.VMEM(compact, F32),
             pltpu.VMEM((2, assets), F32),
-            pltpu.SemaphoreType.DMA((4, paths // (2 * block))),
+            pltpu.SemaphoreType.DMA((4, paths // (2 * wide))),
         ],
         compiler_params=params,
         name="adjoint",

time: 41 us -> 40.8 us (level)
  no operation moved by 1% of the time
where the time goes in v6:
time: 40.8 us; the launch traced here: 40.6 us
  Pallas kernels  19.2 us (47%)
  waiting for transfers between devices  10.2 us (25%)
  starting transfers between devices  9.39 us (23%)
  other arithmetic  0.94 us (2%)
  between operations  0.83 us (2%)
    pallas_call x1, Pallas kernels, per_device(): pl.pallas_call(functools.partial(sums_kernel, assets, wide), in_specs=[re...  11.6 us
    ppermute x7, waiting for transfers between devices, swap(): return lax.ppermute(value, AXES, [(i, i ^ mask) for i in range(count)])  10.2 us
    ppermute x7, starting transfers between devices, swap(): return lax.ppermute(value, AXES, [(i, i ^ mask) for i in range(count)])  9.39 us
    pallas_call x1, Pallas kernels, per_device(): pl.pallas_call(functools.partial(adjoint_kernel, assets, wide), in_specs=...  4.4 us
    pallas_call x1, Pallas kernels, per_device(): pl.pallas_call(solve_kernel, out_shape=jax.ShapeDtypeStruct((8, features)...  3.21 us
    mul x1, other arithmetic, per_device(): keep * scale  0.89 us
  transfers between devices with their start and end apart: 7, of which 6 were waited for; matrix products, arithmetic and copies ran while one was open for 2% of the time, Pallas kernels for 8%

profile of v6, /device:TPU:0, one launch (start us, length us, event | category | flops | bytes accessed | tf_op | source)
XLA Modules:
  0.0 40.6 jit_solution(1150812117100726529)
XLA Ops:
  0.6 11.6 %sums.1 = (f32[32,16384]{1,0:T(8,128)}, f32[32,16384]{1,0:T(8,128)}, f32[128,128]{1,0:T(8,128)}, f32[128,128]{1,0:T(8,128)}, f32[160,128]{1,0:T(8,128)}, /*index=5*/f32[160,128]{1,0:T(8,128)}) custom-call(f32[1,32]{1,0:T(1,128)} %bitcast.11, f32[1,32]{1,0:T(1,128)} %bitcast.13, f32[1,32]{1,0:T(1,128)} %bitcast.15, f32[128,128]{1,0:T(8,128)} %bitcast.7, ...), custom_call_target="tpu_custom_call" | custom-call | tf_op jit(solution)/shard_map/sums/pallas_call | solution.py:481
  12.2 0.5 %collective-permute-start = (f32[160,128]{1,0:T(8,128)}, f32[160,128]{1,0:T(8,128)S(1)}, u32[]{:S(2)}, u32[]{:S(2)}) collective-permute-start(f32[160,128]{1,0:T(8,128)} %get-tuple-element.15), channel_id=1, source_target_pairs={{0,1},{1,0},{2,3},{3,2},{4,5},{5,4},{6,7},{7,6},{8,9},{9,8},{10,11... | collective-permute-start | bytes 245768 | tf_op jit(solution)/shard_map/ppermute | solution.py:451
  12.8 0.9 %broadcast_multiply_fusion = f32[160,128]{1,0:T(8,128)S(1)} fusion(f32[160,128]{1,0:T(8,128)} %get-tuple-element.14), kind=kLoop, calls=%fused_computation.2 | loop fusion | flops 20480 | bytes 163840 | tf_op jit(solution)/shard_map/mul | solution.py:519
  13.7 0.2 collective-permute-done
  13.9 3.9 %collective-permute-start.3 = (f32[160,128]{1,0:T(8,128)S(1)}, f32[160,128]{1,0:T(8,128)S(1)}, u32[]{:S(2)}, u32[]{:S(2)}) collective-permute-start(f32[160,128]{1,0:T(8,128)S(1)} %multiply_add_fusion), channel_id=1, source_target_pairs={{0,18},{1,19},{2,16},{3,17},{4,22},{5,23},{6,20},{7,21},{8,26},{9,... | collective-permute-start | bytes 245768 | tf_op jit(solution)/shard_map/ppermute | solution.py:451
  17.8 0.5 %collective-permute-start.2 = (f32[160,128]{1,0:T(8,128)S(1)}, f32[160,128]{1,0:T(8,128)S(1)}, u32[]{:S(2)}, u32[]{:S(2)}) collective-permute-start(f32[160,128]{1,0:T(8,128)S(1)} %multiply_add_fusion), channel_id=1, source_target_pairs={{0,16},{1,17},{2,18},{3,19},{4,20},{5,21},{6,22},{7,23},{8,24},{9,... | collective-permute-start | bytes 245768 | tf_op jit(solution)/shard_map/ppermute | solution.py:451
  18.3 0.1 collective-permute-start.1
  18.4 2.5 %collective-permute-done.3 = f32[160,128]{1,0:T(8,128)S(1)} collective-permute-done((f32[160,128]{1,0:T(8,128)S(1)}, f32[160,128]{1,0:T(8,128)S(1)}, u32[]{:S(2)}, u32[]{:S(2)}) %collective-permute-start.3) | collective-permute-done | bytes 81952 | tf_op jit(solution)/shard_map/ppermute | solution.py:451
  20.9 1.6 %collective-permute-done.2 = f32[160,128]{1,0:T(8,128)S(1)} collective-permute-done((f32[160,128]{1,0:T(8,128)S(1)}, f32[160,128]{1,0:T(8,128)S(1)}, u32[]{:S(2)}, u32[]{:S(2)}) %collective-permute-start.2) | collective-permute-done | bytes 81952 | tf_op jit(solution)/shard_map/ppermute | solution.py:451
  22.5 0.2 collective-permute-done.1
  22.8 1.6 %collective-permute-start.4 = (f32[160,128]{1,0:T(8,128)S(1)}, f32[160,128]{1,0:T(8,128)S(1)}, u32[]{:S(2)}, u32[]{:S(2)}) collective-permute-start(f32[160,128]{1,0:T(8,128)S(1)} %add_add_fusion), channel_id=1, source_target_pairs={{0,4},{1,5},{2,6},{3,7},{4,0},{5,1},{6,2},{7,3},{8,12},{9,13},{10,... | collective-permute-start | bytes 245768 | tf_op jit(solution)/shard_map/ppermute | solution.py:451
  24.4 2.9 %collective-permute-done.4 = f32[160,128]{1,0:T(8,128)S(1)} collective-permute-done((f32[160,128]{1,0:T(8,128)S(1)}, f32[160,128]{1,0:T(8,128)S(1)}, u32[]{:S(2)}, u32[]{:S(2)}) %collective-permute-start.4) | collective-permute-done | bytes 81952 | tf_op jit(solution)/shard_map/ppermute | solution.py:451
  27.3 2.7 %collective-permute-start.5 = (f32[160,128]{1,0:T(8,128)S(1)}, f32[160,128]{1,0:T(8,128)S(1)}, u32[]{:S(2)}, u32[]{:S(2)}) collective-permute-start(f32[160,128]{1,0:T(8,128)S(1)} %add.22), channel_id=1, source_target_pairs={{0,8},{1,9},{2,10},{3,11},{4,12},{5,13},{6,14},{7,15},{8,0},{9,1},... | collective-permute-start | bytes 245768 | tf_op jit(solution)/shard_map/ppermute | solution.py:451
  29.9 2.8 %collective-permute-done.5 = f32[160,128]{1,0:T(8,128)S(1)} collective-permute-done((f32[160,128]{1,0:T(8,128)S(1)}, f32[160,128]{1,0:T(8,128)S(1)}, u32[]{:S(2)}, u32[]{:S(2)}) %collective-permute-start.5) | collective-permute-done | bytes 81952 | tf_op jit(solution)/shard_map/ppermute | solution.py:451
  32.7 0.0 copy-start
  32.7 0.0 copy-start.1
  32.8 0.0 copy-start.2
  32.8 0.0 copy-start.3
  32.8 0.0 copy-start.4
  32.8 0.0 copy-start.5
  32.8 0.0 copy-start.6
  32.8 0.0 copy-start.7
  32.8 0.0 copy-start.8
  32.8 0.1 collective-permute-start.6
  32.9 3.2 %solve.1.solved = f32[8,128]{1,0:T(8,128)S(1)} custom-call(f32[72,128]{1,0:T(8,128)S(1)} %slice.8.packed), custom_call_target="tpu_custom_call" | custom-call | flops 4000000000 | bytes 15000000 | tf_op jit(solution)/shard_map/solve/pallas_call | solution.py:524
  36.1 0.0 collective-permute-done.6.jac_other
  36.1 0.0 copy-done
  36.1 0.0 copy-done.1
  36.2 0.0 copy-done.2
  36.2 0.0 copy-done.3
  36.2 0.0 copy-done.4
  36.2 0.0 copy-done.5
  36.2 0.0 copy-done.6
  36.2 0.0 copy-done.7
  36.2 0.0 copy-done.8
  36.2 4.4 %adjoint.1 = (f32[128,128]{1,0:T(8,128)}, f32[128,128]{1,0:T(8,128)}, f32[2,32]{1,0:T(2,128)}, f32[32,16384]{1,0:T(8,128)}) custom-call(f32[8,128]{1,0:T(8,128)S(1)} %solve.1.solved, f32[88,128]{1,0:T(8,128)S(1)} %slice.9.jac_mine, f32[88,128]{1,0:T(8,128)S(1)} %collective-permute-done.6.jac_other, f32[1,32]{1,0:T(1,128)S(1)} %bitcast.12, ...), custom_call_target="tpu_custom_call" | custom-call | tf_op jit(solution)/shard_map/adjoint/pallas_call | solution.py:534
  (6 shorter events, 0.1 us)
Async XLA Ops:
  12.2 1.7 %collective-permute-start = (f32[160,128]{1,0:T(8,128)}, f32[160,128]{1,0:T(8,128)S(1)}, u32[]{:S(2)}, u32[]{:S(2)}) collective-permute-start(f32[160,128]{1,0:T(8,128)} %get-tuple-element.15), channel_id=1, source_target_pairs={{0,1},{1,0},{2,3},{3,2},{4,5},{5,4},{6,7},{7,6},{8,9},{9,8},{10,11... | collective-permute-start | bytes 245768 | tf_op jit(solution)/shard_map/ppermute | solution.py:451
  13.9 7.0 %collective-permute-start.3 = (f32[160,128]{1,0:T(8,128)S(1)}, f32[160,128]{1,0:T(8,128)S(1)}, u32[]{:S(2)}, u32[]{:S(2)}) collective-permute-start(f32[160,128]{1,0:T(8,128)S(1)} %multiply_add_fusion), channel_id=1, source_target_pairs={{0,18},{1,19},{2,16},{3,17},{4,22},{5,23},{6,20},{7,21},{8,26},{9,... | collective-permute-start | bytes 245768 | tf_op jit(solution)/shard_map/ppermute | solution.py:451
  17.8 4.8 %collective-permute-start.2 = (f32[160,128]{1,0:T(8,128)S(1)}, f32[160,128]{1,0:T(8,128)S(1)}, u32[]{:S(2)}, u32[]{:S(2)}) collective-permute-start(f32[160,128]{1,0:T(8,128)S(1)} %multiply_add_fusion), channel_id=1, source_target_pairs={{0,16},{1,17},{2,18},{3,19},{4,20},{5,21},{6,22},{7,23},{8,24},{9,... | collective-permute-start | bytes 245768 | tf_op jit(solution)/shard_map/ppermute | solution.py:451
  18.3 4.4 %collective-permute-start.1 = (f32[160,128]{1,0:T(8,128)S(1)}, f32[160,128]{1,0:T(8,128)S(1)}, u32[]{:S(2)}, u32[]{:S(2)}) collective-permute-start(f32[160,128]{1,0:T(8,128)S(1)} %multiply_add_fusion), channel_id=1, source_target_pairs={{0,2},{1,3},{2,0},{3,1},{4,6},{5,7},{6,4},{7,5},{8,10},{9,11},{10,... | collective-permute-start | bytes 245768 | tf_op jit(solution)/shard_map/ppermute | solution.py:451
  22.8 4.5 %collective-permute-start.4 = (f32[160,128]{1,0:T(8,128)S(1)}, f32[160,128]{1,0:T(8,128)S(1)}, u32[]{:S(2)}, u32[]{:S(2)}) collective-permute-start(f32[160,128]{1,0:T(8,128)S(1)} %add_add_fusion), channel_id=1, source_target_pairs={{0,4},{1,5},{2,6},{3,7},{4,0},{5,1},{6,2},{7,3},{8,12},{9,13},{10,... | collective-permute-start | bytes 245768 | tf_op jit(solution)/shard_map/ppermute | solution.py:451
  27.3 5.4 %collective-permute-start.5 = (f32[160,128]{1,0:T(8,128)S(1)}, f32[160,128]{1,0:T(8,128)S(1)}, u32[]{:S(2)}, u32[]{:S(2)}) collective-permute-start(f32[160,128]{1,0:T(8,128)S(1)} %add.22), channel_id=1, source_target_pairs={{0,8},{1,9},{2,10},{3,11},{4,12},{5,13},{6,14},{7,15},{8,0},{9,1},... | collective-permute-start | bytes 245768 | tf_op jit(solution)/shard_map/ppermute | solution.py:451
  32.7 3.4 %copy-start = (f32[32,16384]{1,0:T(8,128)S(1)}, f32[32,16384]{1,0:T(8,128)}, u32[]{:S(2)}) copy-start(f32[32,16384]{1,0:T(8,128)} %get-tuple-element.18.scaled_in) | copy-start | bytes 6291460
  32.7 3.4 %copy-start.1 = (f32[32,16384]{1,0:T(8,128)S(1)}, f32[32,16384]{1,0:T(8,128)}, u32[]{:S(2)}) copy-start(f32[32,16384]{1,0:T(8,128)} %get-tuple-element.19.bounded_in) | copy-start | bytes 6291460
  32.8 3.4 %copy-start.2 = (f32[16384]{0:T(1024)S(1)}, f32[16384]{0:T(1024)}, u32[]{:S(2)}) copy-start(f32[16384]{0:T(1024)} %param.10) | copy-start | bytes 196612
  32.8 3.4 %copy-start.3 = (s32[16384]{0:T(1024)S(1)}, s32[16384]{0:T(1024)}, u32[]{:S(2)}) copy-start(s32[16384]{0:T(1024)} %param.11) | copy-start | bytes 196612
  32.8 3.4 %copy-start.4 = (f32[128,128]{1,0:T(8,128)S(1)}, f32[128,128]{1,0:T(8,128)}, u32[]{:S(2)}) copy-start(f32[128,128]{1,0:T(8,128)} %get-tuple-element.16.value_in) | copy-start | bytes 196612
  32.8 3.4 %copy-start.5 = (f32[128,128]{1,0:T(8,128)S(1)}, f32[128,128]{1,0:T(8,128)}, u32[]{:S(2)}) copy-start(f32[128,128]{1,0:T(8,128)} %get-tuple-element.17.pull_in) | copy-start | bytes 196612
  32.8 3.4 %copy-start.6 = (f32[32]{0:T(128)S(1)}, f32[32]{0:T(128)}, u32[]{:S(2)}) copy-start(f32[32]{0:T(128)} %param.7) | copy-start | bytes 388
  32.8 3.4 %copy-start.7 = (f32[32]{0:T(128)S(1)}, f32[32]{0:T(128)}, u32[]{:S(2)}) copy-start(f32[32]{0:T(128)} %param.8) | copy-start | bytes 388
  32.8 3.4 %copy-start.8 = (f32[32]{0:T(128)S(1)}, f32[32]{0:T(128)}, u32[]{:S(2)}) copy-start(f32[32]{0:T(128)} %param.9) | copy-start | bytes 388
  32.8 3.3 %collective-permute-start.6 = (f32[88,128]{1,0:T(8,128)S(1)}, f32[88,128]{1,0:T(8,128)S(1)}, u32[]{:S(2)}, u32[]{:S(2)}) collective-permute-start(f32[88,128]{1,0:T(8,128)S(1)} %slice.9.jac_mine), channel_id=1, source_target_pairs={{0,1},{1,0},{2,3},{3,2},{4,5},{5,4},{6,7},{7,6},{8,9},{9,8},{10,11... | collective-permute-start | bytes 135176 | tf_op jit(solution)/shard_map/ppermute | solution.py:451

commit v7 on v6

--- a/solution.py
+++ b/solution.py
@@ -492,7 +492,7 @@
             pltpu.VMEM(compact, jnp.int32),
             pltpu.VMEM((assets, paths), F32),
             pltpu.VMEM((4, assets, LANES), F32),
-            pltpu.VMEM((wide // 16, LANES), F32),
+            pltpu.VMEM((wide // 16 + 8, LANES), F32),
             pltpu.VMEM((16, wide), F32),
             pltpu.VMEM((assets, paths), F32),
             pltpu.VMEM((assets, paths), F32),
@@ -538,7 +538,7 @@
         out_shape=[short, short, jax.ShapeDtypeStruct((2, assets), F32), big],
         scratch_shapes=[
             pltpu.VMEM((12, assets, LANES), F32),
-            pltpu.VMEM((2, 2, wide // 16, LANES), F32),
+            pltpu.VMEM((2, 2, wide // 16 + 8, LANES), F32),
             pltpu.VMEM((2, 3, wide // LANES, LANES), F32),
             pltpu.VMEM((2, 2, assets, wide), F32),
             pltpu.VMEM((assets, paths), F32),

time: 40.8 us -> 40.9 us (level)
  no operation moved by 1% of the time
where the time goes in v7:
time: 40.9 us; the launch traced here: 40.7 us
  Pallas kernels  19.2 us (47%)
  waiting for transfers between devices  10.2 us (25%)
  starting transfers between devices  9.39 us (23%)
  other arithmetic  0.94 us (2%)
  between operations  0.83 us (2%)
    pallas_call x1, Pallas kernels, per_device(): pl.pallas_call(functools.partial(sums_kernel, assets, wide), in_specs=[re...  11.6 us
    ppermute x7, waiting for transfers between devices, swap(): return lax.ppermute(value, AXES, [(i, i ^ mask) for i in range(count)])  10.2 us
    ppermute x7, starting transfers between devices, swap(): return lax.ppermute(value, AXES, [(i, i ^ mask) for i in range(count)])  9.39 us
    pallas_call x1, Pallas kernels, per_device(): pl.pallas_call(functools.partial(adjoint_kernel, assets, wide), in_specs=...  4.4 us
    pallas_call x1, Pallas kernels, per_device(): pl.pallas_call(solve_kernel, out_shape=jax.ShapeDtypeStruct((8, features)...  3.21 us
    mul x1, other arithmetic, per_device(): keep * scale  0.89 us
  transfers between devices with their start and end apart: 7, of which 6 were waited for; matrix products, arithmetic and copies ran while one was open for 2% of the time, Pallas kernels for 8%

profile of v7, /device:TPU:0, one launch (start us, length us, event | category | flops | bytes accessed | tf_op | source)
XLA Modules:
  0.0 40.7 jit_solution(9708937697308167535)
XLA Ops:
  0.6 11.6 %sums.1 = (f32[32,16384]{1,0:T(8,128)}, f32[32,16384]{1,0:T(8,128)}, f32[128,128]{1,0:T(8,128)}, f32[128,128]{1,0:T(8,128)}, f32[160,128]{1,0:T(8,128)}, /*index=5*/f32[160,128]{1,0:T(8,128)}) custom-call(f32[1,32]{1,0:T(1,128)} %bitcast.11, f32[1,32]{1,0:T(1,128)} %bitcast.13, f32[1,32]{1,0:T(1,128)} %bitcast.15, f32[128,128]{1,0:T(8,128)} %bitcast.7, ...), custom_call_target="tpu_custom_call" | custom-call | tf_op jit(solution)/shard_map/sums/pallas_call | solution.py:481
  12.3 0.5 %collective-permute-start = (f32[160,128]{1,0:T(8,128)}, f32[160,128]{1,0:T(8,128)S(1)}, u32[]{:S(2)}, u32[]{:S(2)}) collective-permute-start(f32[160,128]{1,0:T(8,128)} %get-tuple-element.15), channel_id=1, source_target_pairs={{0,1},{1,0},{2,3},{3,2},{4,5},{5,4},{6,7},{7,6},{8,9},{9,8},{10,11... | collective-permute-start | bytes 245768 | tf_op jit(solution)/shard_map/ppermute | solution.py:451
  12.8 0.9 %broadcast_multiply_fusion = f32[160,128]{1,0:T(8,128)S(1)} fusion(f32[160,128]{1,0:T(8,128)} %get-tuple-element.14), kind=kLoop, calls=%fused_computation.2 | loop fusion | flops 20480 | bytes 163840 | tf_op jit(solution)/shard_map/mul | solution.py:519
  13.7 0.2 collective-permute-done
  13.9 3.9 %collective-permute-start.3 = (f32[160,128]{1,0:T(8,128)S(1)}, f32[160,128]{1,0:T(8,128)S(1)}, u32[]{:S(2)}, u32[]{:S(2)}) collective-permute-start(f32[160,128]{1,0:T(8,128)S(1)} %multiply_add_fusion), channel_id=1, source_target_pairs={{0,18},{1,19},{2,16},{3,17},{4,22},{5,23},{6,20},{7,21},{8,26},{9,... | collective-permute-start | bytes 245768 | tf_op jit(solution)/shard_map/ppermute | solution.py:451
  17.8 0.5 %collective-permute-start.2 = (f32[160,128]{1,0:T(8,128)S(1)}, f32[160,128]{1,0:T(8,128)S(1)}, u32[]{:S(2)}, u32[]{:S(2)}) collective-permute-start(f32[160,128]{1,0:T(8,128)S(1)} %multiply_add_fusion), channel_id=1, source_target_pairs={{0,16},{1,17},{2,18},{3,19},{4,20},{5,21},{6,22},{7,23},{8,24},{9,... | collective-permute-start | bytes 245768 | tf_op jit(solution)/shard_map/ppermute | solution.py:451
  18.3 0.1 collective-permute-start.1
  18.4 2.5 %collective-permute-done.3 = f32[160,128]{1,0:T(8,128)S(1)} collective-permute-done((f32[160,128]{1,0:T(8,128)S(1)}, f32[160,128]{1,0:T(8,128)S(1)}, u32[]{:S(2)}, u32[]{:S(2)}) %collective-permute-start.3) | collective-permute-done | bytes 81952 | tf_op jit(solution)/shard_map/ppermute | solution.py:451
  20.9 1.6 %collective-permute-done.2 = f32[160,128]{1,0:T(8,128)S(1)} collective-permute-done((f32[160,128]{1,0:T(8,128)S(1)}, f32[160,128]{1,0:T(8,128)S(1)}, u32[]{:S(2)}, u32[]{:S(2)}) %collective-permute-start.2) | collective-permute-done | bytes 81952 | tf_op jit(solution)/shard_map/ppermute | solution.py:451
  22.6 0.2 collective-permute-done.1
  22.8 1.6 %collective-permute-start.4 = (f32[160,128]{1,0:T(8,128)S(1)}, f32[160,128]{1,0:T(8,128)S(1)}, u32[]{:S(2)}, u32[]{:S(2)}) collective-permute-start(f32[160,128]{1,0:T(8,128)S(1)} %add_add_fusion), channel_id=1, source_target_pairs={{0,4},{1,5},{2,6},{3,7},{4,0},{5,1},{6,2},{7,3},{8,12},{9,13},{10,... | collective-permute-start | bytes 245768 | tf_op jit(solution)/shard_map/ppermute | solution.py:451
  24.4 2.9 %collective-permute-done.4 = f32[160,128]{1,0:T(8,128)S(1)} collective-permute-done((f32[160,128]{1,0:T(8,128)S(1)}, f32[160,128]{1,0:T(8,128)S(1)}, u32[]{:S(2)}, u32[]{:S(2)}) %collective-permute-start.4) | collective-permute-done | bytes 81952 | tf_op jit(solution)/shard_map/ppermute | solution.py:451
  27.3 2.7 %collective-permute-start.5 = (f32[160,128]{1,0:T(8,128)S(1)}, f32[160,128]{1,0:T(8,128)S(1)}, u32[]{:S(2)}, u32[]{:S(2)}) collective-permute-start(f32[160,128]{1,0:T(8,128)S(1)} %add.22), channel_id=1, source_target_pairs={{0,8},{1,9},{2,10},{3,11},{4,12},{5,13},{6,14},{7,15},{8,0},{9,1},... | collective-permute-start | bytes 245768 | tf_op jit(solution)/shard_map/ppermute | solution.py:451
  30.0 2.7 %collective-permute-done.5 = f32[160,128]{1,0:T(8,128)S(1)} collective-permute-done((f32[160,128]{1,0:T(8,128)S(1)}, f32[160,128]{1,0:T(8,128)S(1)}, u32[]{:S(2)}, u32[]{:S(2)}) %collective-permute-start.5) | collective-permute-done | bytes 81952 | tf_op jit(solution)/shard_map/ppermute | solution.py:451
  32.8 0.0 copy-start
  32.8 0.0 copy-start.1
  32.8 0.0 copy-start.2
  32.8 0.0 copy-start.3
  32.8 0.0 copy-start.4
  32.8 0.0 copy-start.5
  32.8 0.0 copy-start.6
  32.9 0.0 copy-start.7
  32.9 0.0 copy-start.8
  32.9 0.1 collective-permute-start.6
  33.0 3.2 %solve.1.solved = f32[8,128]{1,0:T(8,128)S(1)} custom-call(f32[72,128]{1,0:T(8,128)S(1)} %slice.8.packed), custom_call_target="tpu_custom_call" | custom-call | flops 4000000000 | bytes 15000000 | tf_op jit(solution)/shard_map/solve/pallas_call | solution.py:524
  36.2 0.0 collective-permute-done.6.jac_other
  36.2 0.0 copy-done
  36.2 0.0 copy-done.1
  36.2 0.0 copy-done.2
  36.2 0.0 copy-done.3
  36.2 0.0 copy-done.4
  36.2 0.0 copy-done.5
  36.2 0.0 copy-done.6
  36.2 0.0 copy-done.7
  36.2 0.0 copy-done.8
  36.3 4.4 %adjoint.1 = (f32[128,128]{1,0:T(8,128)}, f32[128,128]{1,0:T(8,128)}, f32[2,32]{1,0:T(2,128)}, f32[32,16384]{1,0:T(8,128)}) custom-call(f32[8,128]{1,0:T(8,128)S(1)} %solve.1.solved, f32[88,128]{1,0:T(8,128)S(1)} %slice.9.jac_mine, f32[88,128]{1,0:T(8,128)S(1)} %collective-permute-done.6.jac_other, f32[1,32]{1,0:T(1,128)S(1)} %bitcast.12, ...), custom_call_target="tpu_custom_call" | custom-call | tf_op jit(solution)/shard_map/adjoint/pallas_call | solution.py:534
  (6 shorter events, 0.1 us)
Async XLA Ops:
  12.3 1.7 %collective-permute-start = (f32[160,128]{1,0:T(8,128)}, f32[160,128]{1,0:T(8,128)S(1)}, u32[]{:S(2)}, u32[]{:S(2)}) collective-permute-start(f32[160,128]{1,0:T(8,128)} %get-tuple-element.15), channel_id=1, source_target_pairs={{0,1},{1,0},{2,3},{3,2},{4,5},{5,4},{6,7},{7,6},{8,9},{9,8},{10,11... | collective-permute-start | bytes 245768 | tf_op jit(solution)/shard_map/ppermute | solution.py:451
  13.9 7.0 %collective-permute-start.3 = (f32[160,128]{1,0:T(8,128)S(1)}, f32[160,128]{1,0:T(8,128)S(1)}, u32[]{:S(2)}, u32[]{:S(2)}) collective-permute-start(f32[160,128]{1,0:T(8,128)S(1)} %multiply_add_fusion), channel_id=1, source_target_pairs={{0,18},{1,19},{2,16},{3,17},{4,22},{5,23},{6,20},{7,21},{8,26},{9,... | collective-permute-start | bytes 245768 | tf_op jit(solution)/shard_map/ppermute | solution.py:451
  17.8 4.8 %collective-permute-start.2 = (f32[160,128]{1,0:T(8,128)S(1)}, f32[160,128]{1,0:T(8,128)S(1)}, u32[]{:S(2)}, u32[]{:S(2)}) collective-permute-start(f32[160,128]{1,0:T(8,128)S(1)} %multiply_add_fusion), channel_id=1, source_target_pairs={{0,16},{1,17},{2,18},{3,19},{4,20},{5,21},{6,22},{7,23},{8,24},{9,... | collective-permute-start | bytes 245768 | tf_op jit(solution)/shard_map/ppermute | solution.py:451
  18.3 4.4 %collective-permute-start.1 = (f32[160,128]{1,0:T(8,128)S(1)}, f32[160,128]{1,0:T(8,128)S(1)}, u32[]{:S(2)}, u32[]{:S(2)}) collective-permute-start(f32[160,128]{1,0:T(8,128)S(1)} %multiply_add_fusion), channel_id=1, source_target_pairs={{0,2},{1,3},{2,0},{3,1},{4,6},{5,7},{6,4},{7,5},{8,10},{9,11},{10,... | collective-permute-start | bytes 245768 | tf_op jit(solution)/shard_map/ppermute | solution.py:451
  22.8 4.5 %collective-permute-start.4 = (f32[160,128]{1,0:T(8,128)S(1)}, f32[160,128]{1,0:T(8,128)S(1)}, u32[]{:S(2)}, u32[]{:S(2)}) collective-permute-start(f32[160,128]{1,0:T(8,128)S(1)} %add_add_fusion), channel_id=1, source_target_pairs={{0,4},{1,5},{2,6},{3,7},{4,0},{5,1},{6,2},{7,3},{8,12},{9,13},{10,... | collective-permute-start | bytes 245768 | tf_op jit(solution)/shard_map/ppermute | solution.py:451
  27.3 5.4 %collective-permute-start.5 = (f32[160,128]{1,0:T(8,128)S(1)}, f32[160,128]{1,0:T(8,128)S(1)}, u32[]{:S(2)}, u32[]{:S(2)}) collective-permute-start(f32[160,128]{1,0:T(8,128)S(1)} %add.22), channel_id=1, source_target_pairs={{0,8},{1,9},{2,10},{3,11},{4,12},{5,13},{6,14},{7,15},{8,0},{9,1},... | collective-permute-start | bytes 245768 | tf_op jit(solution)/shard_map/ppermute | solution.py:451
  32.8 3.4 %copy-start = (f32[32,16384]{1,0:T(8,128)S(1)}, f32[32,16384]{1,0:T(8,128)}, u32[]{:S(2)}) copy-start(f32[32,16384]{1,0:T(8,128)} %get-tuple-element.18.scaled_in) | copy-start | bytes 6291460
  32.8 3.4 %copy-start.1 = (f32[32,16384]{1,0:T(8,128)S(1)}, f32[32,16384]{1,0:T(8,128)}, u32[]{:S(2)}) copy-start(f32[32,16384]{1,0:T(8,128)} %get-tuple-element.19.bounded_in) | copy-start | bytes 6291460
  32.8 3.4 %copy-start.2 = (f32[16384]{0:T(1024)S(1)}, f32[16384]{0:T(1024)}, u32[]{:S(2)}) copy-start(f32[16384]{0:T(1024)} %param.10) | copy-start | bytes 196612
  32.8 3.4 %copy-start.3 = (s32[16384]{0:T(1024)S(1)}, s32[16384]{0:T(1024)}, u32[]{:S(2)}) copy-start(s32[16384]{0:T(1024)} %param.11) | copy-start | bytes 196612
  32.8 3.4 %copy-start.4 = (f32[128,128]{1,0:T(8,128)S(1)}, f32[128,128]{1,0:T(8,128)}, u32[]{:S(2)}) copy-start(f32[128,128]{1,0:T(8,128)} %get-tuple-element.16.value_in) | copy-start | bytes 196612
  32.8 3.4 %copy-start.5 = (f32[128,128]{1,0:T(8,128)S(1)}, f32[128,128]{1,0:T(8,128)}, u32[]{:S(2)}) copy-start(f32[128,128]{1,0:T(8,128)} %get-tuple-element.17.pull_in) | copy-start | bytes 196612
  32.8 3.4 %copy-start.6 = (f32[32]{0:T(128)S(1)}, f32[32]{0:T(128)}, u32[]{:S(2)}) copy-start(f32[32]{0:T(128)} %param.7) | copy-start | bytes 388
  32.9 3.4 %copy-start.7 = (f32[32]{0:T(128)S(1)}, f32[32]{0:T(128)}, u32[]{:S(2)}) copy-start(f32[32]{0:T(128)} %param.8) | copy-start | bytes 388
  32.9 3.4 %copy-start.8 = (f32[32]{0:T(128)S(1)}, f32[32]{0:T(128)}, u32[]{:S(2)}) copy-start(f32[32]{0:T(128)} %param.9) | copy-start | bytes 388
  32.9 3.3 %collective-permute-start.6 = (f32[88,128]{1,0:T(8,128)S(1)}, f32[88,128]{1,0:T(8,128)S(1)}, u32[]{:S(2)}, u32[]{:S(2)}) collective-permute-start(f32[88,128]{1,0:T(8,128)S(1)} %slice.9.jac_mine), channel_id=1, source_target_pairs={{0,1},{1,0},{2,3},{3,2},{4,5},{5,4},{6,7},{7,6},{8,9},{9,8},{10,11... | collective-permute-start | bytes 135176 | tf_op jit(solution)/shard_map/ppermute | solution.py:451
